TPU v7x, 32 devices: a whole 2x2x4 slice. The times are simulated.
32 devices in a mesh: blk: 8 (over z, x), rep: 4 (over y, core).
Axes of the slice: x: 2, y: 2, z: 4, core: 2. Of those that a mesh axis runs over, the one named last changes fastest.
Arguments:
- image_embed: bfloat16 [4, 192, 1280], P('rep', 'blk'), may hold values from -12 to 12
- text_hidden: bfloat16 [4, 192, 640], P('rep', 'blk'), may hold values from -6 to 6
- text_rest: bfloat16 [4, 192, 1280], P('rep', 'blk'), may hold values from -52 to 52
- proj_window: bfloat16 [640, 1280], P('blk'), may hold values from -0.15625 to 0.15625
- log_scale: float32 [1], replicated, may hold values from 4.66 to 5
Outputs:
- loss: float32 [1], replicated
- grad_log_scale: float32 [1], replicated
- grad_image: bfloat16 [4, 192, 1280], P('rep', 'blk')
- grad_text: bfloat16 [4, 192, 1280], P('rep', 'blk')
- grad_proj: float32 [640, 1280], P('blk')
All inputs are finite; a program needn't handle non-finite values.
Results may differ from a plain program's by a relative error of at most 0.01.
Values may be sent and summed in bfloat16 or wider, within the bound.
No kernel may reach another device: no remote copies, remote signals or barrier semaphores. Data moves between devices by JAX's collectives and lax.ppermute only.
A program may use at most 64 MiB of HBM per device.

v0:
```python
import jax
import jax.numpy as jnp
from jax import lax
from jax.sharding import PartitionSpec as P


def joined(value, axis, join):
    pieces = jax.tree.map(lambda part: lax.all_gather(part, axis), value)
    head = jax.tree.map(lambda part: part[0], pieces)
    tail = jax.tree.map(lambda part: part[1:], pieces)
    running, _ = lax.scan(lambda running, slab: (join(running, slab), None), head, tail)
    return running


def unit_rows(values):
    row_norm = jnp.sqrt(jnp.sum(values * values, axis=-1, keepdims=True) + 1e-06)
    return (values / row_norm, row_norm)


def unit_back(unit_vec, row_norm, grad_unit):
    return (grad_unit - unit_vec * jnp.sum(unit_vec * grad_unit, axis=-1, keepdims=True)) / row_norm


def pair_products(left, right):
    return lax.dot_general(
        left, right, (((1,), (1,)), ((), ())), preferred_element_type=jnp.float32
    )


def combine_parts(earlier, later):
    col_top = jnp.maximum(earlier[0], later[0])
    return (
        col_top,
        earlier[1] * jnp.exp(earlier[0] - col_top) + later[1] * jnp.exp(later[0] - col_top),
    )


def on_device(image_embed, text_hidden, text_rest, proj_window, log_scale):
    hidden = text_hidden[0]
    local_rows = hidden.shape[0]
    group_rows = local_rows * lax.axis_size("blk")
    offset = lax.axis_index("blk") * local_rows
    factor = 1.0 / (2.0 * group_rows * lax.axis_size("rep"))
    logit_scale = jnp.exp(log_scale[0])
    columns = hidden
    projected = jnp.dot(
        columns,
        lax.all_gather(proj_window, "blk", axis=0, tiled=True),
        preferred_element_type=jnp.float32,
    )
    text_unit, text_norm = unit_rows(text_rest[0].astype(jnp.float32) + projected)
    image_unit, image_norm = unit_rows(image_embed[0].astype(jnp.float32))
    text_short = text_unit.astype(jnp.bfloat16)
    image_short = image_unit.astype(jnp.bfloat16)
    all_text = lax.all_gather(text_short, "blk", axis=0, tiled=True)
    logits = logit_scale * pair_products(image_short, all_text)
    row_lse = jax.nn.logsumexp(logits, axis=1)
    col_max = jnp.max(logits, axis=0)
    col_sum = jnp.sum(jnp.exp(logits - col_max[None, :]), axis=0)
    col_top, col_total = joined((col_max, col_sum), "blk", combine_parts)
    col_lse = col_top + jnp.log(col_total)
    positions = lax.broadcasted_iota(jnp.int32, (local_rows, group_rows), 1)
    own_rows = lax.broadcasted_iota(jnp.int32, (local_rows, group_rows), 0) + offset
    diagonal_mask = (positions == own_rows).astype(jnp.float32)
    own_col = lax.dynamic_slice_in_dim(col_lse, offset, local_rows, 0)
    loss_local = factor * (
        jnp.sum(row_lse) + jnp.sum(own_col) - 2.0 * jnp.sum(diagonal_mask * logits)
    )
    coef_image = factor * (
        jnp.exp(logits - row_lse[:, None])
        + jnp.exp(logits - col_lse[None, :])
        - 2.0 * diagonal_mask
    )
    scale_local = jnp.sum(coef_image * logits)
    grad_image_unit = logit_scale * jnp.dot(
        coef_image.astype(jnp.bfloat16), all_text, preferred_element_type=jnp.float32
    )
    grad_image = unit_back(image_unit, image_norm, grad_image_unit).astype(jnp.bfloat16)
    row_all = lax.all_gather(row_lse, "blk", axis=0, tiled=True)
    all_image = lax.all_gather(image_short, "blk", axis=0, tiled=True)
    cross_logits = logit_scale * pair_products(text_short, all_image)
    coef_text = factor * (
        jnp.exp(cross_logits - row_all[None, :])
        + jnp.exp(cross_logits - own_col[:, None])
        - 2.0 * diagonal_mask
    )
    grad_text_unit = logit_scale * jnp.dot(
        coef_text.astype(jnp.bfloat16), all_image, preferred_element_type=jnp.float32
    )
    grad_text = unit_back(text_unit, text_norm, grad_text_unit).astype(jnp.bfloat16)
    columns = hidden
    grad_share = lax.psum_scatter(
        lax.dot_general(
            columns, grad_text, (((0,), (0,)), ((), ())), preferred_element_type=jnp.float32
        ),
        "blk",
        scatter_dimension=0,
        tiled=True,
    )
    grad_proj = lax.psum(grad_share, "rep")
    loss_value, scale_grad = lax.psum((loss_local, scale_local), ("blk", "rep"))
    return (
        loss_value.reshape(1),
        scale_grad.reshape(1),
        grad_image[None],
        grad_text[None],
        grad_proj,
    )


def solution(mesh):
    return jax.shard_map(
        on_device,
        mesh=mesh,
        in_specs=(
            P("rep", "blk", None),
            P("rep", "blk", None),
            P("rep", "blk", None),
            P("blk", None),
            P(),
        ),
        out_specs=(P(), P(), P("rep", "blk", None), P("rep", "blk", None), P("blk", None)),
        check_vma=False,
    )
```

profile of v0, /device:TPU:1, one launch (start us, length us, event | category | flops | bytes accessed | tf_op | source)
XLA Modules:
  0.0 263.4 jit_solution(15782971596549169381)
XLA Ops:
  7.2 0.0 copy-start
  7.2 0.0 all-gather.4.cloned.1.call-start
  7.2 0.7 all-gather.4.cloned.1.call-update
  7.9 0.0 reduce-scatter.4.cloned.1.call-start
  8.7 1.2 dynamic-slice
  11.2 1.0 fusion
  12.2 0.9 fusion.28
  13.1 27.1 %all_gather.30 = bf16[192,1280]{1,0:T(8,128)(2,1)S(1)} all-gather(bf16[24,1280]{1,0:T(8,128)(2,1)S(1)} %fusion.28), channel_id=1, replica_groups=mesh['blk'=8,'rep'=4] {'blk'}, dimensions={0}, use_global_device_ids=true | all-gather | bytes 552960 | tf_op jit(solution)/shard_map/all_gather | solution.py:80
  40.2 17.3 %all-gather.4.cloned.1.call-done = bf16[640,1280]{1,0:T(8,128)(2,1)} async-done(((bf16[80,1280]{1,0:T(8,128)(2,1)}), bf16[640,1280]{1,0:T(8,128)(2,1)}) %all-gather.4.cloned.1.call-update) | async-done | bytes 1638416 | tf_op jit(solution)/shard_map/all_gather | solution.py:48
  57.6 0.0 copy-done
  57.6 1.9 multiply_reduce_fusion.2
  59.5 0.1 fusion.29
  59.6 25.4 %all_gather.25 = bf16[192,1280]{1,0:T(8,128)(2,1)S(1)} all-gather(bf16[24,1280]{1,0:T(8,128)(2,1)S(1)} %fusion.29), channel_id=1, replica_groups=mesh['blk'=8,'rep'=4] {'blk'}, dimensions={0}, use_global_device_ids=true | all-gather | bytes 552960 | tf_op jit(solution)/shard_map/all_gather | solution.py:55
  84.9 0.0 copy-start.1
  84.9 0.8 copy-done.1
  85.7 0.4 fusion.30
  86.1 0.3 dynamic-update-slice
  86.4 0.2 exponential_reduce_fusion
  86.6 0.3 dynamic-update-slice.1
  86.9 0.1 fusion.32
  87.0 29.0 %all-reduce.4 = (f32[1536]{0:T(1024)S(1)}, f32[1536]{0:T(1024)S(1)}, f32[192]{0:T(256)S(1)}) all-reduce(f32[1536]{0:T(1024)S(1)} %dynamic-update-slice, f32[1536]{0:T(1024)S(1)} %dynamic-update-slice.1, f32[192]{0:T(256)S(1)} %get-tuple-element.70), channel_id=2, replica_groups=mesh['blk'=8,'rep'=4] {'blk'}, use_global_device_ids=true, to_apply=%add | all-reduce | flops 3264 | bytes 26112
  115.9 0.1 slice.22
  116.0 0.1 slice.23
  116.1 0.1 reshape.60
  116.2 0.1 reshape.61
  116.2 0.3 while.12
  116.6 0.7 fusion.31
  117.2 0.7 multiply_reduce_fusion
  117.9 0.1 divide_convert_fusion
  118.0 0.0 copy-start.4
  118.1 0.6 convolution_bitcast_fusion
  118.7 0.0 copy-done.4
  118.7 3.0 %copy.12 = f32[640,1280]{1,0:T(8,128)} copy(f32[640,1280]{0,1:T(8,128)S(1)} %convolution_bitcast_fusion) | data formatting | bytes 6553600
  121.7 0.0 copy-start.2
  121.7 0.0 copy-start.3
  121.7 0.0 reduce-scatter.4.cloned.1.call-update
  121.7 0.0 all-reduce.7.cloned.1.call-start
  121.8 1.0 copy-done.2
  122.7 0.0 copy-done.3
  122.7 0.4 multiply_reduce_fusion.1
  123.1 85.3 %reduce-scatter.4.cloned.1.call-done = f32[80,1280]{1,0:T(8,128)} async-done(((f32[640,1280]{1,0:T(8,128)}), f32[80,1280]{1,0:T(8,128)}) %reduce-scatter.4.cloned.1.call-update) | async-done | bytes 409616
  208.4 2.1 copy.13
  210.5 0.0 all-reduce.7.cloned.1.call-update
  210.5 0.7 fusion.1
  211.2 0.6 reduce_sum.93
  211.8 0.7 multiply_reduce_fusion.3
  214.5 40.3 %all-reduce.3 = (f32[1]{0:T(128)}, f32[1]{0:T(128)}) all-reduce(f32[1]{0:T(128)} %bitcast.8, f32[1]{0:T(128)} %bitcast.9), channel_id=1, replica_groups=mesh['blk'=8,'rep'=4] {'blk','rep'}, use_global_device_ids=true, to_apply=%region_11.12 | all-reduce | flops 2 | bytes 16 | tf_op jit(solution)/shard_map/psum | solution.py:101
  254.8 0.0 all-reduce.7.cloned.1.call-done
  254.8 2.1 copy.11
  (24 shorter events, 0.2 us)
Async XLA Ops:
  7.2 50.4 %copy-start = (bf16[1,24,640]{2,1,0:T(8,128)(2,1)S(1)}, bf16[1,24,640]{2,1,0:T(8,128)(2,1)}, u32[]{:S(2)}) copy-start(bf16[1,24,640]{2,1,0:T(8,128)(2,1)} %param.8) | copy-start | bytes 92164
  7.2 50.4 %all-gather.4.cloned.1.call-start = ((), (), s32[]{:S(2)}) async-start(), calls=%async_computation.1 | async-start | bytes 1843200 | tf_op jit(solution)/shard_map/all_gather | solution.py:48
  7.9 200.5 %reduce-scatter.4.cloned.1.call-start = ((), (), s32[]{:S(2)}) async-start(), calls=%async_computation.3 | async-start | bytes 3686400
  84.9 0.8 copy-start.1
  118.0 0.6 copy-start.4
  121.7 1.0 copy-start.2
  121.7 1.0 copy-start.3
  121.7 133.1 %all-reduce.7.cloned.1.call-start = ((), (), s32[]{:S(2)}) async-start(), calls=%async_computation.2 | async-start | bytes 1310720 | tf_op jit(solution)/shard_map/psum | solution.py:100
Sparse Core Ops, SparseCore 0:
  10.2 47.3 all-gather.3
  121.8 86.5 reduce-scatter.3
  210.9 32.0 all-reduce.6
where the time goes:
time: 265 us; the launch traced here: 263 us
  blocking collectives  122 us (46%)
  waiting for transfers between devices  103 us (39%)
  between operations  17.8 us (7%)
  local copies, waits for them, and re-layouts  11 us (4%)
  other arithmetic  5.24 us (2%)
  matrix products  3.92 us (1%)
    unnamed x4, waiting for transfers between devices  86 us
    psum x1, blocking collectives, on_device(): loss_value, scale_grad = lax.psum((loss_local, scale_local), ('blk', 'rep'))  40.3 us
    unnamed x1, blocking collectives  29 us
    all_gather x1, blocking collectives, on_device(): all_image = lax.all_gather(image_short, 'blk', axis=0, tiled=True)  27.1 us
    all_gather x1, blocking collectives, on_device(): all_text = lax.all_gather(text_short, 'blk', axis=0, tiled=True)  25.4 us
    all_gather x1, waiting for transfers between devices, on_device(): lax.all_gather(proj_window, 'blk', axis=0, tiled=True)  17.3 us
    unnamed x19, local copies, waits for them, and re-layouts  10.7 us
  transfers between devices with their start and end apart: 3, of which 2 were waited for; matrix products, arithmetic and copies ran while one was open for 2% of the time, Pallas kernels for 0%

commit v1 on v0

--- a/solution.py
+++ b/solution.py
@@ -1,6 +1,10 @@
+import functools
+
 import jax
 import jax.numpy as jnp
 from jax import lax
+from jax.experimental import pallas as pl
+from jax.experimental.pallas import tpu as pltpu
 from jax.sharding import PartitionSpec as P
 
 
@@ -108,9 +112,265 @@
     )
 
 
+F32 = jnp.float32
+BF16 = jnp.bfloat16
+ROWWISE = (((1,), (1,)), ((), ()))
+IN_VMEM = pl.BlockSpec(memory_space=pltpu.VMEM)
+IN_SMEM = pl.BlockSpec(memory_space=pltpu.SMEM)
+
+
+def number(z, x, y, core):
+    return (z * 2 + x) * 4 + y * 2 + core
+
+
+def moved(value, to):
+    places = [(z, x, y, core) for z in range(4) for x in range(2) for y in range(2) for core in range(2)]
+    return lax.ppermute(
+        value, ("blk", "rep"), [(number(*place), number(*to(*place))) for place in places]
+    )
+
+
+def z_near(value):
+    return moved(value, lambda z, x, y, core: (z ^ 1, x, y, core))
+
+
+def z_far(value):
+    return moved(value, lambda z, x, y, core: (z ^ 2, x, y, core))
+
+
+def x_peer(value):
+    return moved(value, lambda z, x, y, core: (z, 1 - x, y, core))
+
+
+def y_peer(value):
+    return moved(value, lambda z, x, y, core: (z, x, 1 - y, core))
+
+
+def core_peer(value):
+    return moved(value, lambda z, x, y, core: (z, x, y, 1 - core))
+
+
+def regroup(value):
+    return moved(value, lambda z, x, y, core: (z, core, y, x))
+
+
+def in_parts(value):
+    high = value.astype(BF16)
+    rest = value - high.astype(F32)
+    middle = rest.astype(BF16)
+    return high, middle, (rest - middle.astype(F32)).astype(BF16)
+
+
+def lanes_of(values, shape):
+    lane = lax.broadcasted_iota(jnp.int32, shape, 1)
+    row = jnp.zeros(shape, F32)
+    for at, value in enumerate(values):
+        row = jnp.where(lane == at, value.astype(F32), row)
+    return row
+
+
+def inverse_norm(values):
+    return lax.rsqrt(jnp.sum(values * values, axis=-1, keepdims=True) + 1e-06)
+
+
+def group_kernel(factor, place, log_scale, *refs):
+    own_rows, peer_rows, own_proj, peer_proj = refs[:4], refs[4:8], refs[8:12], refs[12:16]
+    keep, send, grads = refs[16:19]
+    image, text, hidden, hidden_t, norms, proj, coefs, grad_all, grad_cols, share = refs[19:]
+    z, x, core = place[0], place[1], place[2]
+    rows, depth = own_rows[0].shape[0], own_proj[0].shape[1]
+    width = image.shape[1]
+    half = width // 2
+    for side, (groups, projs) in enumerate(((own_rows, own_proj), (peer_rows, peer_proj))):
+        for step in range(4):
+            start = pl.multiple_of(((z ^ step) * 2 + (core ^ side)) * rows, 8)
+            block = groups[step]
+            image[pl.ds(start, rows), :] = block[:, :width].astype(F32)
+            text[pl.ds(start, rows), :] = block[:, width : 2 * width].astype(F32)
+            hidden[pl.ds(start, rows), :] = block[:, 2 * width :].astype(F32)
+            for column in range(2):
+                start = pl.multiple_of(((z ^ step) * 2 + (x ^ column)) * depth, 16)
+                proj[core ^ side, pl.ds(start, depth), :] = projs[step][column]
+    hidden_short = hidden[...].astype(BF16)
+    for side in range(2):
+        text[:, side * half : (side + 1) * half] += jnp.dot(
+            hidden_short, proj[side], preferred_element_type=F32
+        )
+    hidden_t[...] = hidden[...].T
+    text_inv = inverse_norm(text[...])
+    text[...] = text[...] * text_inv
+    text_short = text[...].astype(BF16)
+    image_inv = inverse_norm(image[...])
+    norms[...] = jnp.broadcast_to(image_inv, norms.shape)
+    image[...] = image[...] * image_inv
+    image_short = image[...].astype(BF16)
+    scale = jnp.exp(jnp.full((1, 1), log_scale[0], F32))
+    logits = scale * lax.dot_general(
+        image_short, text_short, ROWWISE, preferred_element_type=F32
+    )
+    row_max = jnp.max(logits, axis=1, keepdims=True)
+    row_lse = row_max + jnp.log(jnp.sum(jnp.exp(logits - row_max), axis=1, keepdims=True))
+    col_max = jnp.max(logits, axis=0, keepdims=True)
+    col_lse = col_max + jnp.log(jnp.sum(jnp.exp(logits - col_max), axis=0, keepdims=True))
+    eye = (
+        lax.broadcasted_iota(jnp.int32, logits.shape, 0)
+        == lax.broadcasted_iota(jnp.int32, logits.shape, 1)
+    ).astype(F32)
+    coef = factor * (jnp.exp(logits - row_lse) + jnp.exp(logits - col_lse) - 2.0 * eye)
+    loss = factor * (
+        jnp.sum(row_lse, axis=0, keepdims=True)
+        + jnp.sum(col_lse, axis=1, keepdims=True)
+        - 2.0 * jnp.sum(jnp.sum(eye * logits, axis=1, keepdims=True), axis=0, keepdims=True)
+    )
+    scale_grad = jnp.sum(jnp.sum(coef * logits, axis=1, keepdims=True), axis=0, keepdims=True)
+    coefs[...] = coef
+    own = pl.multiple_of((z * 2 + core) * rows, 8)
+    grad_unit = scale * jnp.dot(
+        coefs[pl.ds(own, rows), :].astype(BF16), text_short, preferred_element_type=F32
+    )
+    unit = image[pl.ds(own, rows), :]
+    grads[0] = (
+        (grad_unit - unit * jnp.sum(unit * grad_unit, axis=-1, keepdims=True))
+        * norms[pl.ds(own, rows), :1]
+    ).astype(BF16)
+    grad_unit = scale * jnp.dot(coef.T.astype(BF16), image_short, preferred_element_type=F32)
+    unit = text[...]
+    grad_all[...] = (
+        grad_unit - unit * jnp.sum(unit * grad_unit, axis=-1, keepdims=True)
+    ) * text_inv
+    grads[1] = grad_all[pl.ds(own, rows), :].astype(BF16)
+    for side in range(2):
+        grad_cols[side] = grad_all[:, side * half : (side + 1) * half].astype(BF16)
+    share[...] = jnp.dot(
+        hidden_t[pl.ds(pl.multiple_of(z * 2 * depth, 8), 2 * depth), :].astype(BF16),
+        grad_cols[core],
+        preferred_element_type=F32,
+    )
+    keep[:depth, :] = share[pl.ds(pl.multiple_of(x * depth, 8), depth), :]
+    keep[depth:, :] = lanes_of((loss, scale_grad), (8, half))
+    send[:depth, :] = share[pl.ds(pl.multiple_of((1 - x) * depth, 8), depth), :].astype(BF16)
+    send[depth:, :] = lanes_of(in_parts(loss) + in_parts(scale_grad), (16, half)).astype(BF16)
+
+
+def total_of(parts):
+    parts = parts.astype(F32)
+    return (
+        parts[:, 0:1] + parts[:, 1:2] + parts[:, 2:3],
+        parts[:, 3:4] + parts[:, 4:5] + parts[:, 5:6],
+    )
+
+
+def fold_x(keep, received, send):
+    depth = keep.shape[0] - 8
+    send[:depth, :] = (keep[:depth, :] + received[:depth, :].astype(F32)).astype(BF16)
+    totals = total_of(received[depth:, :])
+    parts = ()
+    for at in range(2):
+        parts += in_parts(keep[depth : depth + 1, at : at + 1] + totals[at][:1])
+    send[depth:, :] = lanes_of(parts, (16, keep.shape[1])).astype(BF16)
+
+
+def fold_y(sent, received, share, totals):
+    depth = share.shape[0]
+    share[...] = sent[:depth, :].astype(F32) + received[:depth, :].astype(F32)
+    ours, theirs = total_of(sent[depth:, :]), total_of(received[depth:, :])
+    totals[...] = lanes_of([(ours[at] + theirs[at])[:1] for at in range(2)], totals.shape)
+
+
+def joined_halves(place, ours, theirs, out):
+    half = ours.shape[1]
+    for side in range(2):
+        @pl.when(place[2] == side)
+        def _():
+            out[:, side * half : (side + 1) * half] = ours[...]
+            out[:, (1 - side) * half : (2 - side) * half] = theirs[...]
+
+
+def on_device_whole_group(image_embed, text_hidden, text_rest, proj_window, log_scale):
+    rows, width = image_embed.shape[1:]
+    depth = proj_window.shape[0]
+    total_rows, total_depth, half = rows * 8, depth * 8, width // 2
+    factor = 1.0 / (2.0 * total_rows * lax.axis_size("rep"))
+    blk, rep = lax.axis_index("blk"), lax.axis_index("rep")
+    z, x, core = blk // 2, blk % 2, rep % 2
+    place = jnp.stack([z, x, core]).astype(jnp.int32)
+
+    def own_and_z(value):
+        far = z_far(value)
+        return value, z_near(value), far, z_near(far)
+
+    our_half = lax.dynamic_slice_in_dim(proj_window, core * half, half, 1)
+    columns = jnp.stack(own_and_z(our_half))
+    our_proj = jnp.stack([columns, x_peer(columns)], axis=1)
+    their_proj = core_peer(our_proj)
+    samples = jnp.concatenate([image_embed[0], text_rest[0], text_hidden[0]], axis=1)
+    our_rows = own_and_z(regroup(samples))
+    their_rows = core_peer(jnp.stack(our_rows))
+
+    keep, send, grads = pl.pallas_call(
+        functools.partial(group_kernel, factor),
+        out_shape=(
+            jax.ShapeDtypeStruct((depth + 8, half), F32),
+            jax.ShapeDtypeStruct((depth + 16, half), BF16),
+            jax.ShapeDtypeStruct((2, rows, width), BF16),
+        ),
+        in_specs=[IN_SMEM] * 2 + [IN_VMEM] * 16,
+        out_specs=[IN_VMEM] * 3,
+        scratch_shapes=[
+            pltpu.VMEM((total_rows, width), F32),
+            pltpu.VMEM((total_rows, width), F32),
+            pltpu.VMEM((total_rows, total_depth), F32),
+            pltpu.VMEM((total_depth, total_rows), F32),
+            pltpu.VMEM((total_rows, 128), F32),
+            pltpu.VMEM((2, total_depth, half), BF16),
+            pltpu.VMEM((total_rows, total_rows), F32),
+            pltpu.VMEM((total_rows, width), F32),
+            pltpu.VMEM((2, total_rows, half), BF16),
+            pltpu.VMEM((2 * depth, half), F32),
+        ],
+        compiler_params=pltpu.CompilerParams(vmem_limit_bytes=40 * 2**20),
+        name="group_kernel",
+    )(
+        place,
+        log_scale,
+        *our_rows,
+        *(their_rows[step] for step in range(4)),
+        *(our_proj[step] for step in range(4)),
+        *(their_proj[step] for step in range(4)),
+    )
+    grads = regroup(grads)
+    folded = pl.pallas_call(
+        fold_x,
+        out_shape=jax.ShapeDtypeStruct(send.shape, BF16),
+        in_specs=[IN_VMEM] * 2,
+        out_specs=IN_VMEM,
+        name="fold_x",
+    )(keep, x_peer(send))
+    share, totals = pl.pallas_call(
+        fold_y,
+        out_shape=(
+            jax.ShapeDtypeStruct((depth, half), F32),
+            jax.ShapeDtypeStruct((8, 128), F32),
+        ),
+        in_specs=[IN_VMEM] * 2,
+        out_specs=[IN_VMEM] * 2,
+        name="fold_y",
+    )(folded, y_peer(folded))
+    grad_proj = pl.pallas_call(
+        joined_halves,
+        out_shape=jax.ShapeDtypeStruct((depth, width), F32),
+        in_specs=[IN_SMEM] + [IN_VMEM] * 2,
+        out_specs=IN_VMEM,
+        name="joined_halves",
+    )(place, share, core_peer(share))
+    return totals[0, 0:1], totals[0, 1:2], grads[0][None], grads[1][None], grad_proj
+
+
 def solution(mesh):
+    sizes = dict(mesh.shape)
+    whole_group = sizes["blk"] == 8 and sizes["rep"] == 4
     return jax.shard_map(
-        on_device,
+        on_device_whole_group if whole_group else on_device,
         mesh=mesh,
         in_specs=(
             P("rep", "blk", None),

time: 265 us -> 61.7 us (0.23)
  blocking collectives: 122 us -> 0 us
  waiting for transfers between devices: 103 us -> 26.9 us
  starting transfers between devices: 0.12 us -> 18.4 us
  between operations: 17.8 us -> 1.46 us
  Pallas kernels: 0 us -> 8.55 us
  local copies, waits for them, and re-layouts: 11 us -> 4.78 us
  matrix products: 3.92 us -> 0 us
  other arithmetic: 5.24 us -> 1.37 us
    unnamed x4 -> x0, waiting for transfers between devices: 86 us -> none
    all_gather x2 -> x0, blocking collectives: 52.5 us -> none  [the longest x1 27.1 us: on_device(): all_image = lax.all_gather(image_short, 'blk', axis=0, tiled=True)]
    psum x1 -> x0, blocking collectives: 40.3 us -> none  [on_device(): loss_value, scale_grad = lax.psum((loss_local, scale_local), ('blk', 'rep'))]
    unnamed x1 -> x0, blocking collectives: 29 us -> none
    ppermute x0 -> x14, waiting for transfers between devices: none -> 26.9 us  [moved(): lax.ppermute(value, ('blk', 'rep'), [(number(*place), number(*to(*place))...]
    ppermute x0 -> x14, starting transfers between devices: none -> 18.4 us  [moved(): lax.ppermute(value, ('blk', 'rep'), [(number(*place), number(*to(*place))...]
    all_gather x1 -> x0, waiting for transfers between devices: 17.3 us -> none  [on_device(): lax.all_gather(proj_window, 'blk', axis=0, tiled=True)]
    pallas_call x0 -> x4, Pallas kernels: none -> 8.55 us  [the longest x1 3.08 us: on_device_whole_group(): pl.pallas_call(functools.partial(group_kernel, factor), out_shape=(jax.Sh...]
  transfers between devices with their start and end apart: 3 -> 14, of which waited for: 2 -> 8; matrix products, arithmetic and copies ran while one was open for 2% -> 4% of each run, Pallas kernels for 0% -> 3%
where the time goes in v1:
time: 61.7 us; the launch traced here: 61.5 us
  waiting for transfers between devices  26.9 us (44%)
  starting transfers between devices  18.4 us (30%)
  Pallas kernels  8.55 us (14%)
  local copies, waits for them, and re-layouts  4.78 us (8%)
  between operations  1.46 us (2%)
  other arithmetic  1.37 us (2%)
    ppermute x14, waiting for transfers between devices, moved(): lax.ppermute(value, ('blk', 'rep'), [(number(*place), number(*to(*place))...  26.9 us
    ppermute x14, starting transfers between devices, moved(): lax.ppermute(value, ('blk', 'rep'), [(number(*place), number(*to(*place))...  18.4 us
    pallas_call x1, Pallas kernels, on_device_whole_group(): pl.pallas_call(functools.partial(group_kernel, factor), out_shape=(jax.Sh...  3.08 us
    unnamed x12, local copies, waits for them, and re-layouts  2.66 us
    pallas_call x1, Pallas kernels, on_device_whole_group(): pl.pallas_call(fold_x, out_shape=jax.ShapeDtypeStruct(send.shape, BF16),...  1.91 us
    pallas_call x1, Pallas kernels, on_device_whole_group(): pl.pallas_call(joined_halves, out_shape=jax.ShapeDtypeStruct((depth, widt...  1.83 us
    pallas_call x1, Pallas kernels, on_device_whole_group(): pl.pallas_call(fold_y, out_shape=(jax.ShapeDtypeStruct((depth, half), F32...  1.73 us
    slice x1, local copies, waits for them, and re-layouts, on_device_whole_group(): totals[0, 1:2]  1.33 us
  transfers between devices with their start and end apart: 14, of which 8 were waited for; matrix products, arithmetic and copies ran while one was open for 4% of the time, Pallas kernels for 3%

profile of v1, /device:TPU:1, one launch (start us, length us, event | category | flops | bytes accessed | tf_op | source)
XLA Modules:
  0.0 61.5 jit_solution(16990846571638284032)
XLA Ops:
  0.6 0.0 copy-start
  0.6 0.9 %pad_maximum_fusion.3 = bf16[24,3200]{1,0:T(8,128)(2,1)S(1)} fusion(bf16[24,640]{1,0:T(8,128)(2,1)} %bitcast.57, bf16[24,1280]{1,0:T(8,128)(2,1)} %bitcast.55, bf16[24,1280]{1,0:T(8,128)(2,1)} %bitcast.56), kind=kLoop, calls=%fused_computation.27 | loop fusion | flops 460800 | bytes 307200 | tf_op jit(solution)/shard_map/concatenate | solution.py:306
  1.6 4.5 %collective-permute-start = (bf16[24,3200]{1,0:T(8,128)(2,1)S(1)}, bf16[24,3200]{1,0:T(8,128)(2,1)S(1)}, u32[]{:S(2)}, u32[]{:S(2)}) collective-permute-start(bf16[24,3200]{1,0:T(8,128)(2,1)S(1)} %pad_maximum_fusion.3), channel_id=1, source_target_pairs={{0,0},{1,4},{2,2},{3,6},{4,1},{5,5},{6,3},{7,7},{8,8},{9,12},{10,1... | collective-permute-start | bytes 460808 | tf_op jit(solution)/shard_map/ppermute | solution.py:128
  6.1 3.2 %collective-permute-done.refs_0_ = bf16[24,3200]{1,0:T(8,128)(2,1)S(1)} collective-permute-done((bf16[24,3200]{1,0:T(8,128)(2,1)S(1)}, bf16[24,3200]{1,0:T(8,128)(2,1)S(1)}, u32[]{:S(2)}, u32[]{:S(2)}) %collective-permute-start) | collective-permute-done | bytes 153632 | tf_op jit(solution)/shard_map/ppermute | solution.py:128
  9.3 2.3 %collective-permute-start.2 = (bf16[24,3200]{1,0:T(8,128)(2,1)S(1)}, bf16[24,3200]{1,0:T(8,128)(2,1)S(1)}, u32[]{:S(2)}, u32[]{:S(2)}) collective-permute-start(bf16[24,3200]{1,0:T(8,128)(2,1)S(1)} %collective-permute-done.refs_0_), channel_id=1, source_target_pairs={{0,16},{1,17},{2,18},{3,19},{4,20},{5,21},{6,22},{7,23},{8,24},{9,... | collective-permute-start | bytes 460808 | tf_op jit(solution)/shard_map/ppermute | solution.py:128
  11.6 0.0 copy-done
  11.6 0.1 collective-permute-start.6
  11.7 1.3 %collective-permute-start.5 = (bf16[80,640]{1,0:T(8,128)(2,1)S(1)}, bf16[80,640]{1,0:T(8,128)(2,1)S(1)}, u32[]{:S(2)}, u32[]{:S(2)}) collective-permute-start(bf16[80,640]{1,0:T(8,128)(2,1)S(1)} %constant_dynamic-slice_fusion), channel_id=1, source_target_pairs={{0,8},{1,9},{2,10},{3,11},{4,12},{5,13},{6,14},{7,15},{8,0},{9,1},... | collective-permute-start | bytes 307208 | tf_op jit(solution)/shard_map/ppermute | solution.py:128
  13.0 5.2 %collective-permute-done.6 = bf16[80,640]{1,0:T(8,128)(2,1)S(1)} collective-permute-done((bf16[80,640]{1,0:T(8,128)(2,1)S(1)}, bf16[80,640]{1,0:T(8,128)(2,1)S(1)}, u32[]{:S(2)}, u32[]{:S(2)}) %collective-permute-start.6) | collective-permute-done | bytes 102432 | tf_op jit(solution)/shard_map/ppermute | solution.py:128
  18.3 1.1 %collective-permute-start.7 = (bf16[80,640]{1,0:T(8,128)(2,1)S(1)}, bf16[80,640]{1,0:T(8,128)(2,1)S(1)}, u32[]{:S(2)}, u32[]{:S(2)}) collective-permute-start(bf16[80,640]{1,0:T(8,128)(2,1)S(1)} %collective-permute-done.6), channel_id=1, source_target_pairs={{0,8},{1,9},{2,10},{3,11},{4,12},{5,13},{6,14},{7,15},{8,0},{9,1},... | collective-permute-start | bytes 307208 | tf_op jit(solution)/shard_map/ppermute | solution.py:128
  19.4 0.4 collective-permute-start.1
  19.7 0.0 collective-permute-done.2.refs_2_
  19.7 1.1 %collective-permute-start.3 = (bf16[24,3200]{1,0:T(8,128)(2,1)S(1)}, bf16[24,3200]{1,0:T(8,128)(2,1)S(1)}, u32[]{:S(2)}, u32[]{:S(2)}) collective-permute-start(bf16[24,3200]{1,0:T(8,128)(2,1)S(1)} %collective-permute-done.2.refs_2_), channel_id=1, source_target_pairs={{0,8},{1,9},{2,10},{3,11},{4,12},{5,13},{6,14},{7,15},{8,0},{9,1},... | collective-permute-start | bytes 460808 | tf_op jit(solution)/shard_map/ppermute | solution.py:128
  20.8 0.0 collective-permute-done.5
  20.8 2.3 %collective-permute-done.7 = bf16[80,640]{1,0:T(8,128)(2,1)S(1)} collective-permute-done((bf16[80,640]{1,0:T(8,128)(2,1)S(1)}, bf16[80,640]{1,0:T(8,128)(2,1)S(1)}, u32[]{:S(2)}, u32[]{:S(2)}) %collective-permute-start.7) | collective-permute-done | bytes 102432 | tf_op jit(solution)/shard_map/ppermute | solution.py:128
  23.2 0.1 pad_maximum_fusion.2
  23.3 0.1 collective-permute-start.8
  23.3 3.1 %collective-permute-done.1.refs_1_ = bf16[24,3200]{1,0:T(8,128)(2,1)S(1)} collective-permute-done((bf16[24,3200]{1,0:T(8,128)(2,1)S(1)}, bf16[24,3200]{1,0:T(8,128)(2,1)S(1)}, u32[]{:S(2)}, u32[]{:S(2)}) %collective-permute-start.1) | collective-permute-done | bytes 153632 | tf_op jit(solution)/shard_map/ppermute | solution.py:128
  26.5 2.1 %collective-permute-done.3.refs_3_ = bf16[24,3200]{1,0:T(8,128)(2,1)S(1)} collective-permute-done((bf16[24,3200]{1,0:T(8,128)(2,1)S(1)}, bf16[24,3200]{1,0:T(8,128)(2,1)S(1)}, u32[]{:S(2)}, u32[]{:S(2)}) %collective-permute-start.3) | collective-permute-done | bytes 153632 | tf_op jit(solution)/shard_map/ppermute | solution.py:128
  28.5 0.1 pad_maximum_fusion.1
  28.6 0.1 collective-permute-start.4
  29.4 0.1 pad_add_fusion.place
  29.5 0.0 copy-start.2
  29.5 4.7 %collective-permute-done.8 = bf16[4,80,640]{2,1,0:T(8,128)(2,1)S(1)} collective-permute-done((bf16[4,80,640]{2,1,0:T(8,128)(2,1)S(1)}, bf16[4,80,640]{2,1,0:T(8,128)(2,1)S(1)}, u32[]{:S(2)}, u32[]{:S(2)}) %collective-permute-start.8) | collective-permute-done | bytes 409632 | tf_op jit(solution)/shard_map/ppermute | solution.py:128
  34.1 0.1 pad_maximum_fusion
  34.2 1.1 %collective-permute-start.9 = (bf16[4,2,80,640]{3,2,1,0:T(8,128)(2,1)S(1)}, bf16[4,2,80,640]{3,2,1,0:T(8,128)(2,1)S(1)}, u32[]{:S(2)}, u32[]{:S(2)}) collective-permute-start(bf16[4,2,80,640]{3,2,1,0:T(8,128)(2,1)S(1)} %pad_maximum_fusion), channel_id=1, source_target_pairs={{0,1},{1,0},{2,3},{3,2},{4,5},{5,4},{6,7},{7,6},{8,9},{9,8},{10,11... | collective-permute-start | bytes 2457608 | tf_op jit(solution)/shard_map/ppermute | solution.py:128
  35.4 0.1 fusion.7
  35.5 0.0 collective-permute-done.4
  35.5 1.8 %collective-permute-done.9 = bf16[4,2,80,640]{3,2,1,0:T(8,128)(2,1)S(1)} collective-permute-done((bf16[4,2,80,640]{3,2,1,0:T(8,128)(2,1)S(1)}, bf16[4,2,80,640]{3,2,1,0:T(8,128)(2,1)S(1)}, u32[]{:S(2)}, u32[]{:S(2)}) %collective-permute-start.9) | collective-permute-done | bytes 819232 | tf_op jit(solution)/shard_map/ppermute | solution.py:128
  37.3 0.1 slice_bitcast_fusion
  37.4 0.0 copy-done.2
  37.4 3.1 %group_kernel.1 = (f32[88,640]{1,0:T(8,128)S(1)}, bf16[96,640]{1,0:T(8,128)(2,1)S(1)}, bf16[2,24,1280]{2,1,0:T(8,128)(2,1)S(1)}) custom-call(s32[3]{0:T(128)S(1)} %pad_add_fusion.place, f32[1]{0:T(128)S(6)} %copy.11.log_scale, bf16[24,3200]{1,0:T(8,128)(2,1)S(1)} %collective-permute-done.refs_0_, bf16[24,3200]{1,0:T(8,128)(2,1)S(1)} %collective-permute-done.1.refs_1_, ...), custom_call_target="tpu_custom_call" | custom-call | tf_op jit(solution)/shard_map/group_kernel/pallas_call | solution.py:310
  40.5 0.0 copy-start.1
  40.5 0.7 %copy-done.1 = f32[88,640]{1,0:T(8,128)} copy-done((f32[88,640]{1,0:T(8,128)}, f32[88,640]{1,0:T(8,128)S(1)}, u32[]{:S(2)}) %copy-start.1) | copy-done | bytes 225304
  41.2 0.0 collective-permute-start.10
  41.2 4.5 %collective-permute-done.10.received = bf16[96,640]{1,0:T(8,128)(2,1)S(1)} collective-permute-done((bf16[96,640]{1,0:T(8,128)(2,1)S(1)}, bf16[96,640]{1,0:T(8,128)(2,1)S(1)}, u32[]{:S(2)}, u32[]{:S(2)}) %collective-permute-start.10) | collective-permute-done | bytes 122912 | tf_op jit(solution)/shard_map/ppermute | solution.py:128
  45.7 0.0 copy-start.4
  45.7 0.6 %copy-done.4 = bf16[96,640]{1,0:T(8,128)(2,1)} copy-done((bf16[96,640]{1,0:T(8,128)(2,1)}, bf16[96,640]{1,0:T(8,128)(2,1)S(1)}, u32[]{:S(2)}) %copy-start.4) | copy-done | bytes 122904
  46.4 1.9 %fold_x.1.sent = bf16[96,640]{1,0:T(8,128)(2,1)} custom-call(f32[88,640]{1,0:T(8,128)} %copy-done.1, bf16[96,640]{1,0:T(8,128)(2,1)} %copy-done.4), custom_call_target="tpu_custom_call" | custom-call | tf_op jit(solution)/shard_map/fold_x/pallas_call | solution.py:342
  48.3 1.5 %collective-permute-start.11 = (bf16[96,640]{1,0:T(8,128)(2,1)}, bf16[96,640]{1,0:T(8,128)(2,1)S(1)}, u32[]{:S(2)}, u32[]{:S(2)}) collective-permute-start(bf16[96,640]{1,0:T(8,128)(2,1)} %fold_x.1.sent), channel_id=1, source_target_pairs={{0,2},{1,3},{2,0},{3,1},{4,6},{5,7},{6,4},{7,5},{8,10},{9,11},{10,... | collective-permute-start | bytes 368648 | tf_op jit(solution)/shard_map/ppermute | solution.py:128
  49.8 3.3 %collective-permute-start.12 = (bf16[2,24,1280]{2,1,0:T(8,128)(2,1)S(1)}, bf16[2,24,1280]{2,1,0:T(8,128)(2,1)S(1)}, u32[]{:S(2)}, u32[]{:S(2)}) collective-permute-start(bf16[2,24,1280]{2,1,0:T(8,128)(2,1)S(1)} %get-tuple-element.13), channel_id=1, source_target_pairs={{0,0},{1,4},{2,2},{3,6},{4,1},{5,5},{6,3},{7,7},{8,8},{9,12},{10,1... | collective-permute-start | bytes 368648 | tf_op jit(solution)/shard_map/ppermute | solution.py:128
  53.1 0.0 collective-permute-done.11.received
  53.1 0.0 copy-start.5
  53.1 0.6 %copy-done.5 = bf16[96,640]{1,0:T(8,128)(2,1)} copy-done((bf16[96,640]{1,0:T(8,128)(2,1)}, bf16[96,640]{1,0:T(8,128)(2,1)S(1)}, u32[]{:S(2)}) %copy-start.5) | copy-done | bytes 122904
  53.7 1.7 %fold_y.1 = (f32[80,640]{1,0:T(8,128)}, f32[8,128]{1,0:T(8,128)}) custom-call(bf16[96,640]{1,0:T(8,128)(2,1)} %fold_x.1.sent, bf16[96,640]{1,0:T(8,128)(2,1)} %copy-done.5), custom_call_target="tpu_custom_call" | custom-call | tf_op jit(solution)/shard_map/fold_y/pallas_call | solution.py:349
  55.5 1.5 %collective-permute-start.13 = (f32[80,640]{1,0:T(8,128)}, f32[80,640]{1,0:T(8,128)S(1)}, u32[]{:S(2)}, u32[]{:S(2)}) collective-permute-start(f32[80,640]{1,0:T(8,128)} %get-tuple-element.14.ours), channel_id=1, source_target_pairs={{0,1},{1,0},{2,3},{3,2},{4,5},{5,4},{6,7},{7,6},{8,9},{9,8},{10,11... | collective-permute-start | bytes 614408 | tf_op jit(solution)/shard_map/ppermute | solution.py:128
  57.0 0.0 collective-permute-done.12
  57.0 0.7 %fusion.9 = (bf16[1,24,1280]{2,1,0:T(8,128)(2,1)}, bf16[1,24,1280]{2,1,0:T(8,128)(2,1)}) fusion(bf16[2,24,1280]{2,1,0:T(8,128)(2,1)S(1)} %collective-permute-done.12), kind=kLoop, calls=%fused_computation.31 | loop fusion | bytes 245760 | tf_op jit(solution)/shard_map/slice | solution.py:366
  57.6 1.3 %fusion.10 = (f32[1,1]{1,0:T(1,128)}, f32[1,1]{1,0:T(1,128)}) fusion(f32[8,128]{1,0:T(8,128)} %get-tuple-element.12), kind=kLoop, calls=%fused_computation.32 | loop fusion | bytes 16 | tf_op jit(solution)/shard_map/slice | solution.py:366
  58.9 0.0 collective-permute-done.13.theirs
  58.9 0.0 copy-start.3
  58.9 0.7 %copy-done.3 = f32[80,640]{1,0:T(8,128)} copy-done((f32[80,640]{1,0:T(8,128)}, f32[80,640]{1,0:T(8,128)S(1)}, u32[]{:S(2)}) %copy-start.3) | copy-done | bytes 204824
  59.6 1.8 %joined_halves.1 = f32[80,1280]{1,0:T(8,128)} custom-call(s32[3]{0:T(128)} %copy-done.2, f32[80,640]{1,0:T(8,128)} %get-tuple-element.14.ours, f32[80,640]{1,0:T(8,128)} %copy-done.3), custom_call_target="tpu_custom_call" | custom-call | tf_op jit(solution)/shard_map/joined_halves/pallas_call | solution.py:359
  (3 shorter events, 0.1 us)
Async XLA Ops:
  0.6 11.0 %copy-start = (bf16[80,1280]{1,0:T(8,128)(2,1)S(1)}, bf16[80,1280]{1,0:T(8,128)(2,1)}, u32[]{:S(2)}) copy-start(bf16[80,1280]{1,0:T(8,128)(2,1)} %param.8) | copy-start | bytes 614404
  1.6 7.7 %collective-permute-start = (bf16[24,3200]{1,0:T(8,128)(2,1)S(1)}, bf16[24,3200]{1,0:T(8,128)(2,1)S(1)}, u32[]{:S(2)}, u32[]{:S(2)}) collective-permute-start(bf16[24,3200]{1,0:T(8,128)(2,1)S(1)} %pad_maximum_fusion.3), channel_id=1, source_target_pairs={{0,0},{1,4},{2,2},{3,6},{4,1},{5,5},{6,3},{7,7},{8,8},{9,12},{10,1... | collective-permute-start | bytes 460808 | tf_op jit(solution)/shard_map/ppermute | solution.py:128
  9.3 10.5 %collective-permute-start.2 = (bf16[24,3200]{1,0:T(8,128)(2,1)S(1)}, bf16[24,3200]{1,0:T(8,128)(2,1)S(1)}, u32[]{:S(2)}, u32[]{:S(2)}) collective-permute-start(bf16[24,3200]{1,0:T(8,128)(2,1)S(1)} %collective-permute-done.refs_0_), channel_id=1, source_target_pairs={{0,16},{1,17},{2,18},{3,19},{4,20},{5,21},{6,22},{7,23},{8,24},{9,... | collective-permute-start | bytes 460808 | tf_op jit(solution)/shard_map/ppermute | solution.py:128
  11.6 6.7 %collective-permute-start.6 = (bf16[80,640]{1,0:T(8,128)(2,1)S(1)}, bf16[80,640]{1,0:T(8,128)(2,1)S(1)}, u32[]{:S(2)}, u32[]{:S(2)}) collective-permute-start(bf16[80,640]{1,0:T(8,128)(2,1)S(1)} %constant_dynamic-slice_fusion), channel_id=1, source_target_pairs={{0,16},{1,17},{2,18},{3,19},{4,20},{5,21},{6,22},{7,23},{8,24},{9,... | collective-permute-start | bytes 307208 | tf_op jit(solution)/shard_map/ppermute | solution.py:128
  11.7 9.1 %collective-permute-start.5 = (bf16[80,640]{1,0:T(8,128)(2,1)S(1)}, bf16[80,640]{1,0:T(8,128)(2,1)S(1)}, u32[]{:S(2)}, u32[]{:S(2)}) collective-permute-start(bf16[80,640]{1,0:T(8,128)(2,1)S(1)} %constant_dynamic-slice_fusion), channel_id=1, source_target_pairs={{0,8},{1,9},{2,10},{3,11},{4,12},{5,13},{6,14},{7,15},{8,0},{9,1},... | collective-permute-start | bytes 307208 | tf_op jit(solution)/shard_map/ppermute | solution.py:128
  18.3 4.9 %collective-permute-start.7 = (bf16[80,640]{1,0:T(8,128)(2,1)S(1)}, bf16[80,640]{1,0:T(8,128)(2,1)S(1)}, u32[]{:S(2)}, u32[]{:S(2)}) collective-permute-start(bf16[80,640]{1,0:T(8,128)(2,1)S(1)} %collective-permute-done.6), channel_id=1, source_target_pairs={{0,8},{1,9},{2,10},{3,11},{4,12},{5,13},{6,14},{7,15},{8,0},{9,1},... | collective-permute-start | bytes 307208 | tf_op jit(solution)/shard_map/ppermute | solution.py:128
  19.4 7.1 %collective-permute-start.1 = (bf16[24,3200]{1,0:T(8,128)(2,1)S(1)}, bf16[24,3200]{1,0:T(8,128)(2,1)S(1)}, u32[]{:S(2)}, u32[]{:S(2)}) collective-permute-start(bf16[24,3200]{1,0:T(8,128)(2,1)S(1)} %collective-permute-done.refs_0_), channel_id=1, source_target_pairs={{0,8},{1,9},{2,10},{3,11},{4,12},{5,13},{6,14},{7,15},{8,0},{9,1},... | collective-permute-start | bytes 460808 | tf_op jit(solution)/shard_map/ppermute | solution.py:128
  19.7 8.8 %collective-permute-start.3 = (bf16[24,3200]{1,0:T(8,128)(2,1)S(1)}, bf16[24,3200]{1,0:T(8,128)(2,1)S(1)}, u32[]{:S(2)}, u32[]{:S(2)}) collective-permute-start(bf16[24,3200]{1,0:T(8,128)(2,1)S(1)} %collective-permute-done.2.refs_2_), channel_id=1, source_target_pairs={{0,8},{1,9},{2,10},{3,11},{4,12},{5,13},{6,14},{7,15},{8,0},{9,1},... | collective-permute-start | bytes 460808 | tf_op jit(solution)/shard_map/ppermute | solution.py:128
  23.3 10.9 %collective-permute-start.8 = (bf16[4,80,640]{2,1,0:T(8,128)(2,1)S(1)}, bf16[4,80,640]{2,1,0:T(8,128)(2,1)S(1)}, u32[]{:S(2)}, u32[]{:S(2)}) collective-permute-start(bf16[4,80,640]{2,1,0:T(8,128)(2,1)S(1)} %get-tuple-element.27), channel_id=1, source_target_pairs={{0,4},{1,5},{2,6},{3,7},{4,0},{5,1},{6,2},{7,3},{8,12},{9,13},{10,... | collective-permute-start | bytes 1228808 | tf_op jit(solution)/shard_map/ppermute | solution.py:128
  28.6 6.8 %collective-permute-start.4 = (bf16[4,24,3200]{2,1,0:T(8,128)(2,1)S(1)}, bf16[4,24,3200]{2,1,0:T(8,128)(2,1)S(1)}, u32[]{:S(2)}, u32[]{:S(2)}) collective-permute-start(bf16[4,24,3200]{2,1,0:T(8,128)(2,1)S(1)} %pad_maximum_fusion.1), channel_id=1, source_target_pairs={{0,1},{1,0},{2,3},{3,2},{4,5},{5,4},{6,7},{7,6},{8,9},{9,8},{10,11... | collective-permute-start | bytes 1843208 | tf_op jit(solution)/shard_map/ppermute | solution.py:128
  29.5 7.9 %copy-start.2 = (s32[3]{0:T(128)}, s32[3]{0:T(128)S(1)}, u32[]{:S(2)}) copy-start(s32[3]{0:T(128)S(1)} %pad_add_fusion.place) | copy-start | bytes 40
  34.2 3.1 %collective-permute-start.9 = (bf16[4,2,80,640]{3,2,1,0:T(8,128)(2,1)S(1)}, bf16[4,2,80,640]{3,2,1,0:T(8,128)(2,1)S(1)}, u32[]{:S(2)}, u32[]{:S(2)}) collective-permute-start(bf16[4,2,80,640]{3,2,1,0:T(8,128)(2,1)S(1)} %pad_maximum_fusion), channel_id=1, source_target_pairs={{0,1},{1,0},{2,3},{3,2},{4,5},{5,4},{6,7},{7,6},{8,9},{9,8},{10,11... | collective-permute-start | bytes 2457608 | tf_op jit(solution)/shard_map/ppermute | solution.py:128
  40.5 0.7 %copy-start.1 = (f32[88,640]{1,0:T(8,128)}, f32[88,640]{1,0:T(8,128)S(1)}, u32[]{:S(2)}) copy-start(f32[88,640]{1,0:T(8,128)S(1)} %get-tuple-element.10.keep) | copy-start | bytes 675844
  41.2 4.5 %collective-permute-start.10 = (bf16[96,640]{1,0:T(8,128)(2,1)S(1)}, bf16[96,640]{1,0:T(8,128)(2,1)S(1)}, u32[]{:S(2)}, u32[]{:S(2)}) collective-permute-start(bf16[96,640]{1,0:T(8,128)(2,1)S(1)} %get-tuple-element.11), channel_id=1, source_target_pairs={{0,4},{1,5},{2,6},{3,7},{4,0},{5,1},{6,2},{7,3},{8,12},{9,13},{10,... | collective-permute-start | bytes 368648 | tf_op jit(solution)/shard_map/ppermute | solution.py:128
  45.7 0.6 %copy-start.4 = (bf16[96,640]{1,0:T(8,128)(2,1)}, bf16[96,640]{1,0:T(8,128)(2,1)S(1)}, u32[]{:S(2)}) copy-start(bf16[96,640]{1,0:T(8,128)(2,1)S(1)} %collective-permute-done.10.received) | copy-start | bytes 368644
  48.3 4.8 %collective-permute-start.11 = (bf16[96,640]{1,0:T(8,128)(2,1)}, bf16[96,640]{1,0:T(8,128)(2,1)S(1)}, u32[]{:S(2)}, u32[]{:S(2)}) collective-permute-start(bf16[96,640]{1,0:T(8,128)(2,1)} %fold_x.1.sent), channel_id=1, source_target_pairs={{0,2},{1,3},{2,0},{3,1},{4,6},{5,7},{6,4},{7,5},{8,10},{9,11},{10,... | collective-permute-start | bytes 368648 | tf_op jit(solution)/shard_map/ppermute | solution.py:128
  49.8 7.2 %collective-permute-start.12 = (bf16[2,24,1280]{2,1,0:T(8,128)(2,1)S(1)}, bf16[2,24,1280]{2,1,0:T(8,128)(2,1)S(1)}, u32[]{:S(2)}, u32[]{:S(2)}) collective-permute-start(bf16[2,24,1280]{2,1,0:T(8,128)(2,1)S(1)} %get-tuple-element.13), channel_id=1, source_target_pairs={{0,0},{1,4},{2,2},{3,6},{4,1},{5,5},{6,3},{7,7},{8,8},{9,12},{10,1... | collective-permute-start | bytes 368648 | tf_op jit(solution)/shard_map/ppermute | solution.py:128
  53.1 0.7 %copy-start.5 = (bf16[96,640]{1,0:T(8,128)(2,1)}, bf16[96,640]{1,0:T(8,128)(2,1)S(1)}, u32[]{:S(2)}) copy-start(bf16[96,640]{1,0:T(8,128)(2,1)S(1)} %collective-permute-done.11.received) | copy-start | bytes 368644
  55.5 3.5 %collective-permute-start.13 = (f32[80,640]{1,0:T(8,128)}, f32[80,640]{1,0:T(8,128)S(1)}, u32[]{:S(2)}, u32[]{:S(2)}) collective-permute-start(f32[80,640]{1,0:T(8,128)} %get-tuple-element.14.ours), channel_id=1, source_target_pairs={{0,1},{1,0},{2,3},{3,2},{4,5},{5,4},{6,7},{7,6},{8,9},{9,8},{10,11... | collective-permute-start | bytes 614408 | tf_op jit(solution)/shard_map/ppermute | solution.py:128
  58.9 0.7 %copy-start.3 = (f32[80,640]{1,0:T(8,128)}, f32[80,640]{1,0:T(8,128)S(1)}, u32[]{:S(2)}) copy-start(f32[80,640]{1,0:T(8,128)S(1)} %collective-permute-done.13.theirs) | copy-start | bytes 614404

commit v2 on v1

--- a/solution.py
+++ b/solution.py
@@ -117,6 +117,7 @@
 ROWWISE = (((1,), (1,)), ((), ()))
 IN_VMEM = pl.BlockSpec(memory_space=pltpu.VMEM)
 IN_SMEM = pl.BlockSpec(memory_space=pltpu.SMEM)
+PROJ_ORDER = ((0, 0), (0, 1), (1, 0), (2, 0), (1, 1), (2, 1), (3, 0), (3, 1))
 
 
 def number(z, x, y, core):
@@ -161,11 +162,11 @@
     return high, middle, (rest - middle.astype(F32)).astype(BF16)
 
 
-def lanes_of(values, shape):
+def lanes_of(values, group, shape):
     lane = lax.broadcasted_iota(jnp.int32, shape, 1)
     row = jnp.zeros(shape, F32)
     for at, value in enumerate(values):
-        row = jnp.where(lane == at, value.astype(F32), row)
+        row = jnp.where(lane == at * 4 + group, value.astype(F32), row)
     return row
 
 
@@ -174,23 +175,24 @@
 
 
 def group_kernel(factor, place, log_scale, *refs):
-    own_rows, peer_rows, own_proj, peer_proj = refs[:4], refs[4:8], refs[8:12], refs[12:16]
-    keep, send, grads = refs[16:19]
-    image, text, hidden, hidden_t, norms, proj, coefs, grad_all, grad_cols, share = refs[19:]
-    z, x, core = place[0], place[1], place[2]
-    rows, depth = own_rows[0].shape[0], own_proj[0].shape[1]
+    rows_here, rows_there, projs = refs[:4], refs[4:8], refs[8:24]
+    keep, send, grads = refs[24:27]
+    image, text, hidden, hidden_t, norms, proj, coefs, grad_all, grad_cols, share = refs[27:]
+    z, x, y, core = (place[at] for at in range(4))
+    rows, depth = rows_here[0].shape[0], projs[0].shape[0]
     width = image.shape[1]
     half = width // 2
-    for side, (groups, projs) in enumerate(((own_rows, own_proj), (peer_rows, peer_proj))):
+    for side, groups in enumerate((rows_here, rows_there)):
         for step in range(4):
             start = pl.multiple_of(((z ^ step) * 2 + (core ^ side)) * rows, 8)
             block = groups[step]
             image[pl.ds(start, rows), :] = block[:, :width].astype(F32)
             text[pl.ds(start, rows), :] = block[:, width : 2 * width].astype(F32)
             hidden[pl.ds(start, rows), :] = block[:, 2 * width :].astype(F32)
-            for column in range(2):
-                start = pl.multiple_of(((z ^ step) * 2 + (x ^ column)) * depth, 16)
-                proj[core ^ side, pl.ds(start, depth), :] = projs[step][column]
+    for side in range(2):
+        for at, (step, column) in enumerate(PROJ_ORDER):
+            start = pl.multiple_of(((z ^ step) * 2 + (x ^ column)) * depth, 16)
+            proj[core ^ side, pl.ds(start, depth), :] = projs[side * 8 + at][...]
     hidden_short = hidden[...].astype(BF16)
     for side in range(2):
         text[:, side * half : (side + 1) * half] += jnp.dot(
@@ -246,44 +248,11 @@
         grad_cols[core],
         preferred_element_type=F32,
     )
+    totals = lanes_of(in_parts(loss) + in_parts(scale_grad), 2 * y + x, (16, half))
     keep[:depth, :] = share[pl.ds(pl.multiple_of(x * depth, 8), depth), :]
-    keep[depth:, :] = lanes_of((loss, scale_grad), (8, half))
+    keep[depth:, :] = totals
     send[:depth, :] = share[pl.ds(pl.multiple_of((1 - x) * depth, 8), depth), :].astype(BF16)
-    send[depth:, :] = lanes_of(in_parts(loss) + in_parts(scale_grad), (16, half)).astype(BF16)
-
-
-def total_of(parts):
-    parts = parts.astype(F32)
-    return (
-        parts[:, 0:1] + parts[:, 1:2] + parts[:, 2:3],
-        parts[:, 3:4] + parts[:, 4:5] + parts[:, 5:6],
-    )
-
-
-def fold_x(keep, received, send):
-    depth = keep.shape[0] - 8
-    send[:depth, :] = (keep[:depth, :] + received[:depth, :].astype(F32)).astype(BF16)
-    totals = total_of(received[depth:, :])
-    parts = ()
-    for at in range(2):
-        parts += in_parts(keep[depth : depth + 1, at : at + 1] + totals[at][:1])
-    send[depth:, :] = lanes_of(parts, (16, keep.shape[1])).astype(BF16)
-
-
-def fold_y(sent, received, share, totals):
-    depth = share.shape[0]
-    share[...] = sent[:depth, :].astype(F32) + received[:depth, :].astype(F32)
-    ours, theirs = total_of(sent[depth:, :]), total_of(received[depth:, :])
-    totals[...] = lanes_of([(ours[at] + theirs[at])[:1] for at in range(2)], totals.shape)
-
-
-def joined_halves(place, ours, theirs, out):
-    half = ours.shape[1]
-    for side in range(2):
-        @pl.when(place[2] == side)
-        def _():
-            out[:, side * half : (side + 1) * half] = ours[...]
-            out[:, (1 - side) * half : (2 - side) * half] = theirs[...]
+    send[depth:, :] = totals.astype(BF16)
 
 
 def on_device_whole_group(image_embed, text_hidden, text_rest, proj_window, log_scale):
@@ -292,29 +261,42 @@
     total_rows, total_depth, half = rows * 8, depth * 8, width // 2
     factor = 1.0 / (2.0 * total_rows * lax.axis_size("rep"))
     blk, rep = lax.axis_index("blk"), lax.axis_index("rep")
-    z, x, core = blk // 2, blk % 2, rep % 2
-    place = jnp.stack([z, x, core]).astype(jnp.int32)
+    z, x, y, core = blk // 2, blk % 2, rep // 2, rep % 2
+    place = jnp.stack([z, x, y, core]).astype(jnp.int32)
 
     def own_and_z(value):
         far = z_far(value)
         return value, z_near(value), far, z_near(far)
 
-    our_half = lax.dynamic_slice_in_dim(proj_window, core * half, half, 1)
-    columns = jnp.stack(own_and_z(our_half))
-    our_proj = jnp.stack([columns, x_peer(columns)], axis=1)
-    their_proj = core_peer(our_proj)
+    own_proj = lax.dynamic_slice_in_dim(proj_window, core * half, half, 1)
+    far_proj, near_proj, x_proj = z_far(own_proj), z_near(own_proj), x_peer(own_proj)
     samples = jnp.concatenate([image_embed[0], text_rest[0], text_hidden[0]], axis=1)
-    our_rows = own_and_z(regroup(samples))
-    their_rows = core_peer(jnp.stack(our_rows))
+    own_rows = regroup(samples)
+    own_rows, near_proj = lax.optimization_barrier((own_rows, near_proj))
+    far_rows, near_rows = z_far(own_rows), z_near(own_rows)
+    last_proj = z_near(far_proj)
+    x_near_proj, x_far_proj = x_peer(jnp.stack([near_proj, far_proj]))
+    x_last_proj = x_peer(last_proj)
+    last_rows = z_near(far_rows)
+    rows_here = (own_rows, near_rows, far_rows, last_rows)
+    rows_there = (
+        core_peer(own_rows),
+        *core_peer(jnp.stack([near_rows, far_rows])),
+        core_peer(last_rows),
+    )
+    early_proj = (own_proj, x_proj, near_proj, far_proj)
+    late_proj = (x_near_proj, x_far_proj, last_proj, x_last_proj)
+    early_there = core_peer(jnp.stack(early_proj))
+    late_there = core_peer(jnp.stack(late_proj))
 
     keep, send, grads = pl.pallas_call(
         functools.partial(group_kernel, factor),
         out_shape=(
-            jax.ShapeDtypeStruct((depth + 8, half), F32),
+            jax.ShapeDtypeStruct((depth + 16, half), F32),
             jax.ShapeDtypeStruct((depth + 16, half), BF16),
             jax.ShapeDtypeStruct((2, rows, width), BF16),
         ),
-        in_specs=[IN_SMEM] * 2 + [IN_VMEM] * 16,
+        in_specs=[IN_SMEM] * 2 + [IN_VMEM] * 24,
         out_specs=[IN_VMEM] * 3,
         scratch_shapes=[
             pltpu.VMEM((total_rows, width), F32),
@@ -333,37 +315,25 @@
     )(
         place,
         log_scale,
-        *our_rows,
-        *(their_rows[step] for step in range(4)),
-        *(our_proj[step] for step in range(4)),
-        *(their_proj[step] for step in range(4)),
-    )
+        *rows_here,
+        *rows_there,
+        *early_proj,
+        *late_proj,
+        *(early_there[at] for at in range(4)),
+        *(late_there[at] for at in range(4)),
+    )
+    folded = (keep + x_peer(send).astype(F32)).astype(BF16)
+    share = folded.astype(F32) + y_peer(folded).astype(F32)
     grads = regroup(grads)
-    folded = pl.pallas_call(
-        fold_x,
-        out_shape=jax.ShapeDtypeStruct(send.shape, BF16),
-        in_specs=[IN_VMEM] * 2,
-        out_specs=IN_VMEM,
-        name="fold_x",
-    )(keep, x_peer(send))
-    share, totals = pl.pallas_call(
-        fold_y,
-        out_shape=(
-            jax.ShapeDtypeStruct((depth, half), F32),
-            jax.ShapeDtypeStruct((8, 128), F32),
-        ),
-        in_specs=[IN_VMEM] * 2,
-        out_specs=[IN_VMEM] * 2,
-        name="fold_y",
-    )(folded, y_peer(folded))
-    grad_proj = pl.pallas_call(
-        joined_halves,
-        out_shape=jax.ShapeDtypeStruct((depth, width), F32),
-        in_specs=[IN_SMEM] + [IN_VMEM] * 2,
-        out_specs=IN_VMEM,
-        name="joined_halves",
-    )(place, share, core_peer(share))
-    return totals[0, 0:1], totals[0, 1:2], grads[0][None], grads[1][None], grad_proj
+    ours = share[:depth]
+    theirs = core_peer(ours)
+    grad_proj = jnp.where(
+        core == 0,
+        jnp.concatenate([ours, theirs], axis=1),
+        jnp.concatenate([theirs, ours], axis=1),
+    )
+    totals = jnp.sum(share[depth, :24].reshape(2, 12), axis=1)
+    return totals[0:1], totals[1:2], grads[0][None], grads[1][None], grad_proj
 
 
 def solution(mesh):

time: 61.7 us -> 52.2 us (0.85)
  waiting for transfers between devices: 26.9 us -> 18.1 us
  starting transfers between devices: 18.4 us -> 25.4 us
  Pallas kernels: 8.55 us -> 3.08 us
  local copies, waits for them, and re-layouts: 4.78 us -> 2.42 us
    ppermute x14 -> x19, waiting for transfers between devices: 26.9 us -> 18.1 us  [moved(): lax.ppermute(value, ('blk', 'rep'), [(number(*place), number(*to(*place))...]
    ppermute x14 -> x19, starting transfers between devices: 18.4 us -> 25.4 us  [moved(): lax.ppermute(value, ('blk', 'rep'), [(number(*place), number(*to(*place))...]
    pallas_call x3 -> x0, Pallas kernels: 5.47 us -> none  [the longest x1 1.91 us: on_device_whole_group(): pl.pallas_call(fold_x, out_shape=jax.ShapeDtypeStruct(send.shape, BF16),...]
    unnamed x12 -> x8, local copies, waits for them, and re-layouts: 2.66 us -> 0.92 us
    concatenate x1, other arithmetic: 0.93 us -> 0.01 us  [on_device_whole_group(): jnp.concatenate([image_embed[0], text_rest[0], text_hidden[0]], axis=1)]
    select_n x0 -> x1, other arithmetic: none -> 0.78 us  [on_device_whole_group(): jnp.where(core == 0, jnp.concatenate([ours, theirs], axis=1), jnp.concate...]
    slice x2 -> x4, local copies, waits for them, and re-layouts: 1.99 us -> 1.27 us  [the longest x2 1.24 us: on_device_whole_group(): return (totals[0:1], totals[1:2], grads[0][None], grads[1][None], grad_proj)]
  transfers between devices with their start and end apart: 14 -> 19, of which waited for: 8 -> 9; matrix products, arithmetic and copies ran while one was open for 4% -> 4% of each run, Pallas kernels for 3% -> 0%
where the time goes in v2:
time: 52.2 us; the launch traced here: 51.7 us
  starting transfers between devices  25.4 us (49%)
  waiting for transfers between devices  18.1 us (35%)
  Pallas kernels  3.08 us (6%)
  local copies, waits for them, and re-layouts  2.42 us (5%)
  between operations  1.49 us (3%)
  other arithmetic  1.23 us (2%)
    ppermute x19, starting transfers between devices, moved(): lax.ppermute(value, ('blk', 'rep'), [(number(*place), number(*to(*place))...  25.4 us
    ppermute x19, waiting for transfers between devices, moved(): lax.ppermute(value, ('blk', 'rep'), [(number(*place), number(*to(*place))...  18.1 us
    pallas_call x1, Pallas kernels, on_device_whole_group(): pl.pallas_call(functools.partial(group_kernel, factor), out_shape=(jax.Sh...  3.08 us
    slice x2, local copies, waits for them, and re-layouts, on_device_whole_group(): return (totals[0:1], totals[1:2], grads[0][None], grads[1][None], grad_proj)  1.24 us
  transfers between devices with their start and end apart: 19, of which 9 were waited for; matrix products, arithmetic and copies ran while one was open for 4% of the time, Pallas kernels for 0%

profile of v2, /device:TPU:1, one launch (start us, length us, event | category | flops | bytes accessed | tf_op | source)
XLA Modules:
  0.0 51.7 jit_solution(11094869602787481684)
XLA Ops:
  0.6 0.0 copy-start
  0.7 0.9 %copy-done = bf16[80,1280]{1,0:T(8,128)(2,1)S(1)} copy-done((bf16[80,1280]{1,0:T(8,128)(2,1)S(1)}, bf16[80,1280]{1,0:T(8,128)(2,1)}, u32[]{:S(2)}) %copy-start) | copy-done | bytes 204824
  1.6 0.0 copy-start.1
  1.6 0.0 copy-start.2
  1.6 0.0 copy-start.3
  1.6 3.2 %collective-permute-start.9 = (bf16[80,640]{1,0:T(8,128)(2,1)S(1)}, bf16[80,640]{1,0:T(8,128)(2,1)S(1)}, u32[]{:S(2)}, u32[]{:S(2)}) collective-permute-start(bf16[80,640]{1,0:T(8,128)(2,1)S(1)} %constant_dynamic-slice_fusion.refs_8_), channel_id=1, source_target_pairs={{0,16},{1,17},{2,18},{3,19},{4,20},{5,21},{6,22},{7,23},{8,24},{9,... | collective-permute-start | bytes 307208 | tf_op jit(solution)/shard_map/ppermute | solution.py:129
  4.8 1.2 %collective-permute-start.8 = (bf16[80,640]{1,0:T(8,128)(2,1)S(1)}, bf16[80,640]{1,0:T(8,128)(2,1)S(1)}, u32[]{:S(2)}, u32[]{:S(2)}) collective-permute-start(bf16[80,640]{1,0:T(8,128)(2,1)S(1)} %constant_dynamic-slice_fusion.refs_8_), channel_id=1, source_target_pairs={{0,4},{1,5},{2,6},{3,7},{4,0},{5,1},{6,2},{7,3},{8,12},{9,13},{10,... | collective-permute-start | bytes 307208 | tf_op jit(solution)/shard_map/ppermute | solution.py:129
  6.0 1.3 %collective-permute-start.1 = (bf16[80,640]{1,0:T(8,128)(2,1)S(1)}, bf16[80,640]{1,0:T(8,128)(2,1)S(1)}, u32[]{:S(2)}, u32[]{:S(2)}) collective-permute-start(bf16[80,640]{1,0:T(8,128)(2,1)S(1)} %constant_dynamic-slice_fusion.refs_8_), channel_id=1, source_target_pairs={{0,8},{1,9},{2,10},{3,11},{4,12},{5,13},{6,14},{7,15},{8,0},{9,1},... | collective-permute-start | bytes 307208 | tf_op jit(solution)/shard_map/ppermute | solution.py:129
  7.3 0.0 copy-done.1
  7.3 0.0 copy-done.2
  7.3 0.0 copy-done.3
  7.3 3.6 %collective-permute-start = (bf16[24,3200]{1,0:T(8,128)(2,1)S(1)}, bf16[24,3200]{1,0:T(8,128)(2,1)S(1)}, u32[]{:S(2)}, u32[]{:S(2)}) collective-permute-start(bf16[24,3200]{1,0:T(8,128)(2,1)S(1)} %pad_maximum_fusion.4), channel_id=1, source_target_pairs={{0,0},{1,4},{2,2},{3,6},{4,1},{5,5},{6,3},{7,7},{8,8},{9,12},{10,1... | collective-permute-start | bytes 460808 | tf_op jit(solution)/shard_map/ppermute | solution.py:129
  11.6 0.1 pad_add_fusion.place
  11.7 0.0 collective-permute-done.9.refs_11_
  11.7 0.2 collective-permute-start.11
  11.9 0.0 collective-permute-done.1.refs_10_
  11.9 2.3 %collective-permute-done.refs_0_ = bf16[24,3200]{1,0:T(8,128)(2,1)S(1)} collective-permute-done((bf16[24,3200]{1,0:T(8,128)(2,1)S(1)}, bf16[24,3200]{1,0:T(8,128)(2,1)S(1)}, u32[]{:S(2)}, u32[]{:S(2)}) %collective-permute-start) | collective-permute-done | bytes 153632 | tf_op jit(solution)/shard_map/ppermute | solution.py:129
  14.1 0.0 collective-permute-start.5
  14.2 0.6 %collective-permute-start.3 = (bf16[24,3200]{1,0:T(8,128)(2,1)S(1)}, bf16[24,3200]{1,0:T(8,128)(2,1)S(1)}, u32[]{:S(2)}, u32[]{:S(2)}) collective-permute-start(bf16[24,3200]{1,0:T(8,128)(2,1)S(1)} %collective-permute-done.refs_0_), channel_id=1, source_target_pairs={{0,16},{1,17},{2,18},{3,19},{4,20},{5,21},{6,22},{7,23},{8,24},{9,... | collective-permute-start | bytes 460808 | tf_op jit(solution)/shard_map/ppermute | solution.py:129
  14.8 0.6 %collective-permute-start.2 = (bf16[24,3200]{1,0:T(8,128)(2,1)S(1)}, bf16[24,3200]{1,0:T(8,128)(2,1)S(1)}, u32[]{:S(2)}, u32[]{:S(2)}) collective-permute-start(bf16[24,3200]{1,0:T(8,128)(2,1)S(1)} %collective-permute-done.refs_0_), channel_id=1, source_target_pairs={{0,8},{1,9},{2,10},{3,11},{4,12},{5,13},{6,14},{7,15},{8,0},{9,1},... | collective-permute-start | bytes 460808 | tf_op jit(solution)/shard_map/ppermute | solution.py:129
  15.4 0.0 collective-permute-done.8.refs_9_
  15.4 0.6 %collective-permute-start.10 = (bf16[2,80,640]{2,1,0:T(8,128)(2,1)S(1)}, bf16[2,80,640]{2,1,0:T(8,128)(2,1)S(1)}, u32[]{:S(2)}, u32[]{:S(2)}) collective-permute-start(bf16[2,80,640]{2,1,0:T(8,128)(2,1)S(1)} %pad_maximum_fusion.3), channel_id=1, source_target_pairs={{0,4},{1,5},{2,6},{3,7},{4,0},{5,1},{6,2},{7,3},{8,12},{9,13},{10,... | collective-permute-start | bytes 614408 | tf_op jit(solution)/shard_map/ppermute | solution.py:129
  16.0 0.1 pad_maximum_fusion
  16.1 0.0 collective-permute-done.11.refs_14_
  16.1 0.8 %collective-permute-start.13 = (bf16[4,80,640]{2,1,0:T(8,128)(2,1)S(1)}, bf16[4,80,640]{2,1,0:T(8,128)(2,1)S(1)}, u32[]{:S(2)}, u32[]{:S(2)}) collective-permute-start(bf16[4,80,640]{2,1,0:T(8,128)(2,1)S(1)} %pad_maximum_fusion), channel_id=1, source_target_pairs={{0,1},{1,0},{2,3},{3,2},{4,5},{5,4},{6,7},{7,6},{8,9},{9,8},{10,11... | collective-permute-start | bytes 1228808 | tf_op jit(solution)/shard_map/ppermute | solution.py:129
  16.8 7.0 %collective-permute-done.3.refs_2_ = bf16[24,3200]{1,0:T(8,128)(2,1)S(1)} collective-permute-done((bf16[24,3200]{1,0:T(8,128)(2,1)S(1)}, bf16[24,3200]{1,0:T(8,128)(2,1)S(1)}, u32[]{:S(2)}, u32[]{:S(2)}) %collective-permute-start.3) | collective-permute-done | bytes 153632 | tf_op jit(solution)/shard_map/ppermute | solution.py:129
  23.9 1.8 %collective-permute-start.12 = (bf16[80,640]{1,0:T(8,128)(2,1)S(1)}, bf16[80,640]{1,0:T(8,128)(2,1)S(1)}, u32[]{:S(2)}, u32[]{:S(2)}) collective-permute-start(bf16[80,640]{1,0:T(8,128)(2,1)S(1)} %collective-permute-done.11.refs_14_), channel_id=1, source_target_pairs={{0,4},{1,5},{2,6},{3,7},{4,0},{5,1},{6,2},{7,3},{8,12},{9,13},{10,... | collective-permute-start | bytes 307208 | tf_op jit(solution)/shard_map/ppermute | solution.py:129
  25.7 0.0 collective-permute-done.2.refs_1_
  25.7 0.8 %collective-permute-start.6 = (bf16[2,24,3200]{2,1,0:T(8,128)(2,1)S(1)}, bf16[2,24,3200]{2,1,0:T(8,128)(2,1)S(1)}, u32[]{:S(2)}, u32[]{:S(2)}) collective-permute-start(bf16[2,24,3200]{2,1,0:T(8,128)(2,1)S(1)} %pad_maximum_fusion.2), channel_id=1, source_target_pairs={{0,1},{1,0},{2,3},{3,2},{4,5},{5,4},{6,7},{7,6},{8,9},{9,8},{10,11... | collective-permute-start | bytes 921608 | tf_op jit(solution)/shard_map/ppermute | solution.py:129
  26.5 2.0 %collective-permute-done.12.refs_15_ = bf16[80,640]{1,0:T(8,128)(2,1)S(1)} collective-permute-done((bf16[80,640]{1,0:T(8,128)(2,1)S(1)}, bf16[80,640]{1,0:T(8,128)(2,1)S(1)}, u32[]{:S(2)}, u32[]{:S(2)}) %collective-permute-start.12) | collective-permute-done | bytes 102432 | tf_op jit(solution)/shard_map/ppermute | solution.py:129
  28.4 0.0 collective-permute-start.4
  28.4 0.0 collective-permute-done.10
  28.4 0.1 pad_maximum_fusion.1
  28.5 1.1 %collective-permute-start.14 = (bf16[4,80,640]{2,1,0:T(8,128)(2,1)S(1)}, bf16[4,80,640]{2,1,0:T(8,128)(2,1)S(1)}, u32[]{:S(2)}, u32[]{:S(2)}) collective-permute-start(bf16[4,80,640]{2,1,0:T(8,128)(2,1)S(1)} %pad_maximum_fusion.1), channel_id=1, source_target_pairs={{0,1},{1,0},{2,3},{3,2},{4,5},{5,4},{6,7},{7,6},{8,9},{9,8},{10,11... | collective-permute-start | bytes 1228808 | tf_op jit(solution)/shard_map/ppermute | solution.py:129
  29.7 3.2 %collective-permute-done.4.refs_3_ = bf16[24,3200]{1,0:T(8,128)(2,1)S(1)} collective-permute-done((bf16[24,3200]{1,0:T(8,128)(2,1)S(1)}, bf16[24,3200]{1,0:T(8,128)(2,1)S(1)}, u32[]{:S(2)}, u32[]{:S(2)}) %collective-permute-start.4) | collective-permute-done | bytes 153632 | tf_op jit(solution)/shard_map/ppermute | solution.py:129
  32.9 2.0 %collective-permute-start.7 = (bf16[24,3200]{1,0:T(8,128)(2,1)S(1)}, bf16[24,3200]{1,0:T(8,128)(2,1)S(1)}, u32[]{:S(2)}, u32[]{:S(2)}) collective-permute-start(bf16[24,3200]{1,0:T(8,128)(2,1)S(1)} %collective-permute-done.4.refs_3_), channel_id=1, source_target_pairs={{0,1},{1,0},{2,3},{3,2},{4,5},{5,4},{6,7},{7,6},{8,9},{9,8},{10,11... | collective-permute-start | bytes 460808 | tf_op jit(solution)/shard_map/ppermute | solution.py:129
  34.8 0.0 collective-permute-done.13
  34.9 0.0 collective-permute-done.6
  34.9 0.0 collective-permute-done.14
  35.0 0.0 collective-permute-done.5.refs_4_
  35.0 0.9 %collective-permute-done.7.refs_7_ = bf16[24,3200]{1,0:T(8,128)(2,1)S(1)} collective-permute-done((bf16[24,3200]{1,0:T(8,128)(2,1)S(1)}, bf16[24,3200]{1,0:T(8,128)(2,1)S(1)}, u32[]{:S(2)}, u32[]{:S(2)}) %collective-permute-start.7) | collective-permute-done | bytes 153632 | tf_op jit(solution)/shard_map/ppermute | solution.py:129
  35.9 3.1 %group_kernel.1 = (f32[96,640]{1,0:T(8,128)S(1)}, bf16[96,640]{1,0:T(8,128)(2,1)S(1)}, bf16[2,24,1280]{2,1,0:T(8,128)(2,1)S(1)}) custom-call(s32[4]{0:T(128)S(1)} %pad_add_fusion.place, f32[1]{0:T(128)S(6)} %copy.10.log_scale, bf16[24,3200]{1,0:T(8,128)(2,1)S(1)} %collective-permute-done.refs_0_, bf16[24,3200]{1,0:T(8,128)(2,1)S(1)} %collective-permute-done.2.refs_1_, ...), custom_call_target="tpu_custom_call" | custom-call | tf_op jit(solution)/shard_map/group_kernel/pallas_call | solution.py:292
  38.9 1.4 %collective-permute-start.15 = (bf16[96,640]{1,0:T(8,128)(2,1)S(1)}, bf16[96,640]{1,0:T(8,128)(2,1)S(1)}, u32[]{:S(2)}, u32[]{:S(2)}) collective-permute-start(bf16[96,640]{1,0:T(8,128)(2,1)S(1)} %get-tuple-element.13), channel_id=1, source_target_pairs={{0,4},{1,5},{2,6},{3,7},{4,0},{5,1},{6,2},{7,3},{8,12},{9,13},{10,... | collective-permute-start | bytes 368648 | tf_op jit(solution)/shard_map/ppermute | solution.py:129
  40.3 2.6 %collective-permute-start.17 = (bf16[2,24,1280]{2,1,0:T(8,128)(2,1)S(1)}, bf16[2,24,1280]{2,1,0:T(8,128)(2,1)S(1)}, u32[]{:S(2)}, u32[]{:S(2)}) collective-permute-start(bf16[2,24,1280]{2,1,0:T(8,128)(2,1)S(1)} %get-tuple-element.14), channel_id=1, source_target_pairs={{0,0},{1,4},{2,2},{3,6},{4,1},{5,5},{6,3},{7,7},{8,8},{9,12},{10,1... | collective-permute-start | bytes 368648 | tf_op jit(solution)/shard_map/ppermute | solution.py:129
  42.9 0.7 %collective-permute-done.15 = bf16[96,640]{1,0:T(8,128)(2,1)S(1)} collective-permute-done((bf16[96,640]{1,0:T(8,128)(2,1)S(1)}, bf16[96,640]{1,0:T(8,128)(2,1)S(1)}, u32[]{:S(2)}, u32[]{:S(2)}) %collective-permute-start.15) | collective-permute-done | bytes 122912 | tf_op jit(solution)/shard_map/ppermute | solution.py:129
  43.6 1.3 %collective-permute-start.16 = (bf16[96,640]{1,0:T(8,128)(2,1)S(1)}, bf16[96,640]{1,0:T(8,128)(2,1)S(1)}, u32[]{:S(2)}, u32[]{:S(2)}) collective-permute-start(bf16[96,640]{1,0:T(8,128)(2,1)S(1)} %add_convert_fusion), channel_id=1, source_target_pairs={{0,2},{1,3},{2,0},{3,1},{4,6},{5,7},{6,4},{7,5},{8,10},{9,11},{10,... | collective-permute-start | bytes 368648 | tf_op jit(solution)/shard_map/ppermute | solution.py:129
  44.9 1.6 %collective-permute-done.17 = bf16[2,24,1280]{2,1,0:T(8,128)(2,1)S(1)} collective-permute-done((bf16[2,24,1280]{2,1,0:T(8,128)(2,1)S(1)}, bf16[2,24,1280]{2,1,0:T(8,128)(2,1)S(1)}, u32[]{:S(2)}, u32[]{:S(2)}) %collective-permute-start.17) | collective-permute-done | bytes 122912 | tf_op jit(solution)/shard_map/ppermute | solution.py:129
  46.5 0.7 %fusion = (bf16[1,24,1280]{2,1,0:T(8,128)(2,1)}, bf16[1,24,1280]{2,1,0:T(8,128)(2,1)}) fusion(bf16[2,24,1280]{2,1,0:T(8,128)(2,1)S(1)} %collective-permute-done.17), kind=kLoop, calls=%fused_computation.23 | loop fusion | bytes 245760 | tf_op jit(solution)/shard_map/slice | solution.py:336
  47.2 0.2 collective-permute-done.16
  47.4 2.4 %collective-permute-start.18 = (f32[80,640]{1,0:T(8,128)S(1)}, f32[80,640]{1,0:T(8,128)S(1)}, u32[]{:S(2)}, u32[]{:S(2)}) collective-permute-start(f32[80,640]{1,0:T(8,128)S(1)} %slice.68), channel_id=1, source_target_pairs={{0,1},{1,0},{2,3},{3,2},{4,5},{5,4},{6,7},{7,6},{8,9},{9,8},{10,11... | collective-permute-start | bytes 614408 | tf_op jit(solution)/shard_map/ppermute | solution.py:129
  49.9 0.1 reshape_squeeze.3
  49.9 0.1 reduce_sum.9
  50.1 0.6 %fusion.1 = (f32[1]{0:T(128)}, f32[1]{0:T(128)}) fusion(f32[2]{0:T(128)S(1)} %reduce_sum.9), kind=kLoop, calls=%fused_computation.24 | loop fusion | bytes 16 | tf_op jit(solution)/shard_map/slice | solution.py:336
  50.7 0.3 collective-permute-done.18
  50.9 0.8 %maximum_select_fusion = f32[80,1280]{1,0:T(8,128)} fusion(f32[80,640]{1,0:T(8,128)S(1)} %collective-permute-done.18, f32[80,640]{1,0:T(8,128)S(1)} %slice.68, pred[]{:T(512)S(6)} %eq.6), kind=kLoop, calls=%fused_computation.2 | loop fusion | flops 307200 | bytes 819201 | tf_op jit(solution)/shard_map/jit(_where)/select_n | solution.py:330
  (13 shorter events, 0.3 us)
Async XLA Ops:
  0.6 0.9 %copy-start = (bf16[80,1280]{1,0:T(8,128)(2,1)S(1)}, bf16[80,1280]{1,0:T(8,128)(2,1)}, u32[]{:S(2)}) copy-start(bf16[80,1280]{1,0:T(8,128)(2,1)} %param.8) | copy-start | bytes 614404
  1.6 5.7 %copy-start.1 = (bf16[1,24,1280]{2,1,0:T(8,128)(2,1)S(1)}, bf16[1,24,1280]{2,1,0:T(8,128)(2,1)}, u32[]{:S(2)}) copy-start(bf16[1,24,1280]{2,1,0:T(8,128)(2,1)} %param.7) | copy-start | bytes 184324
  1.6 5.7 %copy-start.2 = (bf16[1,24,1280]{2,1,0:T(8,128)(2,1)S(1)}, bf16[1,24,1280]{2,1,0:T(8,128)(2,1)}, u32[]{:S(2)}) copy-start(bf16[1,24,1280]{2,1,0:T(8,128)(2,1)} %param.5) | copy-start | bytes 184324
  1.6 5.7 %copy-start.3 = (bf16[1,24,640]{2,1,0:T(8,128)(2,1)S(1)}, bf16[1,24,640]{2,1,0:T(8,128)(2,1)}, u32[]{:S(2)}) copy-start(bf16[1,24,640]{2,1,0:T(8,128)(2,1)} %param.6) | copy-start | bytes 92164
  1.6 10.1 %collective-permute-start.9 = (bf16[80,640]{1,0:T(8,128)(2,1)S(1)}, bf16[80,640]{1,0:T(8,128)(2,1)S(1)}, u32[]{:S(2)}, u32[]{:S(2)}) collective-permute-start(bf16[80,640]{1,0:T(8,128)(2,1)S(1)} %constant_dynamic-slice_fusion.refs_8_), channel_id=1, source_target_pairs={{0,16},{1,17},{2,18},{3,19},{4,20},{5,21},{6,22},{7,23},{8,24},{9,... | collective-permute-start | bytes 307208 | tf_op jit(solution)/shard_map/ppermute | solution.py:129
  4.8 10.6 %collective-permute-start.8 = (bf16[80,640]{1,0:T(8,128)(2,1)S(1)}, bf16[80,640]{1,0:T(8,128)(2,1)S(1)}, u32[]{:S(2)}, u32[]{:S(2)}) collective-permute-start(bf16[80,640]{1,0:T(8,128)(2,1)S(1)} %constant_dynamic-slice_fusion.refs_8_), channel_id=1, source_target_pairs={{0,4},{1,5},{2,6},{3,7},{4,0},{5,1},{6,2},{7,3},{8,12},{9,13},{10,... | collective-permute-start | bytes 307208 | tf_op jit(solution)/shard_map/ppermute | solution.py:129
  6.0 5.9 %collective-permute-start.1 = (bf16[80,640]{1,0:T(8,128)(2,1)S(1)}, bf16[80,640]{1,0:T(8,128)(2,1)S(1)}, u32[]{:S(2)}, u32[]{:S(2)}) collective-permute-start(bf16[80,640]{1,0:T(8,128)(2,1)S(1)} %constant_dynamic-slice_fusion.refs_8_), channel_id=1, source_target_pairs={{0,8},{1,9},{2,10},{3,11},{4,12},{5,13},{6,14},{7,15},{8,0},{9,1},... | collective-permute-start | bytes 307208 | tf_op jit(solution)/shard_map/ppermute | solution.py:129
  7.3 6.8 %collective-permute-start = (bf16[24,3200]{1,0:T(8,128)(2,1)S(1)}, bf16[24,3200]{1,0:T(8,128)(2,1)S(1)}, u32[]{:S(2)}, u32[]{:S(2)}) collective-permute-start(bf16[24,3200]{1,0:T(8,128)(2,1)S(1)} %pad_maximum_fusion.4), channel_id=1, source_target_pairs={{0,0},{1,4},{2,2},{3,6},{4,1},{5,5},{6,3},{7,7},{8,8},{9,12},{10,1... | collective-permute-start | bytes 460808 | tf_op jit(solution)/shard_map/ppermute | solution.py:129
  11.7 4.4 %collective-permute-start.11 = (bf16[80,640]{1,0:T(8,128)(2,1)S(1)}, bf16[80,640]{1,0:T(8,128)(2,1)S(1)}, u32[]{:S(2)}, u32[]{:S(2)}) collective-permute-start(bf16[80,640]{1,0:T(8,128)(2,1)S(1)} %collective-permute-done.9.refs_11_), channel_id=1, source_target_pairs={{0,8},{1,9},{2,10},{3,11},{4,12},{5,13},{6,14},{7,15},{8,0},{9,1},... | collective-permute-start | bytes 307208 | tf_op jit(solution)/shard_map/ppermute | solution.py:129
  14.1 20.8 %collective-permute-start.5 = (bf16[24,3200]{1,0:T(8,128)(2,1)S(1)}, bf16[24,3200]{1,0:T(8,128)(2,1)S(1)}, u32[]{:S(2)}, u32[]{:S(2)}) collective-permute-start(bf16[24,3200]{1,0:T(8,128)(2,1)S(1)} %collective-permute-done.refs_0_), channel_id=1, source_target_pairs={{0,1},{1,0},{2,3},{3,2},{4,5},{5,4},{6,7},{7,6},{8,9},{9,8},{10,11... | collective-permute-start | bytes 460808 | tf_op jit(solution)/shard_map/ppermute | solution.py:129
  14.2 9.7 %collective-permute-start.3 = (bf16[24,3200]{1,0:T(8,128)(2,1)S(1)}, bf16[24,3200]{1,0:T(8,128)(2,1)S(1)}, u32[]{:S(2)}, u32[]{:S(2)}) collective-permute-start(bf16[24,3200]{1,0:T(8,128)(2,1)S(1)} %collective-permute-done.refs_0_), channel_id=1, source_target_pairs={{0,16},{1,17},{2,18},{3,19},{4,20},{5,21},{6,22},{7,23},{8,24},{9,... | collective-permute-start | bytes 460808 | tf_op jit(solution)/shard_map/ppermute | solution.py:129
  14.8 10.9 %collective-permute-start.2 = (bf16[24,3200]{1,0:T(8,128)(2,1)S(1)}, bf16[24,3200]{1,0:T(8,128)(2,1)S(1)}, u32[]{:S(2)}, u32[]{:S(2)}) collective-permute-start(bf16[24,3200]{1,0:T(8,128)(2,1)S(1)} %collective-permute-done.refs_0_), channel_id=1, source_target_pairs={{0,8},{1,9},{2,10},{3,11},{4,12},{5,13},{6,14},{7,15},{8,0},{9,1},... | collective-permute-start | bytes 460808 | tf_op jit(solution)/shard_map/ppermute | solution.py:129
  15.4 13.1 %collective-permute-start.10 = (bf16[2,80,640]{2,1,0:T(8,128)(2,1)S(1)}, bf16[2,80,640]{2,1,0:T(8,128)(2,1)S(1)}, u32[]{:S(2)}, u32[]{:S(2)}) collective-permute-start(bf16[2,80,640]{2,1,0:T(8,128)(2,1)S(1)} %pad_maximum_fusion.3), channel_id=1, source_target_pairs={{0,4},{1,5},{2,6},{3,7},{4,0},{5,1},{6,2},{7,3},{8,12},{9,13},{10,... | collective-permute-start | bytes 614408 | tf_op jit(solution)/shard_map/ppermute | solution.py:129
  16.1 18.8 %collective-permute-start.13 = (bf16[4,80,640]{2,1,0:T(8,128)(2,1)S(1)}, bf16[4,80,640]{2,1,0:T(8,128)(2,1)S(1)}, u32[]{:S(2)}, u32[]{:S(2)}) collective-permute-start(bf16[4,80,640]{2,1,0:T(8,128)(2,1)S(1)} %pad_maximum_fusion), channel_id=1, source_target_pairs={{0,1},{1,0},{2,3},{3,2},{4,5},{5,4},{6,7},{7,6},{8,9},{9,8},{10,11... | collective-permute-start | bytes 1228808 | tf_op jit(solution)/shard_map/ppermute | solution.py:129
  23.9 4.6 %collective-permute-start.12 = (bf16[80,640]{1,0:T(8,128)(2,1)S(1)}, bf16[80,640]{1,0:T(8,128)(2,1)S(1)}, u32[]{:S(2)}, u32[]{:S(2)}) collective-permute-start(bf16[80,640]{1,0:T(8,128)(2,1)S(1)} %collective-permute-done.11.refs_14_), channel_id=1, source_target_pairs={{0,4},{1,5},{2,6},{3,7},{4,0},{5,1},{6,2},{7,3},{8,12},{9,13},{10,... | collective-permute-start | bytes 307208 | tf_op jit(solution)/shard_map/ppermute | solution.py:129
  25.7 9.2 %collective-permute-start.6 = (bf16[2,24,3200]{2,1,0:T(8,128)(2,1)S(1)}, bf16[2,24,3200]{2,1,0:T(8,128)(2,1)S(1)}, u32[]{:S(2)}, u32[]{:S(2)}) collective-permute-start(bf16[2,24,3200]{2,1,0:T(8,128)(2,1)S(1)} %pad_maximum_fusion.2), channel_id=1, source_target_pairs={{0,1},{1,0},{2,3},{3,2},{4,5},{5,4},{6,7},{7,6},{8,9},{9,8},{10,11... | collective-permute-start | bytes 921608 | tf_op jit(solution)/shard_map/ppermute | solution.py:129
  28.4 4.4 %collective-permute-start.4 = (bf16[24,3200]{1,0:T(8,128)(2,1)S(1)}, bf16[24,3200]{1,0:T(8,128)(2,1)S(1)}, u32[]{:S(2)}, u32[]{:S(2)}) collective-permute-start(bf16[24,3200]{1,0:T(8,128)(2,1)S(1)} %collective-permute-done.3.refs_2_), channel_id=1, source_target_pairs={{0,8},{1,9},{2,10},{3,11},{4,12},{5,13},{6,14},{7,15},{8,0},{9,1},... | collective-permute-start | bytes 460808 | tf_op jit(solution)/shard_map/ppermute | solution.py:129
  28.5 6.4 %collective-permute-start.14 = (bf16[4,80,640]{2,1,0:T(8,128)(2,1)S(1)}, bf16[4,80,640]{2,1,0:T(8,128)(2,1)S(1)}, u32[]{:S(2)}, u32[]{:S(2)}) collective-permute-start(bf16[4,80,640]{2,1,0:T(8,128)(2,1)S(1)} %pad_maximum_fusion.1), channel_id=1, source_target_pairs={{0,1},{1,0},{2,3},{3,2},{4,5},{5,4},{6,7},{7,6},{8,9},{9,8},{10,11... | collective-permute-start | bytes 1228808 | tf_op jit(solution)/shard_map/ppermute | solution.py:129
  32.9 3.0 %collective-permute-start.7 = (bf16[24,3200]{1,0:T(8,128)(2,1)S(1)}, bf16[24,3200]{1,0:T(8,128)(2,1)S(1)}, u32[]{:S(2)}, u32[]{:S(2)}) collective-permute-start(bf16[24,3200]{1,0:T(8,128)(2,1)S(1)} %collective-permute-done.4.refs_3_), channel_id=1, source_target_pairs={{0,1},{1,0},{2,3},{3,2},{4,5},{5,4},{6,7},{7,6},{8,9},{9,8},{10,11... | collective-permute-start | bytes 460808 | tf_op jit(solution)/shard_map/ppermute | solution.py:129
  38.9 4.6 %collective-permute-start.15 = (bf16[96,640]{1,0:T(8,128)(2,1)S(1)}, bf16[96,640]{1,0:T(8,128)(2,1)S(1)}, u32[]{:S(2)}, u32[]{:S(2)}) collective-permute-start(bf16[96,640]{1,0:T(8,128)(2,1)S(1)} %get-tuple-element.13), channel_id=1, source_target_pairs={{0,4},{1,5},{2,6},{3,7},{4,0},{5,1},{6,2},{7,3},{8,12},{9,13},{10,... | collective-permute-start | bytes 368648 | tf_op jit(solution)/shard_map/ppermute | solution.py:129
  40.3 6.2 %collective-permute-start.17 = (bf16[2,24,1280]{2,1,0:T(8,128)(2,1)S(1)}, bf16[2,24,1280]{2,1,0:T(8,128)(2,1)S(1)}, u32[]{:S(2)}, u32[]{:S(2)}) collective-permute-start(bf16[2,24,1280]{2,1,0:T(8,128)(2,1)S(1)} %get-tuple-element.14), channel_id=1, source_target_pairs={{0,0},{1,4},{2,2},{3,6},{4,1},{5,5},{6,3},{7,7},{8,8},{9,12},{10,1... | collective-permute-start | bytes 368648 | tf_op jit(solution)/shard_map/ppermute | solution.py:129
  43.6 3.8 %collective-permute-start.16 = (bf16[96,640]{1,0:T(8,128)(2,1)S(1)}, bf16[96,640]{1,0:T(8,128)(2,1)S(1)}, u32[]{:S(2)}, u32[]{:S(2)}) collective-permute-start(bf16[96,640]{1,0:T(8,128)(2,1)S(1)} %add_convert_fusion), channel_id=1, source_target_pairs={{0,2},{1,3},{2,0},{3,1},{4,6},{5,7},{6,4},{7,5},{8,10},{9,11},{10,... | collective-permute-start | bytes 368648 | tf_op jit(solution)/shard_map/ppermute | solution.py:129
  47.4 3.5 %collective-permute-start.18 = (f32[80,640]{1,0:T(8,128)S(1)}, f32[80,640]{1,0:T(8,128)S(1)}, u32[]{:S(2)}, u32[]{:S(2)}) collective-permute-start(f32[80,640]{1,0:T(8,128)S(1)} %slice.68), channel_id=1, source_target_pairs={{0,1},{1,0},{2,3},{3,2},{4,5},{5,4},{6,7},{7,6},{8,9},{9,8},{10,11... | collective-permute-start | bytes 614408 | tf_op jit(solution)/shard_map/ppermute | solution.py:129

commit v3 on v2

--- a/solution.py
+++ b/solution.py
@@ -117,8 +117,8 @@
 ROWWISE = (((1,), (1,)), ((), ()))
 IN_VMEM = pl.BlockSpec(memory_space=pltpu.VMEM)
 IN_SMEM = pl.BlockSpec(memory_space=pltpu.SMEM)
-PROJ_ORDER = ((0, 0), (0, 1), (1, 0), (2, 0), (1, 1), (2, 1), (3, 0), (3, 1))
-
+ROW_STEPS = ((0, 1, 3, 2), (0, 2, 1, 3))
+PROJ_STEPS = (((0, 2), 0), ((1, 3), 0), ((0, 2), 1), ((1, 3), 1))
 
 def number(z, x, y, core):
     return (z * 2 + x) * 4 + y * 2 + core
@@ -147,12 +147,36 @@
     return moved(value, lambda z, x, y, core: (z, x, 1 - y, core))
 
 
+def xy_peer(value):
+    return moved(value, lambda z, x, y, core: (z, 1 - x, 1 - y, core))
+
+
 def core_peer(value):
     return moved(value, lambda z, x, y, core: (z, x, y, 1 - core))
 
 
-def regroup(value):
-    return moved(value, lambda z, x, y, core: (z, core, y, x))
+def is_ahead(x, core):
+    return x == core
+
+
+def trade(z, x, y, core):
+    return z, core, y, x
+
+
+def first_move(value):
+    return moved(value, lambda z, x, y, core: (z ^ 2, x, y, core) if is_ahead(x, core) else trade(z, x, y, core))
+
+
+def second_move(value):
+    return moved(value, lambda z, x, y, core: (z ^ 1 if is_ahead(x, core) else z ^ 2, x, y, core))
+
+
+def fourth_move(value):
+    return moved(value, lambda z, x, y, core: (z, x, 1 - y, core) if is_ahead(x, core) else (z ^ 1, x, y, core))
+
+
+def trade_back(value):
+    return moved(value, lambda z, x, y, core: (z ^ 1, x, y, core) if is_ahead(x, core) else trade(z, x, y, core))
 
 
 def in_parts(value):
@@ -175,24 +199,26 @@
 
 
 def group_kernel(factor, place, log_scale, *refs):
-    rows_here, rows_there, projs = refs[:4], refs[4:8], refs[8:24]
-    keep, send, grads = refs[24:27]
-    image, text, hidden, hidden_t, norms, proj, coefs, grad_all, grad_cols, share = refs[27:]
+    rows_here, rows_there, projs = refs[:4], refs[4:8], refs[8:16]
+    keep, send, grads = refs[16:19]
+    image, text, hidden, hidden_t, norms, proj, coefs, grad_all, grad_cols, share = refs[19:]
     z, x, y, core = (place[at] for at in range(4))
-    rows, depth = rows_here[0].shape[0], projs[0].shape[0]
+    rows, depth = rows_here[0].shape[0], projs[0].shape[1]
     width = image.shape[1]
     half = width // 2
-    for side, groups in enumerate((rows_here, rows_there)):
-        for step in range(4):
+    ahead = is_ahead(x, core)
+    for side, blocks in enumerate((rows_here, rows_there)):
+        for block, *steps in zip(blocks, *ROW_STEPS):
+            step = jnp.where(ahead, steps[side], steps[1 - side])
             start = pl.multiple_of(((z ^ step) * 2 + (core ^ side)) * rows, 8)
-            block = groups[step]
             image[pl.ds(start, rows), :] = block[:, :width].astype(F32)
             text[pl.ds(start, rows), :] = block[:, width : 2 * width].astype(F32)
             hidden[pl.ds(start, rows), :] = block[:, 2 * width :].astype(F32)
-    for side in range(2):
-        for at, (step, column) in enumerate(PROJ_ORDER):
+    for at, blocks in enumerate(projs):
+        steps, column = PROJ_STEPS[at % 4]
+        for block, step in enumerate(steps):
             start = pl.multiple_of(((z ^ step) * 2 + (x ^ column)) * depth, 16)
-            proj[core ^ side, pl.ds(start, depth), :] = projs[side * 8 + at][...]
+            proj[core ^ (at // 4), pl.ds(start, depth), :] = blocks[block]
     hidden_short = hidden[...].astype(BF16)
     for side in range(2):
         text[:, side * half : (side + 1) * half] += jnp.dot(
@@ -249,8 +275,8 @@
         preferred_element_type=F32,
     )
     totals = lanes_of(in_parts(loss) + in_parts(scale_grad), 2 * y + x, (16, half))
-    keep[:depth, :] = share[pl.ds(pl.multiple_of(x * depth, 8), depth), :]
-    keep[depth:, :] = totals
+    keep[:depth, :] = share[pl.ds(pl.multiple_of(x * depth, 8), depth), :].astype(BF16)
+    keep[depth:, :] = totals.astype(BF16)
     send[:depth, :] = share[pl.ds(pl.multiple_of((1 - x) * depth, 8), depth), :].astype(BF16)
     send[depth:, :] = totals.astype(BF16)
 
@@ -268,35 +294,42 @@
         far = z_far(value)
         return value, z_near(value), far, z_near(far)
 
+    ahead = is_ahead(x, core)
     own_proj = lax.dynamic_slice_in_dim(proj_window, core * half, half, 1)
-    far_proj, near_proj, x_proj = z_far(own_proj), z_near(own_proj), x_peer(own_proj)
     samples = jnp.concatenate([image_embed[0], text_rest[0], text_hidden[0]], axis=1)
-    own_rows = regroup(samples)
-    own_rows, near_proj = lax.optimization_barrier((own_rows, near_proj))
-    far_rows, near_rows = z_far(own_rows), z_near(own_rows)
-    last_proj = z_near(far_proj)
-    x_near_proj, x_far_proj = x_peer(jnp.stack([near_proj, far_proj]))
-    x_last_proj = x_peer(last_proj)
-    last_rows = z_near(far_rows)
-    rows_here = (own_rows, near_rows, far_rows, last_rows)
-    rows_there = (
-        core_peer(own_rows),
-        *core_peer(jnp.stack([near_rows, far_rows])),
-        core_peer(last_rows),
-    )
-    early_proj = (own_proj, x_proj, near_proj, far_proj)
-    late_proj = (x_near_proj, x_far_proj, last_proj, x_last_proj)
-    early_there = core_peer(jnp.stack(early_proj))
-    late_there = core_peer(jnp.stack(late_proj))
+    far_proj = z_far(own_proj)
+    even = jnp.stack([own_proj, far_proj])
+    (tied_first_0,), _ = lax.optimization_barrier(((samples,), far_proj))
+    first = first_move(tied_first_0)
+    own_rows = jnp.where(ahead, samples, first)
+    second = second_move(own_rows)
+    odd = z_near(even)
+    even_across = x_peer(even)
+    (tied_third_0,), _ = lax.optimization_barrier(((first,), even_across))
+    third = z_near(tied_third_0)
+    (tied_odd_across_0,), _ = lax.optimization_barrier(((odd,), first))
+    odd_across = x_peer(tied_odd_across_0)
+    (tied_fourth_0,), _ = lax.optimization_barrier(((second,), even_across))
+    fourth = fourth_move(tied_fourth_0)
+    fourth_rows = jnp.where(ahead, first, fourth)
+    (tied_cg0_0, tied_cg0_1,), _ = lax.optimization_barrier(((own_rows, second,), odd))
+    cg0 = core_peer(jnp.stack([tied_cg0_0, tied_cg0_1]))
+    (tied_cg1_0, tied_cg1_1,), _ = lax.optimization_barrier(((third, fourth_rows,), even_across))
+    cg1 = core_peer(jnp.stack([tied_cg1_0, tied_cg1_1]))
+    cq0 = core_peer(jnp.stack([even, odd, even_across, odd_across]))
+    rows_here = (own_rows, second, third, fourth_rows)
+    rows_there = (cg0[0], cg0[1], cg1[0], cg1[1])
+    proj_here = (even, odd, even_across, odd_across)
+    proj_there = (cq0[0], cq0[1], cq0[2], cq0[3])
 
     keep, send, grads = pl.pallas_call(
         functools.partial(group_kernel, factor),
         out_shape=(
-            jax.ShapeDtypeStruct((depth + 16, half), F32),
+            jax.ShapeDtypeStruct((depth + 16, half), BF16),
             jax.ShapeDtypeStruct((depth + 16, half), BF16),
             jax.ShapeDtypeStruct((2, rows, width), BF16),
         ),
-        in_specs=[IN_SMEM] * 2 + [IN_VMEM] * 24,
+        in_specs=[IN_SMEM] * 2 + [IN_VMEM] * 16,
         out_specs=[IN_VMEM] * 3,
         scratch_shapes=[
             pltpu.VMEM((total_rows, width), F32),
@@ -317,14 +350,12 @@
         log_scale,
         *rows_here,
         *rows_there,
-        *early_proj,
-        *late_proj,
-        *(early_there[at] for at in range(4)),
-        *(late_there[at] for at in range(4)),
-    )
-    folded = (keep + x_peer(send).astype(F32)).astype(BF16)
-    share = folded.astype(F32) + y_peer(folded).astype(F32)
-    grads = regroup(grads)
+        *proj_here,
+        *proj_there,
+    )
+    across = xy_peer(send).astype(F32)
+    share = (keep.astype(F32) + y_peer(keep).astype(F32)) + (x_peer(send).astype(F32) + across)
+    grads = jnp.where(is_ahead(x, core), grads, trade_back(grads))
     ours = share[:depth]
     theirs = core_peer(ours)
     grad_proj = jnp.where(

time: 52.2 us -> 47.7 us (0.914)
  starting transfers between devices: 25.4 us -> 22.1 us
  waiting for transfers between devices: 18.1 us -> 17.1 us
    ppermute x19 -> x16, starting transfers between devices: 25.4 us -> 22.1 us  [moved(): lax.ppermute(value, ('blk', 'rep'), [(number(*place), number(*to(*place))...]
    ppermute x19 -> x16, waiting for transfers between devices: 18.1 us -> 17.1 us  [moved(): lax.ppermute(value, ('blk', 'rep'), [(number(*place), number(*to(*place))...]
  transfers between devices with their start and end apart: 19 -> 16, of which waited for: 9 -> 7; matrix products, arithmetic and copies ran while one was open for 4% -> 4% of each run, Pallas kernels for 0% -> 0%
where the time goes in v3:
time: 47.7 us; the launch traced here: 47.6 us
  starting transfers between devices  22.1 us (46%)
  waiting for transfers between devices  17.1 us (36%)
  Pallas kernels  3.09 us (6%)
  local copies, waits for them, and re-layouts  2.41 us (5%)
  between operations  1.46 us (3%)
  other arithmetic  1.36 us (3%)
    ppermute x16, starting transfers between devices, moved(): lax.ppermute(value, ('blk', 'rep'), [(number(*place), number(*to(*place))...  22.1 us
    ppermute x16, waiting for transfers between devices, moved(): lax.ppermute(value, ('blk', 'rep'), [(number(*place), number(*to(*place))...  17.1 us
    pallas_call x1, Pallas kernels, on_device_whole_group(): pl.pallas_call(functools.partial(group_kernel, factor), out_shape=(jax.Sh...  3.09 us
    slice x2, local copies, waits for them, and re-layouts, on_device_whole_group(): return (totals[0:1], totals[1:2], grads[0][None], grads[1][None], grad_proj)  1.24 us
  transfers between devices with their start and end apart: 16, of which 7 were waited for; matrix products, arithmetic and copies ran while one was open for 4% of the time, Pallas kernels for 0%

profile of v3, /device:TPU:1, one launch (start us, length us, event | category | flops | bytes accessed | tf_op | source)
XLA Modules:
  0.0 47.6 jit_solution(14954103790642061606)
XLA Ops:
  0.6 0.0 copy-start
  0.7 0.9 %copy-done = bf16[80,1280]{1,0:T(8,128)(2,1)S(1)} copy-done((bf16[80,1280]{1,0:T(8,128)(2,1)S(1)}, bf16[80,1280]{1,0:T(8,128)(2,1)}, u32[]{:S(2)}) %copy-start) | copy-done | bytes 204824
  1.6 0.0 copy-start.1
  1.6 0.0 copy-start.2
  1.6 0.0 copy-start.3
  1.6 3.2 %collective-permute-start = (bf16[80,640]{1,0:T(8,128)(2,1)S(1)}, bf16[80,640]{1,0:T(8,128)(2,1)S(1)}, u32[]{:S(2)}, u32[]{:S(2)}) collective-permute-start(bf16[80,640]{1,0:T(8,128)(2,1)S(1)} %constant_dynamic-slice_fusion), channel_id=1, source_target_pairs={{0,16},{1,17},{2,18},{3,19},{4,20},{5,21},{6,22},{7,23},{8,24},{9,... | collective-permute-start | bytes 307208 | tf_op jit(solution)/shard_map/ppermute | solution.py:129
  4.8 0.0 copy-done.1
  4.8 0.0 copy-done.2
  4.8 0.0 copy-done.3
  4.8 4.8 %collective-permute-done = bf16[80,640]{1,0:T(8,128)(2,1)S(1)} collective-permute-done((bf16[80,640]{1,0:T(8,128)(2,1)S(1)}, bf16[80,640]{1,0:T(8,128)(2,1)S(1)}, u32[]{:S(2)}, u32[]{:S(2)}) %collective-permute-start) | collective-permute-done | bytes 102432 | tf_op jit(solution)/shard_map/ppermute | solution.py:129
  9.6 2.4 %collective-permute-start.1 = (bf16[24,3200]{1,0:T(8,128)(2,1)S(1)}, bf16[24,3200]{1,0:T(8,128)(2,1)S(1)}, u32[]{:S(2)}, u32[]{:S(2)}) collective-permute-start(bf16[24,3200]{1,0:T(8,128)(2,1)S(1)} %pad_maximum_fusion.4), channel_id=1, source_target_pairs={{0,16},{1,4},{2,18},{3,6},{4,1},{5,21},{6,3},{7,23},{8,24},{9,12},... | collective-permute-start | bytes 460808 | tf_op jit(solution)/shard_map/ppermute | solution.py:129
  12.0 0.5 collective-permute-start.6
  12.5 2.7 %collective-permute-start.3 = (bf16[2,80,640]{2,1,0:T(8,128)(2,1)S(1)}, bf16[2,80,640]{2,1,0:T(8,128)(2,1)S(1)}, u32[]{:S(2)}, u32[]{:S(2)}) collective-permute-start(bf16[2,80,640]{2,1,0:T(8,128)(2,1)S(1)} %get-tuple-element.36.refs_8_), channel_id=1, source_target_pairs={{0,4},{1,5},{2,6},{3,7},{4,0},{5,1},{6,2},{7,3},{8,12},{9,13},{10,... | collective-permute-start | bytes 614408 | tf_op jit(solution)/shard_map/ppermute | solution.py:129
  15.2 0.0 collective-permute-done.1
  15.3 0.4 collective-permute-start.2
  16.4 0.1 pad_add_fusion.place
  16.5 5.3 %collective-permute-done.6.refs_9_ = bf16[2,80,640]{2,1,0:T(8,128)(2,1)S(1)} collective-permute-done((bf16[2,80,640]{2,1,0:T(8,128)(2,1)S(1)}, bf16[2,80,640]{2,1,0:T(8,128)(2,1)S(1)}, u32[]{:S(2)}, u32[]{:S(2)}) %collective-permute-start.6) | collective-permute-done | bytes 204832 | tf_op jit(solution)/shard_map/ppermute | solution.py:129
  21.8 0.0 collective-permute-start.9
  21.8 0.0 collective-permute-done.3.refs_10_
  21.8 0.0 collective-permute-start.4
  21.8 0.0 collective-permute-done.2.refs_1_
  21.8 2.4 %collective-permute-start.5 = (bf16[24,3200]{1,0:T(8,128)(2,1)S(1)}, bf16[24,3200]{1,0:T(8,128)(2,1)S(1)}, u32[]{:S(2)}, u32[]{:S(2)}) collective-permute-start(bf16[24,3200]{1,0:T(8,128)(2,1)S(1)} %collective-permute-done.2.refs_1_), channel_id=1, source_target_pairs={{0,2},{1,9},{2,0},{3,11},{4,12},{5,7},{6,14},{7,5},{8,10},{9,1},{1... | collective-permute-start | bytes 460808 | tf_op jit(solution)/shard_map/ppermute | solution.py:129
  24.3 1.9 %collective-permute-start.7 = (bf16[2,24,3200]{2,1,0:T(8,128)(2,1)S(1)}, bf16[2,24,3200]{2,1,0:T(8,128)(2,1)S(1)}, u32[]{:S(2)}, u32[]{:S(2)}) collective-permute-start(bf16[2,24,3200]{2,1,0:T(8,128)(2,1)S(1)} %pad_maximum_fusion.1), channel_id=1, source_target_pairs={{0,1},{1,0},{2,3},{3,2},{4,5},{5,4},{6,7},{7,6},{8,9},{9,8},{10,11... | collective-permute-start | bytes 921608 | tf_op jit(solution)/shard_map/ppermute | solution.py:129
  26.2 1.0 %collective-permute-done.9.refs_11_ = bf16[2,80,640]{2,1,0:T(8,128)(2,1)S(1)} collective-permute-done((bf16[2,80,640]{2,1,0:T(8,128)(2,1)S(1)}, bf16[2,80,640]{2,1,0:T(8,128)(2,1)S(1)}, u32[]{:S(2)}, u32[]{:S(2)}) %collective-permute-start.9) | collective-permute-done | bytes 204832 | tf_op jit(solution)/shard_map/ppermute | solution.py:129
  27.2 0.1 pad_maximum_fusion
  27.3 2.1 %collective-permute-start.10 = (bf16[4,2,80,640]{3,2,1,0:T(8,128)(2,1)S(1)}, bf16[4,2,80,640]{3,2,1,0:T(8,128)(2,1)S(1)}, u32[]{:S(2)}, u32[]{:S(2)}) collective-permute-start(bf16[4,2,80,640]{3,2,1,0:T(8,128)(2,1)S(1)} %pad_maximum_fusion), channel_id=1, source_target_pairs={{0,1},{1,0},{2,3},{3,2},{4,5},{5,4},{6,7},{7,6},{8,9},{9,8},{10,11... | collective-permute-start | bytes 2457608 | tf_op jit(solution)/shard_map/ppermute | solution.py:129
  29.5 0.0 collective-permute-done.5
  29.5 0.0 collective-permute-done.4.refs_2_
  29.5 0.4 collective-permute-start.8
  29.9 0.0 collective-permute-done.7
  29.9 1.9 %collective-permute-done.8 = bf16[2,24,3200]{2,1,0:T(8,128)(2,1)S(1)} collective-permute-done((bf16[2,24,3200]{2,1,0:T(8,128)(2,1)S(1)}, bf16[2,24,3200]{2,1,0:T(8,128)(2,1)S(1)}, u32[]{:S(2)}, u32[]{:S(2)}) %collective-permute-start.8) | collective-permute-done | bytes 307232 | tf_op jit(solution)/shard_map/ppermute | solution.py:129
  31.9 0.0 collective-permute-done.10
  31.9 0.1 slice_bitcast_fusion
  32.0 3.1 %group_kernel.1 = (bf16[96,640]{1,0:T(8,128)(2,1)S(1)}, bf16[96,640]{1,0:T(8,128)(2,1)S(1)}, bf16[2,24,1280]{2,1,0:T(8,128)(2,1)S(1)}) custom-call(s32[4]{0:T(128)S(1)} %pad_add_fusion.place, f32[1]{0:T(128)S(6)} %copy.10.log_scale, bf16[24,3200]{1,0:T(8,128)(2,1)S(1)} %broadcast_select_fusion.1.refs_0_, ...), custom_call_target="tpu_custom_call" | custom-call | tf_op jit(solution)/shard_map/group_kernel/pallas_call | solution.py:325
  35.1 1.3 %collective-permute-start.11 = (bf16[96,640]{1,0:T(8,128)(2,1)S(1)}, bf16[96,640]{1,0:T(8,128)(2,1)S(1)}, u32[]{:S(2)}, u32[]{:S(2)}) collective-permute-start(bf16[96,640]{1,0:T(8,128)(2,1)S(1)} %get-tuple-element.24), channel_id=1, source_target_pairs={{0,2},{1,3},{2,0},{3,1},{4,6},{5,7},{6,4},{7,5},{8,10},{9,11},{10,... | collective-permute-start | bytes 368648 | tf_op jit(solution)/shard_map/ppermute | solution.py:129
  36.3 1.1 %collective-permute-start.12 = (bf16[96,640]{1,0:T(8,128)(2,1)S(1)}, bf16[96,640]{1,0:T(8,128)(2,1)S(1)}, u32[]{:S(2)}, u32[]{:S(2)}) collective-permute-start(bf16[96,640]{1,0:T(8,128)(2,1)S(1)} %get-tuple-element.25), channel_id=1, source_target_pairs={{0,4},{1,5},{2,6},{3,7},{4,0},{5,1},{6,2},{7,3},{8,12},{9,13},{10,... | collective-permute-start | bytes 368648 | tf_op jit(solution)/shard_map/ppermute | solution.py:129
  37.4 0.4 collective-permute-start.13
  37.8 2.1 %collective-permute-start.14 = (bf16[2,24,1280]{2,1,0:T(8,128)(2,1)S(1)}, bf16[2,24,1280]{2,1,0:T(8,128)(2,1)S(1)}, u32[]{:S(2)}, u32[]{:S(2)}) collective-permute-start(bf16[2,24,1280]{2,1,0:T(8,128)(2,1)S(1)} %get-tuple-element.26), channel_id=1, source_target_pairs={{0,8},{1,4},{2,10},{3,6},{4,1},{5,13},{6,3},{7,15},{8,0},{9,12},{1... | collective-permute-start | bytes 368648 | tf_op jit(solution)/shard_map/ppermute | solution.py:129
  39.9 0.0 collective-permute-done.11
  39.9 0.6 %collective-permute-done.12 = bf16[96,640]{1,0:T(8,128)(2,1)S(1)} collective-permute-done((bf16[96,640]{1,0:T(8,128)(2,1)S(1)}, bf16[96,640]{1,0:T(8,128)(2,1)S(1)}, u32[]{:S(2)}, u32[]{:S(2)}) %collective-permute-start.12) | collective-permute-done | bytes 122912 | tf_op jit(solution)/shard_map/ppermute | solution.py:129
  40.5 3.0 %collective-permute-done.13 = bf16[96,640]{1,0:T(8,128)(2,1)S(1)} collective-permute-done((bf16[96,640]{1,0:T(8,128)(2,1)S(1)}, bf16[96,640]{1,0:T(8,128)(2,1)S(1)}, u32[]{:S(2)}, u32[]{:S(2)}) %collective-permute-start.13) | collective-permute-done | bytes 122912 | tf_op jit(solution)/shard_map/ppermute | solution.py:129
  43.5 0.1 add_add_fusion
  43.6 1.2 %collective-permute-start.15 = (f32[80,640]{1,0:T(8,128)S(1)}, f32[80,640]{1,0:T(8,128)S(1)}, u32[]{:S(2)}, u32[]{:S(2)}) collective-permute-start(f32[80,640]{1,0:T(8,128)S(1)} %slice.67), channel_id=1, source_target_pairs={{0,1},{1,0},{2,3},{3,2},{4,5},{5,4},{6,7},{7,6},{8,9},{9,8},{10,11... | collective-permute-start | bytes 614408 | tf_op jit(solution)/shard_map/ppermute | solution.py:129
  44.8 0.5 %collective-permute-done.14 = bf16[2,24,1280]{2,1,0:T(8,128)(2,1)S(1)} collective-permute-done((bf16[2,24,1280]{2,1,0:T(8,128)(2,1)S(1)}, bf16[2,24,1280]{2,1,0:T(8,128)(2,1)S(1)}, u32[]{:S(2)}, u32[]{:S(2)}) %collective-permute-start.14) | collective-permute-done | bytes 122912 | tf_op jit(solution)/shard_map/ppermute | solution.py:129
  45.3 0.7 %fusion.1 = (bf16[1,24,1280]{2,1,0:T(8,128)(2,1)}, bf16[1,24,1280]{2,1,0:T(8,128)(2,1)}) fusion(bf16[2,24,1280]{2,1,0:T(8,128)(2,1)S(1)} %broadcast_select_fusion.2), kind=kLoop, calls=%fused_computation.22 | loop fusion | bytes 245760 | tf_op jit(solution)/shard_map/slice | solution.py:367
  46.0 0.1 reshape_squeeze.3
  46.1 0.1 reduce_sum.9
  46.2 0.6 %fusion.2 = (f32[1]{0:T(128)}, f32[1]{0:T(128)}) fusion(f32[2]{0:T(128)S(1)} %reduce_sum.9), kind=kLoop, calls=%fused_computation.23 | loop fusion | bytes 16 | tf_op jit(solution)/shard_map/slice | solution.py:367
  46.8 0.0 collective-permute-done.15
  46.8 0.8 %maximum_select_fusion = f32[80,1280]{1,0:T(8,128)} fusion(f32[80,640]{1,0:T(8,128)S(1)} %collective-permute-done.15, f32[80,640]{1,0:T(8,128)S(1)} %slice.67, pred[]{:T(512)S(6)} %eq.11), kind=kLoop, calls=%fused_computation.1 | loop fusion | flops 307200 | bytes 819201 | tf_op jit(solution)/shard_map/jit(_where)/select_n | solution.py:361
  (13 shorter events, 0.3 us)
Async XLA Ops:
  0.6 0.9 %copy-start = (bf16[80,1280]{1,0:T(8,128)(2,1)S(1)}, bf16[80,1280]{1,0:T(8,128)(2,1)}, u32[]{:S(2)}) copy-start(bf16[80,1280]{1,0:T(8,128)(2,1)} %param.8) | copy-start | bytes 614404
  1.6 3.2 %copy-start.1 = (bf16[1,24,1280]{2,1,0:T(8,128)(2,1)S(1)}, bf16[1,24,1280]{2,1,0:T(8,128)(2,1)}, u32[]{:S(2)}) copy-start(bf16[1,24,1280]{2,1,0:T(8,128)(2,1)} %param.7) | copy-start | bytes 184324
  1.6 3.2 %copy-start.2 = (bf16[1,24,1280]{2,1,0:T(8,128)(2,1)S(1)}, bf16[1,24,1280]{2,1,0:T(8,128)(2,1)}, u32[]{:S(2)}) copy-start(bf16[1,24,1280]{2,1,0:T(8,128)(2,1)} %param.5) | copy-start | bytes 184324
  1.6 3.2 %copy-start.3 = (bf16[1,24,640]{2,1,0:T(8,128)(2,1)S(1)}, bf16[1,24,640]{2,1,0:T(8,128)(2,1)}, u32[]{:S(2)}) copy-start(bf16[1,24,640]{2,1,0:T(8,128)(2,1)} %param.6) | copy-start | bytes 92164
  1.6 8.0 %collective-permute-start = (bf16[80,640]{1,0:T(8,128)(2,1)S(1)}, bf16[80,640]{1,0:T(8,128)(2,1)S(1)}, u32[]{:S(2)}, u32[]{:S(2)}) collective-permute-start(bf16[80,640]{1,0:T(8,128)(2,1)S(1)} %constant_dynamic-slice_fusion), channel_id=1, source_target_pairs={{0,16},{1,17},{2,18},{3,19},{4,20},{5,21},{6,22},{7,23},{8,24},{9,... | collective-permute-start | bytes 307208 | tf_op jit(solution)/shard_map/ppermute | solution.py:129
  9.6 5.6 %collective-permute-start.1 = (bf16[24,3200]{1,0:T(8,128)(2,1)S(1)}, bf16[24,3200]{1,0:T(8,128)(2,1)S(1)}, u32[]{:S(2)}, u32[]{:S(2)}) collective-permute-start(bf16[24,3200]{1,0:T(8,128)(2,1)S(1)} %pad_maximum_fusion.4), channel_id=1, source_target_pairs={{0,16},{1,4},{2,18},{3,6},{4,1},{5,21},{6,3},{7,23},{8,24},{9,12},... | collective-permute-start | bytes 460808 | tf_op jit(solution)/shard_map/ppermute | solution.py:129
  12.0 9.7 %collective-permute-start.6 = (bf16[2,80,640]{2,1,0:T(8,128)(2,1)S(1)}, bf16[2,80,640]{2,1,0:T(8,128)(2,1)S(1)}, u32[]{:S(2)}, u32[]{:S(2)}) collective-permute-start(bf16[2,80,640]{2,1,0:T(8,128)(2,1)S(1)} %get-tuple-element.36.refs_8_), channel_id=1, source_target_pairs={{0,8},{1,9},{2,10},{3,11},{4,12},{5,13},{6,14},{7,15},{8,0},{9,1},... | collective-permute-start | bytes 614408 | tf_op jit(solution)/shard_map/ppermute | solution.py:129
  12.5 9.3 %collective-permute-start.3 = (bf16[2,80,640]{2,1,0:T(8,128)(2,1)S(1)}, bf16[2,80,640]{2,1,0:T(8,128)(2,1)S(1)}, u32[]{:S(2)}, u32[]{:S(2)}) collective-permute-start(bf16[2,80,640]{2,1,0:T(8,128)(2,1)S(1)} %get-tuple-element.36.refs_8_), channel_id=1, source_target_pairs={{0,4},{1,5},{2,6},{3,7},{4,0},{5,1},{6,2},{7,3},{8,12},{9,13},{10,... | collective-permute-start | bytes 614408 | tf_op jit(solution)/shard_map/ppermute | solution.py:129
  15.3 6.5 %collective-permute-start.2 = (bf16[24,3200]{1,0:T(8,128)(2,1)S(1)}, bf16[24,3200]{1,0:T(8,128)(2,1)S(1)}, u32[]{:S(2)}, u32[]{:S(2)}) collective-permute-start(bf16[24,3200]{1,0:T(8,128)(2,1)S(1)} %broadcast_select_fusion.1.refs_0_), channel_id=1, source_target_pairs={{0,8},{1,17},{2,10},{3,19},{4,20},{5,13},{6,22},{7,15},{8,0},{9,25... | collective-permute-start | bytes 460808 | tf_op jit(solution)/shard_map/ppermute | solution.py:129
  21.8 5.4 %collective-permute-start.9 = (bf16[2,80,640]{2,1,0:T(8,128)(2,1)S(1)}, bf16[2,80,640]{2,1,0:T(8,128)(2,1)S(1)}, u32[]{:S(2)}, u32[]{:S(2)}) collective-permute-start(bf16[2,80,640]{2,1,0:T(8,128)(2,1)S(1)} %collective-permute-done.6.refs_9_), channel_id=1, source_target_pairs={{0,4},{1,5},{2,6},{3,7},{4,0},{5,1},{6,2},{7,3},{8,12},{9,13},{10,... | collective-permute-start | bytes 614408 | tf_op jit(solution)/shard_map/ppermute | solution.py:129
  21.8 7.7 %collective-permute-start.4 = (bf16[24,3200]{1,0:T(8,128)(2,1)S(1)}, bf16[24,3200]{1,0:T(8,128)(2,1)S(1)}, u32[]{:S(2)}, u32[]{:S(2)}) collective-permute-start(bf16[24,3200]{1,0:T(8,128)(2,1)S(1)} %collective-permute-done.1), channel_id=1, source_target_pairs={{0,8},{1,9},{2,10},{3,11},{4,12},{5,13},{6,14},{7,15},{8,0},{9,1},... | collective-permute-start | bytes 460808 | tf_op jit(solution)/shard_map/ppermute | solution.py:129
  21.8 7.7 %collective-permute-start.5 = (bf16[24,3200]{1,0:T(8,128)(2,1)S(1)}, bf16[24,3200]{1,0:T(8,128)(2,1)S(1)}, u32[]{:S(2)}, u32[]{:S(2)}) collective-permute-start(bf16[24,3200]{1,0:T(8,128)(2,1)S(1)} %collective-permute-done.2.refs_1_), channel_id=1, source_target_pairs={{0,2},{1,9},{2,0},{3,11},{4,12},{5,7},{6,14},{7,5},{8,10},{9,1},{1... | collective-permute-start | bytes 460808 | tf_op jit(solution)/shard_map/ppermute | solution.py:129
  24.3 5.6 %collective-permute-start.7 = (bf16[2,24,3200]{2,1,0:T(8,128)(2,1)S(1)}, bf16[2,24,3200]{2,1,0:T(8,128)(2,1)S(1)}, u32[]{:S(2)}, u32[]{:S(2)}) collective-permute-start(bf16[2,24,3200]{2,1,0:T(8,128)(2,1)S(1)} %pad_maximum_fusion.1), channel_id=1, source_target_pairs={{0,1},{1,0},{2,3},{3,2},{4,5},{5,4},{6,7},{7,6},{8,9},{9,8},{10,11... | collective-permute-start | bytes 921608 | tf_op jit(solution)/shard_map/ppermute | solution.py:129
  27.3 4.5 %collective-permute-start.10 = (bf16[4,2,80,640]{3,2,1,0:T(8,128)(2,1)S(1)}, bf16[4,2,80,640]{3,2,1,0:T(8,128)(2,1)S(1)}, u32[]{:S(2)}, u32[]{:S(2)}) collective-permute-start(bf16[4,2,80,640]{3,2,1,0:T(8,128)(2,1)S(1)} %pad_maximum_fusion), channel_id=1, source_target_pairs={{0,1},{1,0},{2,3},{3,2},{4,5},{5,4},{6,7},{7,6},{8,9},{9,8},{10,11... | collective-permute-start | bytes 2457608 | tf_op jit(solution)/shard_map/ppermute | solution.py:129
  29.5 2.3 %collective-permute-start.8 = (bf16[2,24,3200]{2,1,0:T(8,128)(2,1)S(1)}, bf16[2,24,3200]{2,1,0:T(8,128)(2,1)S(1)}, u32[]{:S(2)}, u32[]{:S(2)}) collective-permute-start(bf16[2,24,3200]{2,1,0:T(8,128)(2,1)S(1)} %pad_maximum_fusion.2), channel_id=1, source_target_pairs={{0,1},{1,0},{2,3},{3,2},{4,5},{5,4},{6,7},{7,6},{8,9},{9,8},{10,11... | collective-permute-start | bytes 921608 | tf_op jit(solution)/shard_map/ppermute | solution.py:129
  35.1 4.8 %collective-permute-start.11 = (bf16[96,640]{1,0:T(8,128)(2,1)S(1)}, bf16[96,640]{1,0:T(8,128)(2,1)S(1)}, u32[]{:S(2)}, u32[]{:S(2)}) collective-permute-start(bf16[96,640]{1,0:T(8,128)(2,1)S(1)} %get-tuple-element.24), channel_id=1, source_target_pairs={{0,2},{1,3},{2,0},{3,1},{4,6},{5,7},{6,4},{7,5},{8,10},{9,11},{10,... | collective-permute-start | bytes 368648 | tf_op jit(solution)/shard_map/ppermute | solution.py:129
  36.3 4.2 %collective-permute-start.12 = (bf16[96,640]{1,0:T(8,128)(2,1)S(1)}, bf16[96,640]{1,0:T(8,128)(2,1)S(1)}, u32[]{:S(2)}, u32[]{:S(2)}) collective-permute-start(bf16[96,640]{1,0:T(8,128)(2,1)S(1)} %get-tuple-element.25), channel_id=1, source_target_pairs={{0,4},{1,5},{2,6},{3,7},{4,0},{5,1},{6,2},{7,3},{8,12},{9,13},{10,... | collective-permute-start | bytes 368648 | tf_op jit(solution)/shard_map/ppermute | solution.py:129
  37.4 6.1 %collective-permute-start.13 = (bf16[96,640]{1,0:T(8,128)(2,1)S(1)}, bf16[96,640]{1,0:T(8,128)(2,1)S(1)}, u32[]{:S(2)}, u32[]{:S(2)}) collective-permute-start(bf16[96,640]{1,0:T(8,128)(2,1)S(1)} %get-tuple-element.25), channel_id=1, source_target_pairs={{0,6},{1,7},{2,4},{3,5},{4,2},{5,3},{6,0},{7,1},{8,14},{9,15},{10,... | collective-permute-start | bytes 368648 | tf_op jit(solution)/shard_map/ppermute | solution.py:129
  37.8 7.5 %collective-permute-start.14 = (bf16[2,24,1280]{2,1,0:T(8,128)(2,1)S(1)}, bf16[2,24,1280]{2,1,0:T(8,128)(2,1)S(1)}, u32[]{:S(2)}, u32[]{:S(2)}) collective-permute-start(bf16[2,24,1280]{2,1,0:T(8,128)(2,1)S(1)} %get-tuple-element.26), channel_id=1, source_target_pairs={{0,8},{1,4},{2,10},{3,6},{4,1},{5,13},{6,3},{7,15},{8,0},{9,12},{1... | collective-permute-start | bytes 368648 | tf_op jit(solution)/shard_map/ppermute | solution.py:129
  43.6 3.2 %collective-permute-start.15 = (f32[80,640]{1,0:T(8,128)S(1)}, f32[80,640]{1,0:T(8,128)S(1)}, u32[]{:S(2)}, u32[]{:S(2)}) collective-permute-start(f32[80,640]{1,0:T(8,128)S(1)} %slice.67), channel_id=1, source_target_pairs={{0,1},{1,0},{2,3},{3,2},{4,5},{5,4},{6,7},{7,6},{8,9},{9,8},{10,11... | collective-permute-start | bytes 614408 | tf_op jit(solution)/shard_map/ppermute | solution.py:129

commit v4 on v3

--- a/solution.py
+++ b/solution.py
@@ -118,10 +118,15 @@
 IN_VMEM = pl.BlockSpec(memory_space=pltpu.VMEM)
 IN_SMEM = pl.BlockSpec(memory_space=pltpu.SMEM)
 ROW_STEPS = ((0, 1, 3, 2), (0, 2, 1, 3))
-PROJ_STEPS = (((0, 2), 0), ((1, 3), 0), ((0, 2), 1), ((1, 3), 1))
+PROJ_STEPS = (((0, 2), 0), ((1,), 0), ((3,), 0), ((0, 2), 1), ((1, 3), 1))
 
 def number(z, x, y, core):
     return (z * 2 + x) * 4 + y * 2 + core
+
+
+def own_place():
+    blk, rep = lax.axis_index("blk"), lax.axis_index("rep")
+    return blk // 2, blk % 2, rep // 2, rep % 2
 
 
 def moved(value, to):
@@ -198,12 +203,13 @@
     return lax.rsqrt(jnp.sum(values * values, axis=-1, keepdims=True) + 1e-06)
 
 
-def group_kernel(factor, place, log_scale, *refs):
-    rows_here, rows_there, projs = refs[:4], refs[4:8], refs[8:16]
-    keep, send, grads = refs[16:19]
-    image, text, hidden, hidden_t, norms, proj, coefs, grad_all, grad_cols, share = refs[19:]
-    z, x, y, core = (place[at] for at in range(4))
-    rows, depth = rows_here[0].shape[0], projs[0].shape[1]
+def group_kernel(factor, log_scale, *refs):
+    count = 2 * len(PROJ_STEPS)
+    rows_here, rows_there, projs = refs[:4], refs[4:8], refs[8 : 8 + count]
+    keep, send, grads = refs[8 + count : 11 + count]
+    image, text, hidden, hidden_t, norms, proj, coefs, grad_all, grad_cols, share = refs[11 + count :]
+    z, x, y, core = own_place()
+    rows, depth = rows_here[0].shape[0], proj.shape[1] // 8
     width = image.shape[1]
     half = width // 2
     ahead = is_ahead(x, core)
@@ -215,10 +221,11 @@
             text[pl.ds(start, rows), :] = block[:, width : 2 * width].astype(F32)
             hidden[pl.ds(start, rows), :] = block[:, 2 * width :].astype(F32)
     for at, blocks in enumerate(projs):
-        steps, column = PROJ_STEPS[at % 4]
+        side, kind = divmod(at, len(PROJ_STEPS))
+        steps, column = PROJ_STEPS[kind]
         for block, step in enumerate(steps):
             start = pl.multiple_of(((z ^ step) * 2 + (x ^ column)) * depth, 16)
-            proj[core ^ (at // 4), pl.ds(start, depth), :] = blocks[block]
+            proj[core ^ side, pl.ds(start, depth), :] = blocks[block]
     hidden_short = hidden[...].astype(BF16)
     for side in range(2):
         text[:, side * half : (side + 1) * half] += jnp.dot(
@@ -286,42 +293,37 @@
     depth = proj_window.shape[0]
     total_rows, total_depth, half = rows * 8, depth * 8, width // 2
     factor = 1.0 / (2.0 * total_rows * lax.axis_size("rep"))
-    blk, rep = lax.axis_index("blk"), lax.axis_index("rep")
-    z, x, y, core = blk // 2, blk % 2, rep // 2, rep % 2
-    place = jnp.stack([z, x, y, core]).astype(jnp.int32)
-
-    def own_and_z(value):
-        far = z_far(value)
-        return value, z_near(value), far, z_near(far)
-
+    z, x, y, core = own_place()
     ahead = is_ahead(x, core)
-    own_proj = lax.dynamic_slice_in_dim(proj_window, core * half, half, 1)
+    own = lax.dynamic_slice_in_dim(proj_window, core * half, half, 1)
+    own, = lax.optimization_barrier((own,))
     samples = jnp.concatenate([image_embed[0], text_rest[0], text_hidden[0]], axis=1)
-    far_proj = z_far(own_proj)
-    even = jnp.stack([own_proj, far_proj])
-    (tied_first_0,), _ = lax.optimization_barrier(((samples,), far_proj))
-    first = first_move(tied_first_0)
+    far = z_far(own)
+    even = jnp.stack([own, far])
+    first = first_move(samples)
     own_rows = jnp.where(ahead, samples, first)
-    second = second_move(own_rows)
-    odd = z_near(even)
-    even_across = x_peer(even)
-    (tied_third_0,), _ = lax.optimization_barrier(((first,), even_across))
-    third = z_near(tied_third_0)
-    (tied_odd_across_0,), _ = lax.optimization_barrier(((odd,), first))
-    odd_across = x_peer(tied_odd_across_0)
-    (tied_fourth_0,), _ = lax.optimization_barrier(((second,), even_across))
-    fourth = fourth_move(tied_fourth_0)
+    near = z_near(own)[None]
+    (tied_second_0,), _ = lax.optimization_barrier(((own_rows,), far))
+    second = second_move(tied_second_0)
+    last = z_near(far)[None]
+    even_x = x_peer(even)
+    third = z_near(first)
+    (tied_odd_x_0, tied_odd_x_1,), _ = lax.optimization_barrier(((near, last,), first))
+    odd_x = x_peer(jnp.concatenate([tied_odd_x_0, tied_odd_x_1]))
+    fourth = fourth_move(second)
     fourth_rows = jnp.where(ahead, first, fourth)
-    (tied_cg0_0, tied_cg0_1,), _ = lax.optimization_barrier(((own_rows, second,), odd))
+    (tied_cg0_0, tied_cg0_1,), _ = lax.optimization_barrier(((own_rows, second,), odd_x))
     cg0 = core_peer(jnp.stack([tied_cg0_0, tied_cg0_1]))
-    (tied_cg1_0, tied_cg1_1,), _ = lax.optimization_barrier(((third, fourth_rows,), even_across))
-    cg1 = core_peer(jnp.stack([tied_cg1_0, tied_cg1_1]))
-    cq0 = core_peer(jnp.stack([even, odd, even_across, odd_across]))
+    cg1 = core_peer(third)
+    cg2 = core_peer(fourth_rows)
+    cq0 = core_peer(jnp.concatenate([even, near, last, even_x]))
+    (tied_cq1_0,), _ = lax.optimization_barrier(((odd_x,), third))
+    cq1 = core_peer(tied_cq1_0)
     rows_here = (own_rows, second, third, fourth_rows)
-    rows_there = (cg0[0], cg0[1], cg1[0], cg1[1])
-    proj_here = (even, odd, even_across, odd_across)
-    proj_there = (cq0[0], cq0[1], cq0[2], cq0[3])
-
+    rows_there = (cg0[0], cg0[1], cg1, cg2)
+    proj_here = (even, near, last, even_x, odd_x)
+    proj_there = (cq0[0:2], cq0[2:3], cq0[3:4], cq0[4:6], cq1)
+    arrived = rows_here + rows_there + proj_here + proj_there
     keep, send, grads = pl.pallas_call(
         functools.partial(group_kernel, factor),
         out_shape=(
@@ -329,7 +331,7 @@
             jax.ShapeDtypeStruct((depth + 16, half), BF16),
             jax.ShapeDtypeStruct((2, rows, width), BF16),
         ),
-        in_specs=[IN_SMEM] * 2 + [IN_VMEM] * 16,
+        in_specs=[IN_SMEM] + [IN_VMEM] * len(arrived),
         out_specs=[IN_VMEM] * 3,
         scratch_shapes=[
             pltpu.VMEM((total_rows, width), F32),
@@ -346,16 +348,14 @@
         compiler_params=pltpu.CompilerParams(vmem_limit_bytes=40 * 2**20),
         name="group_kernel",
     )(
-        place,
         log_scale,
-        *rows_here,
-        *rows_there,
-        *proj_here,
-        *proj_there,
-    )
-    across = xy_peer(send).astype(F32)
-    share = (keep.astype(F32) + y_peer(keep).astype(F32)) + (x_peer(send).astype(F32) + across)
-    grads = jnp.where(is_ahead(x, core), grads, trade_back(grads))
+        *arrived
+    )
+    over_y, over_x, over_both = y_peer(keep), x_peer(send), xy_peer(send)
+    (tied_grads,), _ = lax.optimization_barrier(((grads,), over_y))
+    grads = jnp.where(ahead, grads, trade_back(tied_grads))
+    image_out, text_out = grads[0][None], grads[1][None]
+    share = (keep.astype(F32) + over_y.astype(F32)) + (over_x.astype(F32) + over_both.astype(F32))
     ours = share[:depth]
     theirs = core_peer(ours)
     grad_proj = jnp.where(
@@ -364,7 +364,7 @@
         jnp.concatenate([theirs, ours], axis=1),
     )
     totals = jnp.sum(share[depth, :24].reshape(2, 12), axis=1)
-    return totals[0:1], totals[1:2], grads[0][None], grads[1][None], grad_proj
+    return totals[0:1], totals[1:2], image_out, text_out, grad_proj
 
 
 def solution(mesh):

time: 47.7 us -> 44 us (0.922)
  waiting for transfers between devices: 17.1 us -> 9.9 us
  starting transfers between devices: 22.1 us -> 26.2 us
  Pallas kernels: 3.09 us -> 2.56 us
    ppermute x16 -> x19, waiting for transfers between devices: 17.1 us -> 9.9 us  [moved(): lax.ppermute(value, ('blk', 'rep'), [(number(*place), number(*to(*place))...]
    ppermute x16 -> x19, starting transfers between devices: 22.1 us -> 26.2 us  [moved(): lax.ppermute(value, ('blk', 'rep'), [(number(*place), number(*to(*place))...]
    pallas_call x1, Pallas kernels: 3.09 us -> 2.56 us  [on_device_whole_group(): pl.pallas_call(functools.partial(group_kernel, factor), out_shape=(jax.Sh...]
    unnamed x8 -> x12, local copies, waits for them, and re-layouts: 0.92 us -> 0.98 us
    slice x2 -> x4, local copies, waits for them, and re-layouts: 1.24 us -> 1.3 us  [the longest x1 0.65 us: on_device_whole_group(): image_out, text_out = (grads[0][None], grads[1][None])]
  transfers between devices with their start and end apart: 16 -> 19, of which waited for: 7 -> 6; matrix products, arithmetic and copies ran while one was open for 4% -> 4% of each run, Pallas kernels for 0% -> 0%
where the time goes in v4:
time: 44 us; the launch traced here: 43.8 us
  starting transfers between devices  26.2 us (60%)
  waiting for transfers between devices  9.9 us (22%)
  Pallas kernels  2.56 us (6%)
  local copies, waits for them, and re-layouts  2.45 us (6%)
  between operations  1.5 us (3%)
  other arithmetic  1.14 us (3%)
    ppermute x19, starting transfers between devices, moved(): lax.ppermute(value, ('blk', 'rep'), [(number(*place), number(*to(*place))...  26.2 us
    ppermute x19, waiting for transfers between devices, moved(): lax.ppermute(value, ('blk', 'rep'), [(number(*place), number(*to(*place))...  9.9 us
    pallas_call x1, Pallas kernels, on_device_whole_group(): pl.pallas_call(functools.partial(group_kernel, factor), out_shape=(jax.Sh...  2.56 us
    unnamed x12, local copies, waits for them, and re-layouts  0.98 us
  transfers between devices with their start and end apart: 19, of which 6 were waited for; matrix products, arithmetic and copies ran while one was open for 4% of the time, Pallas kernels for 0%

profile of v4, /device:TPU:1, one launch (start us, length us, event | category | flops | bytes accessed | tf_op | source)
XLA Modules:
  0.0 43.8 jit_solution(12221401044474557393)
XLA Ops:
  0.6 0.0 copy-start
  0.7 0.9 %copy-done = bf16[80,1280]{1,0:T(8,128)(2,1)S(1)} copy-done((bf16[80,1280]{1,0:T(8,128)(2,1)S(1)}, bf16[80,1280]{1,0:T(8,128)(2,1)}, u32[]{:S(2)}) %copy-start) | copy-done | bytes 204824
  1.6 0.0 copy-start.1
  1.6 0.0 copy-start.2
  1.6 0.0 copy-start.3
  1.6 3.2 %collective-permute-start.1 = (bf16[80,640]{1,0:T(8,128)(2,1)S(1)}, bf16[80,640]{1,0:T(8,128)(2,1)S(1)}, u32[]{:S(2)}, u32[]{:S(2)}) collective-permute-start(bf16[80,640]{1,0:T(8,128)(2,1)S(1)} %constant_dynamic-slice_fusion), channel_id=1, source_target_pairs={{0,16},{1,17},{2,18},{3,19},{4,20},{5,21},{6,22},{7,23},{8,24},{9,... | collective-permute-start | bytes 307208 | tf_op jit(solution)/shard_map/ppermute | solution.py:134
  4.8 1.3 %collective-permute-start.5 = (bf16[80,640]{1,0:T(8,128)(2,1)S(1)}, bf16[80,640]{1,0:T(8,128)(2,1)S(1)}, u32[]{:S(2)}, u32[]{:S(2)}) collective-permute-start(bf16[80,640]{1,0:T(8,128)(2,1)S(1)} %constant_dynamic-slice_fusion), channel_id=1, source_target_pairs={{0,8},{1,9},{2,10},{3,11},{4,12},{5,13},{6,14},{7,15},{8,0},{9,1},... | collective-permute-start | bytes 307208 | tf_op jit(solution)/shard_map/ppermute | solution.py:134
  6.1 0.0 copy-done.1
  6.1 0.0 copy-done.2
  6.1 0.0 copy-done.3
  6.1 2.4 %collective-permute-start = (bf16[24,3200]{1,0:T(8,128)(2,1)S(1)}, bf16[24,3200]{1,0:T(8,128)(2,1)S(1)}, u32[]{:S(2)}, u32[]{:S(2)}) collective-permute-start(bf16[24,3200]{1,0:T(8,128)(2,1)S(1)} %pad_maximum_fusion.3), channel_id=1, source_target_pairs={{0,16},{1,4},{2,18},{3,6},{4,1},{5,21},{6,3},{7,23},{8,24},{9,12},... | collective-permute-start | bytes 460808 | tf_op jit(solution)/shard_map/ppermute | solution.py:134
  9.2 0.0 collective-permute-done.1
  9.2 0.1 collective-permute-start.11
  9.3 3.1 %collective-permute-start.6 = (bf16[80,640]{1,0:T(8,128)(2,1)S(1)}, bf16[80,640]{1,0:T(8,128)(2,1)S(1)}, u32[]{:S(2)}, u32[]{:S(2)}) collective-permute-start(bf16[80,640]{1,0:T(8,128)(2,1)S(1)} %collective-permute-done.1), channel_id=1, source_target_pairs={{0,8},{1,9},{2,10},{3,11},{4,12},{5,13},{6,14},{7,15},{8,0},{9,1},... | collective-permute-start | bytes 307208 | tf_op jit(solution)/shard_map/ppermute | solution.py:134
  12.4 0.0 collective-permute-done.5
  12.4 0.0 collective-permute-done
  12.5 3.7 %collective-permute-start.2 = (bf16[24,3200]{1,0:T(8,128)(2,1)S(1)}, bf16[24,3200]{1,0:T(8,128)(2,1)S(1)}, u32[]{:S(2)}, u32[]{:S(2)}) collective-permute-start(bf16[24,3200]{1,0:T(8,128)(2,1)S(1)} %broadcast_select_fusion.1.refs_0_), channel_id=1, source_target_pairs={{0,8},{1,17},{2,10},{3,19},{4,20},{5,13},{6,22},{7,15},{8,0},{9,25... | collective-permute-start | bytes 460808 | tf_op jit(solution)/shard_map/ppermute | solution.py:134
  16.1 0.0 collective-permute-start.3
  16.2 0.0 collective-permute-done.6
  16.2 0.3 collective-permute-start.7
  16.5 0.0 collective-permute-done.11.refs_11_
  16.5 2.2 %collective-permute-start.12 = (bf16[6,80,640]{2,1,0:T(8,128)(2,1)S(1)}, bf16[6,80,640]{2,1,0:T(8,128)(2,1)S(1)}, u32[]{:S(2)}, u32[]{:S(2)}) collective-permute-start(bf16[6,80,640]{2,1,0:T(8,128)(2,1)S(1)} %constant_dynamic-update-slice_fusion), channel_id=1, source_target_pairs={{0,1},{1,0},{2,3},{3,2},{4,5},{5,4},{6,7},{7,6},{8,9},{9,8},{10,11... | collective-permute-start | bytes 1843208 | tf_op jit(solution)/shard_map/ppermute | solution.py:134
  18.7 1.8 %collective-permute-done.2.refs_1_ = bf16[24,3200]{1,0:T(8,128)(2,1)S(1)} collective-permute-done((bf16[24,3200]{1,0:T(8,128)(2,1)S(1)}, bf16[24,3200]{1,0:T(8,128)(2,1)S(1)}, u32[]{:S(2)}, u32[]{:S(2)}) %collective-permute-start.2) | collective-permute-done | bytes 153632 | tf_op jit(solution)/shard_map/ppermute | solution.py:134
  20.5 0.0 collective-permute-start.4
  20.5 2.6 %collective-permute-done.3.refs_2_ = bf16[24,3200]{1,0:T(8,128)(2,1)S(1)} collective-permute-done((bf16[24,3200]{1,0:T(8,128)(2,1)S(1)}, bf16[24,3200]{1,0:T(8,128)(2,1)S(1)}, u32[]{:S(2)}, u32[]{:S(2)}) %collective-permute-start.3) | collective-permute-done | bytes 153632 | tf_op jit(solution)/shard_map/ppermute | solution.py:134
  23.1 2.9 %collective-permute-start.9 = (bf16[24,3200]{1,0:T(8,128)(2,1)S(1)}, bf16[24,3200]{1,0:T(8,128)(2,1)S(1)}, u32[]{:S(2)}, u32[]{:S(2)}) collective-permute-start(bf16[24,3200]{1,0:T(8,128)(2,1)S(1)} %collective-permute-done.3.refs_2_), channel_id=1, source_target_pairs={{0,1},{1,0},{2,3},{3,2},{4,5},{5,4},{6,7},{7,6},{8,9},{9,8},{10,11... | collective-permute-start | bytes 460808 | tf_op jit(solution)/shard_map/ppermute | solution.py:134
  25.9 0.0 collective-permute-done.7.refs_12_
  26.0 0.1 collective-permute-start.8
  26.0 0.5 %collective-permute-start.13 = (bf16[2,80,640]{2,1,0:T(8,128)(2,1)S(1)}, bf16[2,80,640]{2,1,0:T(8,128)(2,1)S(1)}, u32[]{:S(2)}, u32[]{:S(2)}) collective-permute-start(bf16[2,80,640]{2,1,0:T(8,128)(2,1)S(1)} %collective-permute-done.7.refs_12_), channel_id=1, source_target_pairs={{0,1},{1,0},{2,3},{3,2},{4,5},{5,4},{6,7},{7,6},{8,9},{9,8},{10,11... | collective-permute-start | bytes 614408 | tf_op jit(solution)/shard_map/ppermute | solution.py:134
  26.5 0.0 collective-permute-done.4
  26.6 1.6 %collective-permute-start.10 = (bf16[24,3200]{1,0:T(8,128)(2,1)S(1)}, bf16[24,3200]{1,0:T(8,128)(2,1)S(1)}, u32[]{:S(2)}, u32[]{:S(2)}) collective-permute-start(bf16[24,3200]{1,0:T(8,128)(2,1)S(1)} %broadcast_select_fusion.refs_3_), channel_id=1, source_target_pairs={{0,1},{1,0},{2,3},{3,2},{4,5},{5,4},{6,7},{7,6},{8,9},{9,8},{10,11... | collective-permute-start | bytes 460808 | tf_op jit(solution)/shard_map/ppermute | solution.py:134
  28.1 0.0 collective-permute-done.8
  28.2 0.0 collective-permute-done.12
  28.3 0.0 collective-permute-done.9.refs_6_
  28.3 0.0 collective-permute-done.13.refs_17_
  28.3 0.9 %collective-permute-done.10.refs_7_ = bf16[24,3200]{1,0:T(8,128)(2,1)S(1)} collective-permute-done((bf16[24,3200]{1,0:T(8,128)(2,1)S(1)}, bf16[24,3200]{1,0:T(8,128)(2,1)S(1)}, u32[]{:S(2)}, u32[]{:S(2)}) %collective-permute-start.10) | collective-permute-done | bytes 153632 | tf_op jit(solution)/shard_map/ppermute | solution.py:134
  29.2 2.6 %group_kernel.1 = (bf16[96,640]{1,0:T(8,128)(2,1)S(1)}, bf16[96,640]{1,0:T(8,128)(2,1)S(1)}, bf16[2,24,1280]{2,1,0:T(8,128)(2,1)S(1)}) custom-call(f32[1]{0:T(128)S(6)} %copy.14.log_scale, bf16[24,3200]{1,0:T(8,128)(2,1)S(1)} %broadcast_select_fusion.1.refs_0_, bf16[24,3200]{1,0:T(8,128)(2,1)S(1)} %collective-permute-done.2.refs_1_, ...), custom_call_target="tpu_custom_call" | custom-call | tf_op jit(solution)/shard_map/group_kernel/pallas_call | solution.py:327
  31.7 1.3 %collective-permute-start.14 = (bf16[96,640]{1,0:T(8,128)(2,1)S(1)}, bf16[96,640]{1,0:T(8,128)(2,1)S(1)}, u32[]{:S(2)}, u32[]{:S(2)}) collective-permute-start(bf16[96,640]{1,0:T(8,128)(2,1)S(1)} %get-tuple-element.21), channel_id=1, source_target_pairs={{0,2},{1,3},{2,0},{3,1},{4,6},{5,7},{6,4},{7,5},{8,10},{9,11},{10,... | collective-permute-start | bytes 368648 | tf_op jit(solution)/shard_map/ppermute | solution.py:134
  33.0 0.0 collective-permute-start.15
  33.0 1.4 %collective-permute-start.16 = (bf16[96,640]{1,0:T(8,128)(2,1)S(1)}, bf16[96,640]{1,0:T(8,128)(2,1)S(1)}, u32[]{:S(2)}, u32[]{:S(2)}) collective-permute-start(bf16[96,640]{1,0:T(8,128)(2,1)S(1)} %get-tuple-element.22), channel_id=1, source_target_pairs={{0,6},{1,7},{2,4},{3,5},{4,2},{5,3},{6,0},{7,1},{8,14},{9,15},{10,... | collective-permute-start | bytes 368648 | tf_op jit(solution)/shard_map/ppermute | solution.py:134
  34.4 1.9 %collective-permute-done.14 = bf16[96,640]{1,0:T(8,128)(2,1)S(1)} collective-permute-done((bf16[96,640]{1,0:T(8,128)(2,1)S(1)}, bf16[96,640]{1,0:T(8,128)(2,1)S(1)}, u32[]{:S(2)}, u32[]{:S(2)}) %collective-permute-start.14) | collective-permute-done | bytes 122912 | tf_op jit(solution)/shard_map/ppermute | solution.py:134
  36.3 0.7 %collective-permute-start.17 = (bf16[2,24,1280]{2,1,0:T(8,128)(2,1)S(1)}, bf16[2,24,1280]{2,1,0:T(8,128)(2,1)S(1)}, u32[]{:S(2)}, u32[]{:S(2)}) collective-permute-start(bf16[2,24,1280]{2,1,0:T(8,128)(2,1)S(1)} %get-tuple-element.24), channel_id=1, source_target_pairs={{0,8},{1,4},{2,10},{3,6},{4,1},{5,13},{6,3},{7,15},{8,0},{9,12},{1... | collective-permute-start | bytes 368648 | tf_op jit(solution)/shard_map/ppermute | solution.py:134
  37.1 0.2 collective-permute-done.15
  37.3 2.6 %collective-permute-done.16 = bf16[96,640]{1,0:T(8,128)(2,1)S(1)} collective-permute-done((bf16[96,640]{1,0:T(8,128)(2,1)S(1)}, bf16[96,640]{1,0:T(8,128)(2,1)S(1)}, u32[]{:S(2)}, u32[]{:S(2)}) %collective-permute-start.16) | collective-permute-done | bytes 122912 | tf_op jit(solution)/shard_map/ppermute | solution.py:134
  39.8 0.1 add_add_fusion
  39.9 1.6 %collective-permute-start.18 = (f32[80,640]{1,0:T(8,128)S(1)}, f32[80,640]{1,0:T(8,128)S(1)}, u32[]{:S(2)}, u32[]{:S(2)}) collective-permute-start(f32[80,640]{1,0:T(8,128)S(1)} %slice.57), channel_id=1, source_target_pairs={{0,1},{1,0},{2,3},{3,2},{4,5},{5,4},{6,7},{7,6},{8,9},{9,8},{10,11... | collective-permute-start | bytes 614408 | tf_op jit(solution)/shard_map/ppermute | solution.py:134
  41.5 0.1 reshape_squeeze.3
  41.6 0.1 reduce_sum.9
  41.7 0.6 %fusion.3 = (f32[1]{0:T(128)}, f32[1]{0:T(128)}) fusion(f32[2]{0:T(128)S(1)} %reduce_sum.9), kind=kLoop, calls=%fused_computation.21 | loop fusion | bytes 16 | tf_op jit(solution)/shard_map/slice | solution.py:367
  42.3 0.0 collective-permute-done.17
  42.3 0.7 %fusion.2 = (bf16[1,24,1280]{2,1,0:T(8,128)(2,1)}, bf16[1,24,1280]{2,1,0:T(8,128)(2,1)}) fusion(bf16[2,24,1280]{2,1,0:T(8,128)(2,1)S(1)} %broadcast_select_fusion.2), kind=kLoop, calls=%fused_computation.20 | loop fusion | bytes 245760 | tf_op jit(solution)/shard_map/slice | solution.py:357
  43.0 0.0 collective-permute-done.18
  43.0 0.8 %maximum_select_fusion = f32[80,1280]{1,0:T(8,128)} fusion(f32[80,640]{1,0:T(8,128)S(1)} %collective-permute-done.18, f32[80,640]{1,0:T(8,128)S(1)} %slice.57, pred[]{:T(512)S(6)} %eq.10), kind=kLoop, calls=%fused_computation | loop fusion | flops 307200 | bytes 819201 | tf_op jit(solution)/shard_map/jit(_where)/select_n | solution.py:361
  (18 shorter events, 0.4 us)
Async XLA Ops:
  0.6 0.9 %copy-start = (bf16[80,1280]{1,0:T(8,128)(2,1)S(1)}, bf16[80,1280]{1,0:T(8,128)(2,1)}, u32[]{:S(2)}) copy-start(bf16[80,1280]{1,0:T(8,128)(2,1)} %param.8) | copy-start | bytes 614404
  1.6 4.5 %copy-start.1 = (bf16[1,24,1280]{2,1,0:T(8,128)(2,1)S(1)}, bf16[1,24,1280]{2,1,0:T(8,128)(2,1)}, u32[]{:S(2)}) copy-start(bf16[1,24,1280]{2,1,0:T(8,128)(2,1)} %param.7) | copy-start | bytes 184324
  1.6 4.5 %copy-start.2 = (bf16[1,24,1280]{2,1,0:T(8,128)(2,1)S(1)}, bf16[1,24,1280]{2,1,0:T(8,128)(2,1)}, u32[]{:S(2)}) copy-start(bf16[1,24,1280]{2,1,0:T(8,128)(2,1)} %param.5) | copy-start | bytes 184324
  1.6 4.5 %copy-start.3 = (bf16[1,24,640]{2,1,0:T(8,128)(2,1)S(1)}, bf16[1,24,640]{2,1,0:T(8,128)(2,1)}, u32[]{:S(2)}) copy-start(bf16[1,24,640]{2,1,0:T(8,128)(2,1)} %param.6) | copy-start | bytes 92164
  1.6 7.6 %collective-permute-start.1 = (bf16[80,640]{1,0:T(8,128)(2,1)S(1)}, bf16[80,640]{1,0:T(8,128)(2,1)S(1)}, u32[]{:S(2)}, u32[]{:S(2)}) collective-permute-start(bf16[80,640]{1,0:T(8,128)(2,1)S(1)} %constant_dynamic-slice_fusion), channel_id=1, source_target_pairs={{0,16},{1,17},{2,18},{3,19},{4,20},{5,21},{6,22},{7,23},{8,24},{9,... | collective-permute-start | bytes 307208 | tf_op jit(solution)/shard_map/ppermute | solution.py:134
  4.8 7.6 %collective-permute-start.5 = (bf16[80,640]{1,0:T(8,128)(2,1)S(1)}, bf16[80,640]{1,0:T(8,128)(2,1)S(1)}, u32[]{:S(2)}, u32[]{:S(2)}) collective-permute-start(bf16[80,640]{1,0:T(8,128)(2,1)S(1)} %constant_dynamic-slice_fusion), channel_id=1, source_target_pairs={{0,8},{1,9},{2,10},{3,11},{4,12},{5,13},{6,14},{7,15},{8,0},{9,1},... | collective-permute-start | bytes 307208 | tf_op jit(solution)/shard_map/ppermute | solution.py:134
  6.1 6.3 %collective-permute-start = (bf16[24,3200]{1,0:T(8,128)(2,1)S(1)}, bf16[24,3200]{1,0:T(8,128)(2,1)S(1)}, u32[]{:S(2)}, u32[]{:S(2)}) collective-permute-start(bf16[24,3200]{1,0:T(8,128)(2,1)S(1)} %pad_maximum_fusion.3), channel_id=1, source_target_pairs={{0,16},{1,4},{2,18},{3,6},{4,1},{5,21},{6,3},{7,23},{8,24},{9,12},... | collective-permute-start | bytes 460808 | tf_op jit(solution)/shard_map/ppermute | solution.py:134
  9.2 7.3 %collective-permute-start.11 = (bf16[2,80,640]{2,1,0:T(8,128)(2,1)S(1)}, bf16[2,80,640]{2,1,0:T(8,128)(2,1)S(1)}, u32[]{:S(2)}, u32[]{:S(2)}) collective-permute-start(bf16[2,80,640]{2,1,0:T(8,128)(2,1)S(1)} %pad_maximum_fusion.2.refs_8_), channel_id=1, source_target_pairs={{0,4},{1,5},{2,6},{3,7},{4,0},{5,1},{6,2},{7,3},{8,12},{9,13},{10,... | collective-permute-start | bytes 614408 | tf_op jit(solution)/shard_map/ppermute | solution.py:134
  9.3 6.8 %collective-permute-start.6 = (bf16[80,640]{1,0:T(8,128)(2,1)S(1)}, bf16[80,640]{1,0:T(8,128)(2,1)S(1)}, u32[]{:S(2)}, u32[]{:S(2)}) collective-permute-start(bf16[80,640]{1,0:T(8,128)(2,1)S(1)} %collective-permute-done.1), channel_id=1, source_target_pairs={{0,8},{1,9},{2,10},{3,11},{4,12},{5,13},{6,14},{7,15},{8,0},{9,1},... | collective-permute-start | bytes 307208 | tf_op jit(solution)/shard_map/ppermute | solution.py:134
  12.5 8.0 %collective-permute-start.2 = (bf16[24,3200]{1,0:T(8,128)(2,1)S(1)}, bf16[24,3200]{1,0:T(8,128)(2,1)S(1)}, u32[]{:S(2)}, u32[]{:S(2)}) collective-permute-start(bf16[24,3200]{1,0:T(8,128)(2,1)S(1)} %broadcast_select_fusion.1.refs_0_), channel_id=1, source_target_pairs={{0,8},{1,17},{2,10},{3,19},{4,20},{5,13},{6,22},{7,15},{8,0},{9,25... | collective-permute-start | bytes 460808 | tf_op jit(solution)/shard_map/ppermute | solution.py:134
  16.1 6.9 %collective-permute-start.3 = (bf16[24,3200]{1,0:T(8,128)(2,1)S(1)}, bf16[24,3200]{1,0:T(8,128)(2,1)S(1)}, u32[]{:S(2)}, u32[]{:S(2)}) collective-permute-start(bf16[24,3200]{1,0:T(8,128)(2,1)S(1)} %collective-permute-done), channel_id=1, source_target_pairs={{0,8},{1,9},{2,10},{3,11},{4,12},{5,13},{6,14},{7,15},{8,0},{9,1},... | collective-permute-start | bytes 460808 | tf_op jit(solution)/shard_map/ppermute | solution.py:134
  16.2 9.7 %collective-permute-start.7 = (bf16[2,80,640]{2,1,0:T(8,128)(2,1)S(1)}, bf16[2,80,640]{2,1,0:T(8,128)(2,1)S(1)}, u32[]{:S(2)}, u32[]{:S(2)}) collective-permute-start(bf16[2,80,640]{2,1,0:T(8,128)(2,1)S(1)} %pad_maximum_fusion.1), channel_id=1, source_target_pairs={{0,4},{1,5},{2,6},{3,7},{4,0},{5,1},{6,2},{7,3},{8,12},{9,13},{10,... | collective-permute-start | bytes 614408 | tf_op jit(solution)/shard_map/ppermute | solution.py:134
  16.5 11.6 %collective-permute-start.12 = (bf16[6,80,640]{2,1,0:T(8,128)(2,1)S(1)}, bf16[6,80,640]{2,1,0:T(8,128)(2,1)S(1)}, u32[]{:S(2)}, u32[]{:S(2)}) collective-permute-start(bf16[6,80,640]{2,1,0:T(8,128)(2,1)S(1)} %constant_dynamic-update-slice_fusion), channel_id=1, source_target_pairs={{0,1},{1,0},{2,3},{3,2},{4,5},{5,4},{6,7},{7,6},{8,9},{9,8},{10,11... | collective-permute-start | bytes 1843208 | tf_op jit(solution)/shard_map/ppermute | solution.py:134
  20.5 6.0 %collective-permute-start.4 = (bf16[24,3200]{1,0:T(8,128)(2,1)S(1)}, bf16[24,3200]{1,0:T(8,128)(2,1)S(1)}, u32[]{:S(2)}, u32[]{:S(2)}) collective-permute-start(bf16[24,3200]{1,0:T(8,128)(2,1)S(1)} %collective-permute-done.2.refs_1_), channel_id=1, source_target_pairs={{0,2},{1,9},{2,0},{3,11},{4,12},{5,7},{6,14},{7,5},{8,10},{9,1},{1... | collective-permute-start | bytes 460808 | tf_op jit(solution)/shard_map/ppermute | solution.py:134
  23.1 5.2 %collective-permute-start.9 = (bf16[24,3200]{1,0:T(8,128)(2,1)S(1)}, bf16[24,3200]{1,0:T(8,128)(2,1)S(1)}, u32[]{:S(2)}, u32[]{:S(2)}) collective-permute-start(bf16[24,3200]{1,0:T(8,128)(2,1)S(1)} %collective-permute-done.3.refs_2_), channel_id=1, source_target_pairs={{0,1},{1,0},{2,3},{3,2},{4,5},{5,4},{6,7},{7,6},{8,9},{9,8},{10,11... | collective-permute-start | bytes 460808 | tf_op jit(solution)/shard_map/ppermute | solution.py:134
  26.0 2.2 %collective-permute-start.8 = (bf16[2,24,3200]{2,1,0:T(8,128)(2,1)S(1)}, bf16[2,24,3200]{2,1,0:T(8,128)(2,1)S(1)}, u32[]{:S(2)}, u32[]{:S(2)}) collective-permute-start(bf16[2,24,3200]{2,1,0:T(8,128)(2,1)S(1)} %pad_maximum_fusion), channel_id=1, source_target_pairs={{0,1},{1,0},{2,3},{3,2},{4,5},{5,4},{6,7},{7,6},{8,9},{9,8},{10,11... | collective-permute-start | bytes 921608 | tf_op jit(solution)/shard_map/ppermute | solution.py:134
  26.0 2.2 %collective-permute-start.13 = (bf16[2,80,640]{2,1,0:T(8,128)(2,1)S(1)}, bf16[2,80,640]{2,1,0:T(8,128)(2,1)S(1)}, u32[]{:S(2)}, u32[]{:S(2)}) collective-permute-start(bf16[2,80,640]{2,1,0:T(8,128)(2,1)S(1)} %collective-permute-done.7.refs_12_), channel_id=1, source_target_pairs={{0,1},{1,0},{2,3},{3,2},{4,5},{5,4},{6,7},{7,6},{8,9},{9,8},{10,11... | collective-permute-start | bytes 614408 | tf_op jit(solution)/shard_map/ppermute | solution.py:134
  26.6 2.6 %collective-permute-start.10 = (bf16[24,3200]{1,0:T(8,128)(2,1)S(1)}, bf16[24,3200]{1,0:T(8,128)(2,1)S(1)}, u32[]{:S(2)}, u32[]{:S(2)}) collective-permute-start(bf16[24,3200]{1,0:T(8,128)(2,1)S(1)} %broadcast_select_fusion.refs_3_), channel_id=1, source_target_pairs={{0,1},{1,0},{2,3},{3,2},{4,5},{5,4},{6,7},{7,6},{8,9},{9,8},{10,11... | collective-permute-start | bytes 460808 | tf_op jit(solution)/shard_map/ppermute | solution.py:134
  31.7 4.6 %collective-permute-start.14 = (bf16[96,640]{1,0:T(8,128)(2,1)S(1)}, bf16[96,640]{1,0:T(8,128)(2,1)S(1)}, u32[]{:S(2)}, u32[]{:S(2)}) collective-permute-start(bf16[96,640]{1,0:T(8,128)(2,1)S(1)} %get-tuple-element.21), channel_id=1, source_target_pairs={{0,2},{1,3},{2,0},{3,1},{4,6},{5,7},{6,4},{7,5},{8,10},{9,11},{10,... | collective-permute-start | bytes 368648 | tf_op jit(solution)/shard_map/ppermute | solution.py:134
  33.0 4.2 %collective-permute-start.15 = (bf16[96,640]{1,0:T(8,128)(2,1)S(1)}, bf16[96,640]{1,0:T(8,128)(2,1)S(1)}, u32[]{:S(2)}, u32[]{:S(2)}) collective-permute-start(bf16[96,640]{1,0:T(8,128)(2,1)S(1)} %get-tuple-element.22), channel_id=1, source_target_pairs={{0,4},{1,5},{2,6},{3,7},{4,0},{5,1},{6,2},{7,3},{8,12},{9,13},{10,... | collective-permute-start | bytes 368648 | tf_op jit(solution)/shard_map/ppermute | solution.py:134
  33.0 6.8 %collective-permute-start.16 = (bf16[96,640]{1,0:T(8,128)(2,1)S(1)}, bf16[96,640]{1,0:T(8,128)(2,1)S(1)}, u32[]{:S(2)}, u32[]{:S(2)}) collective-permute-start(bf16[96,640]{1,0:T(8,128)(2,1)S(1)} %get-tuple-element.22), channel_id=1, source_target_pairs={{0,6},{1,7},{2,4},{3,5},{4,2},{5,3},{6,0},{7,1},{8,14},{9,15},{10,... | collective-permute-start | bytes 368648 | tf_op jit(solution)/shard_map/ppermute | solution.py:134
  36.3 6.0 %collective-permute-start.17 = (bf16[2,24,1280]{2,1,0:T(8,128)(2,1)S(1)}, bf16[2,24,1280]{2,1,0:T(8,128)(2,1)S(1)}, u32[]{:S(2)}, u32[]{:S(2)}) collective-permute-start(bf16[2,24,1280]{2,1,0:T(8,128)(2,1)S(1)} %get-tuple-element.24), channel_id=1, source_target_pairs={{0,8},{1,4},{2,10},{3,6},{4,1},{5,13},{6,3},{7,15},{8,0},{9,12},{1... | collective-permute-start | bytes 368648 | tf_op jit(solution)/shard_map/ppermute | solution.py:134
  39.9 3.0 %collective-permute-start.18 = (f32[80,640]{1,0:T(8,128)S(1)}, f32[80,640]{1,0:T(8,128)S(1)}, u32[]{:S(2)}, u32[]{:S(2)}) collective-permute-start(f32[80,640]{1,0:T(8,128)S(1)} %slice.57), channel_id=1, source_target_pairs={{0,1},{1,0},{2,3},{3,2},{4,5},{5,4},{6,7},{7,6},{8,9},{9,8},{10,11... | collective-permute-start | bytes 614408 | tf_op jit(solution)/shard_map/ppermute | solution.py:134

commit v5 on v4

--- a/solution.py
+++ b/solution.py
@@ -124,6 +124,10 @@
     return (z * 2 + x) * 4 + y * 2 + core
 
 
+def after(done, *values):
+    return lax.optimization_barrier((values, done))[0]
+
+
 def own_place():
     blk, rep = lax.axis_index("blk"), lax.axis_index("rep")
     return blk // 2, blk % 2, rep // 2, rep % 2
@@ -177,7 +181,7 @@
 
 
 def fourth_move(value):
-    return moved(value, lambda z, x, y, core: (z, x, 1 - y, core) if is_ahead(x, core) else (z ^ 1, x, y, core))
+    return moved(value, lambda z, x, y, core: (z, 1 - x, y, 1 - core) if is_ahead(x, core) else (z ^ 1, x, y, core))
 
 
 def trade_back(value):
@@ -207,7 +211,7 @@
     count = 2 * len(PROJ_STEPS)
     rows_here, rows_there, projs = refs[:4], refs[4:8], refs[8 : 8 + count]
     keep, send, grads = refs[8 + count : 11 + count]
-    image, text, hidden, hidden_t, norms, proj, coefs, grad_all, grad_cols, share = refs[11 + count :]
+    image, text, hidden, hidden_t, norms, proj, coefs, grad_all, share = refs[11 + count :]
     z, x, y, core = own_place()
     rows, depth = rows_here[0].shape[0], proj.shape[1] // 8
     width = image.shape[1]
@@ -233,12 +237,10 @@
         )
     hidden_t[...] = hidden[...].T
     text_inv = inverse_norm(text[...])
-    text[...] = text[...] * text_inv
-    text_short = text[...].astype(BF16)
+    text_short = (text[...] * text_inv).astype(BF16)
     image_inv = inverse_norm(image[...])
     norms[...] = jnp.broadcast_to(image_inv, norms.shape)
-    image[...] = image[...] * image_inv
-    image_short = image[...].astype(BF16)
+    image_short = (image[...] * image_inv).astype(BF16)
     scale = jnp.exp(jnp.full((1, 1), log_scale[0], F32))
     logits = scale * lax.dot_general(
         image_short, text_short, ROWWISE, preferred_element_type=F32
@@ -263,25 +265,23 @@
     grad_unit = scale * jnp.dot(
         coefs[pl.ds(own, rows), :].astype(BF16), text_short, preferred_element_type=F32
     )
-    unit = image[pl.ds(own, rows), :]
+    inverse = norms[pl.ds(own, rows), :1]
+    unit = image[pl.ds(own, rows), :] * inverse
     grads[0] = (
-        (grad_unit - unit * jnp.sum(unit * grad_unit, axis=-1, keepdims=True))
-        * norms[pl.ds(own, rows), :1]
+        (grad_unit - unit * jnp.sum(unit * grad_unit, axis=-1, keepdims=True)) * inverse
     ).astype(BF16)
     grad_unit = scale * jnp.dot(coef.T.astype(BF16), image_short, preferred_element_type=F32)
-    unit = text[...]
+    unit = text[...] * text_inv
     grad_all[...] = (
         grad_unit - unit * jnp.sum(unit * grad_unit, axis=-1, keepdims=True)
     ) * text_inv
     grads[1] = grad_all[pl.ds(own, rows), :].astype(BF16)
-    for side in range(2):
-        grad_cols[side] = grad_all[:, side * half : (side + 1) * half].astype(BF16)
     share[...] = jnp.dot(
         hidden_t[pl.ds(pl.multiple_of(z * 2 * depth, 8), 2 * depth), :].astype(BF16),
-        grad_cols[core],
+        grad_all[:, pl.ds(pl.multiple_of(core * half, 128), half)].astype(BF16),
         preferred_element_type=F32,
     )
-    totals = lanes_of(in_parts(loss) + in_parts(scale_grad), 2 * y + x, (16, half))
+    totals = lanes_of(in_parts(loss) + in_parts(scale_grad), 2 * y + x, (8, half))
     keep[:depth, :] = share[pl.ds(pl.multiple_of(x * depth, 8), depth), :].astype(BF16)
     keep[depth:, :] = totals.astype(BF16)
     send[:depth, :] = share[pl.ds(pl.multiple_of((1 - x) * depth, 8), depth), :].astype(BF16)
@@ -295,40 +295,34 @@
     factor = 1.0 / (2.0 * total_rows * lax.axis_size("rep"))
     z, x, y, core = own_place()
     ahead = is_ahead(x, core)
-    own = lax.dynamic_slice_in_dim(proj_window, core * half, half, 1)
-    own, = lax.optimization_barrier((own,))
+    (own,) = lax.optimization_barrier((lax.dynamic_slice_in_dim(proj_window, core * half, half, 1),))
     samples = jnp.concatenate([image_embed[0], text_rest[0], text_hidden[0]], axis=1)
     far = z_far(own)
     even = jnp.stack([own, far])
     first = first_move(samples)
     own_rows = jnp.where(ahead, samples, first)
     near = z_near(own)[None]
-    (tied_second_0,), _ = lax.optimization_barrier(((own_rows,), far))
-    second = second_move(tied_second_0)
+    second = second_move(*after(far, own_rows))
     last = z_near(far)[None]
-    even_x = x_peer(even)
+    even_x = x_peer(*after(near, even))
     third = z_near(first)
-    (tied_odd_x_0, tied_odd_x_1,), _ = lax.optimization_barrier(((near, last,), first))
-    odd_x = x_peer(jnp.concatenate([tied_odd_x_0, tied_odd_x_1]))
-    fourth = fourth_move(second)
-    fourth_rows = jnp.where(ahead, first, fourth)
-    (tied_cg0_0, tied_cg0_1,), _ = lax.optimization_barrier(((own_rows, second,), odd_x))
-    cg0 = core_peer(jnp.stack([tied_cg0_0, tied_cg0_1]))
-    cg1 = core_peer(third)
-    cg2 = core_peer(fourth_rows)
-    cq0 = core_peer(jnp.concatenate([even, near, last, even_x]))
-    (tied_cq1_0,), _ = lax.optimization_barrier(((odd_x,), third))
-    cq1 = core_peer(tied_cq1_0)
-    rows_here = (own_rows, second, third, fourth_rows)
-    rows_there = (cg0[0], cg0[1], cg1, cg2)
-    proj_here = (even, near, last, even_x, odd_x)
-    proj_there = (cq0[0:2], cq0[2:3], cq0[3:4], cq0[4:6], cq1)
+    odd_x = x_peer(jnp.concatenate([near, last]))
+    fourth = jnp.where(ahead, first, fourth_move(second))
+    there_01 = core_peer(jnp.stack(after(odd_x, own_rows, second)))
+    there_third = core_peer(third)
+    there_fourth = core_peer(fourth)
+    proj_early = core_peer(jnp.concatenate([even, near, last, even_x]))
+    proj_late = core_peer(*after(third, odd_x))
+    rows_here = own_rows, second, third, fourth
+    rows_there = there_01[0], there_01[1], there_third, there_fourth
+    proj_here = even, near, last, even_x, odd_x
+    proj_there = proj_early[0:2], proj_early[2:3], proj_early[3:4], proj_early[4:6], proj_late
     arrived = rows_here + rows_there + proj_here + proj_there
     keep, send, grads = pl.pallas_call(
         functools.partial(group_kernel, factor),
         out_shape=(
-            jax.ShapeDtypeStruct((depth + 16, half), BF16),
-            jax.ShapeDtypeStruct((depth + 16, half), BF16),
+            jax.ShapeDtypeStruct((depth + 8, half), BF16),
+            jax.ShapeDtypeStruct((depth + 8, half), BF16),
             jax.ShapeDtypeStruct((2, rows, width), BF16),
         ),
         in_specs=[IN_SMEM] + [IN_VMEM] * len(arrived),
@@ -342,7 +336,6 @@
             pltpu.VMEM((2, total_depth, half), BF16),
             pltpu.VMEM((total_rows, total_rows), F32),
             pltpu.VMEM((total_rows, width), F32),
-            pltpu.VMEM((2, total_rows, half), BF16),
             pltpu.VMEM((2 * depth, half), F32),
         ],
         compiler_params=pltpu.CompilerParams(vmem_limit_bytes=40 * 2**20),
@@ -352,9 +345,7 @@
         *arrived
     )
     over_y, over_x, over_both = y_peer(keep), x_peer(send), xy_peer(send)
-    (tied_grads,), _ = lax.optimization_barrier(((grads,), over_y))
-    grads = jnp.where(ahead, grads, trade_back(tied_grads))
-    image_out, text_out = grads[0][None], grads[1][None]
+    grads = jnp.where(ahead, grads, trade_back(*after(over_y, grads)))
     share = (keep.astype(F32) + over_y.astype(F32)) + (over_x.astype(F32) + over_both.astype(F32))
     ours = share[:depth]
     theirs = core_peer(ours)
@@ -364,7 +355,7 @@
         jnp.concatenate([theirs, ours], axis=1),
     )
     totals = jnp.sum(share[depth, :24].reshape(2, 12), axis=1)
-    return totals[0:1], totals[1:2], image_out, text_out, grad_proj
+    return totals[0:1], totals[1:2], grads[0][None], grads[1][None], grad_proj
 
 
 def solution(mesh):

time: 44 us -> 43.1 us (0.980)
  waiting for transfers between devices: 9.9 us -> 9.05 us
    ppermute x19, waiting for transfers between devices: 9.9 us -> 9.05 us  [moved(): lax.ppermute(value, ('blk', 'rep'), [(number(*place), number(*to(*place))...]
where the time goes in v5:
time: 43.1 us; the launch traced here: 42.7 us
  starting transfers between devices  26 us (60%)
  waiting for transfers between devices  9.05 us (21%)
  Pallas kernels  2.54 us (6%)
  local copies, waits for them, and re-layouts  2.45 us (6%)
  between operations  1.48 us (3%)
  other arithmetic  1.14 us (3%)
    ppermute x19, starting transfers between devices, moved(): lax.ppermute(value, ('blk', 'rep'), [(number(*place), number(*to(*place))...  26 us
    ppermute x19, waiting for transfers between devices, moved(): lax.ppermute(value, ('blk', 'rep'), [(number(*place), number(*to(*place))...  9.05 us
    pallas_call x1, Pallas kernels, on_device_whole_group(): pl.pallas_call(functools.partial(group_kernel, factor), out_shape=(jax.Sh...  2.54 us
    slice x2, local copies, waits for them, and re-layouts, on_device_whole_group(): return (totals[0:1], totals[1:2], grads[0][None], grads[1][None], grad_proj)  1.24 us
    unnamed x12, local copies, waits for them, and re-layouts  0.98 us
  transfers between devices with their start and end apart: 19, of which 6 were waited for; matrix products, arithmetic and copies ran while one was open for 4% of the time, Pallas kernels for 0%

profile of v5, /device:TPU:1, one launch (start us, length us, event | category | flops | bytes accessed | tf_op | source)
XLA Modules:
  0.0 42.7 jit_solution(18037218643151878343)
XLA Ops:
  0.6 0.0 copy-start
  0.7 0.9 %copy-done = bf16[80,1280]{1,0:T(8,128)(2,1)S(1)} copy-done((bf16[80,1280]{1,0:T(8,128)(2,1)S(1)}, bf16[80,1280]{1,0:T(8,128)(2,1)}, u32[]{:S(2)}) %copy-start) | copy-done | bytes 204824
  1.6 0.0 copy-start.1
  1.6 0.0 copy-start.2
  1.6 0.0 copy-start.3
  1.6 3.2 %collective-permute-start.1 = (bf16[80,640]{1,0:T(8,128)(2,1)S(1)}, bf16[80,640]{1,0:T(8,128)(2,1)S(1)}, u32[]{:S(2)}, u32[]{:S(2)}) collective-permute-start(bf16[80,640]{1,0:T(8,128)(2,1)S(1)} %constant_dynamic-slice_fusion), channel_id=1, source_target_pairs={{0,16},{1,17},{2,18},{3,19},{4,20},{5,21},{6,22},{7,23},{8,24},{9,... | collective-permute-start | bytes 307208 | tf_op jit(solution)/shard_map/ppermute | solution.py:138
  4.8 1.3 %collective-permute-start.5 = (bf16[80,640]{1,0:T(8,128)(2,1)S(1)}, bf16[80,640]{1,0:T(8,128)(2,1)S(1)}, u32[]{:S(2)}, u32[]{:S(2)}) collective-permute-start(bf16[80,640]{1,0:T(8,128)(2,1)S(1)} %constant_dynamic-slice_fusion), channel_id=1, source_target_pairs={{0,8},{1,9},{2,10},{3,11},{4,12},{5,13},{6,14},{7,15},{8,0},{9,1},... | collective-permute-start | bytes 307208 | tf_op jit(solution)/shard_map/ppermute | solution.py:138
  6.1 0.0 copy-done.1
  6.1 0.0 copy-done.2
  6.1 0.0 copy-done.3
  6.1 2.4 %collective-permute-start = (bf16[24,3200]{1,0:T(8,128)(2,1)S(1)}, bf16[24,3200]{1,0:T(8,128)(2,1)S(1)}, u32[]{:S(2)}, u32[]{:S(2)}) collective-permute-start(bf16[24,3200]{1,0:T(8,128)(2,1)S(1)} %pad_maximum_fusion.3), channel_id=1, source_target_pairs={{0,16},{1,4},{2,18},{3,6},{4,1},{5,21},{6,3},{7,23},{8,24},{9,12},... | collective-permute-start | bytes 460808 | tf_op jit(solution)/shard_map/ppermute | solution.py:138
  9.2 0.0 collective-permute-done.1
  9.2 0.0 collective-permute-done.5
  9.2 0.8 %collective-permute-start.11 = (bf16[2,80,640]{2,1,0:T(8,128)(2,1)S(1)}, bf16[2,80,640]{2,1,0:T(8,128)(2,1)S(1)}, u32[]{:S(2)}, u32[]{:S(2)}) collective-permute-start(bf16[2,80,640]{2,1,0:T(8,128)(2,1)S(1)} %pad_maximum_fusion.2.refs_8_), channel_id=1, source_target_pairs={{0,4},{1,5},{2,6},{3,7},{4,0},{5,1},{6,2},{7,3},{8,12},{9,13},{10,... | collective-permute-start | bytes 614408 | tf_op jit(solution)/shard_map/ppermute | solution.py:138
  10.1 2.3 %collective-permute-start.6 = (bf16[80,640]{1,0:T(8,128)(2,1)S(1)}, bf16[80,640]{1,0:T(8,128)(2,1)S(1)}, u32[]{:S(2)}, u32[]{:S(2)}) collective-permute-start(bf16[80,640]{1,0:T(8,128)(2,1)S(1)} %collective-permute-done.1), channel_id=1, source_target_pairs={{0,8},{1,9},{2,10},{3,11},{4,12},{5,13},{6,14},{7,15},{8,0},{9,1},... | collective-permute-start | bytes 307208 | tf_op jit(solution)/shard_map/ppermute | solution.py:138
  12.4 0.0 collective-permute-done
  12.5 3.7 %collective-permute-start.2 = (bf16[24,3200]{1,0:T(8,128)(2,1)S(1)}, bf16[24,3200]{1,0:T(8,128)(2,1)S(1)}, u32[]{:S(2)}, u32[]{:S(2)}) collective-permute-start(bf16[24,3200]{1,0:T(8,128)(2,1)S(1)} %broadcast_select_fusion.1.refs_0_), channel_id=1, source_target_pairs={{0,8},{1,17},{2,10},{3,19},{4,20},{5,13},{6,22},{7,15},{8,0},{9,25... | collective-permute-start | bytes 460808 | tf_op jit(solution)/shard_map/ppermute | solution.py:138
  16.1 0.0 collective-permute-start.3
  16.2 0.0 collective-permute-done.6
  16.2 0.3 collective-permute-start.7
  16.5 0.0 collective-permute-done.11.refs_11_
  16.5 2.2 %collective-permute-start.12 = (bf16[6,80,640]{2,1,0:T(8,128)(2,1)S(1)}, bf16[6,80,640]{2,1,0:T(8,128)(2,1)S(1)}, u32[]{:S(2)}, u32[]{:S(2)}) collective-permute-start(bf16[6,80,640]{2,1,0:T(8,128)(2,1)S(1)} %constant_dynamic-update-slice_fusion), channel_id=1, source_target_pairs={{0,1},{1,0},{2,3},{3,2},{4,5},{5,4},{6,7},{7,6},{8,9},{9,8},{10,11... | collective-permute-start | bytes 1843208 | tf_op jit(solution)/shard_map/ppermute | solution.py:138
  18.7 1.8 %collective-permute-done.2.refs_1_ = bf16[24,3200]{1,0:T(8,128)(2,1)S(1)} collective-permute-done((bf16[24,3200]{1,0:T(8,128)(2,1)S(1)}, bf16[24,3200]{1,0:T(8,128)(2,1)S(1)}, u32[]{:S(2)}, u32[]{:S(2)}) %collective-permute-start.2) | collective-permute-done | bytes 153632 | tf_op jit(solution)/shard_map/ppermute | solution.py:138
  20.5 0.0 collective-permute-start.4
  20.5 2.7 %collective-permute-done.3.refs_2_ = bf16[24,3200]{1,0:T(8,128)(2,1)S(1)} collective-permute-done((bf16[24,3200]{1,0:T(8,128)(2,1)S(1)}, bf16[24,3200]{1,0:T(8,128)(2,1)S(1)}, u32[]{:S(2)}, u32[]{:S(2)}) %collective-permute-start.3) | collective-permute-done | bytes 153632 | tf_op jit(solution)/shard_map/ppermute | solution.py:138
  23.2 2.7 %collective-permute-start.9 = (bf16[24,3200]{1,0:T(8,128)(2,1)S(1)}, bf16[24,3200]{1,0:T(8,128)(2,1)S(1)}, u32[]{:S(2)}, u32[]{:S(2)}) collective-permute-start(bf16[24,3200]{1,0:T(8,128)(2,1)S(1)} %collective-permute-done.3.refs_2_), channel_id=1, source_target_pairs={{0,1},{1,0},{2,3},{3,2},{4,5},{5,4},{6,7},{7,6},{8,9},{9,8},{10,11... | collective-permute-start | bytes 460808 | tf_op jit(solution)/shard_map/ppermute | solution.py:138
  25.9 0.0 collective-permute-done.7.refs_12_
  25.9 0.1 collective-permute-start.8
  26.0 0.5 %collective-permute-start.13 = (bf16[2,80,640]{2,1,0:T(8,128)(2,1)S(1)}, bf16[2,80,640]{2,1,0:T(8,128)(2,1)S(1)}, u32[]{:S(2)}, u32[]{:S(2)}) collective-permute-start(bf16[2,80,640]{2,1,0:T(8,128)(2,1)S(1)} %collective-permute-done.7.refs_12_), channel_id=1, source_target_pairs={{0,1},{1,0},{2,3},{3,2},{4,5},{5,4},{6,7},{7,6},{8,9},{9,8},{10,11... | collective-permute-start | bytes 614408 | tf_op jit(solution)/shard_map/ppermute | solution.py:138
  26.5 0.0 collective-permute-done.4
  26.5 1.0 %collective-permute-start.10 = (bf16[24,3200]{1,0:T(8,128)(2,1)S(1)}, bf16[24,3200]{1,0:T(8,128)(2,1)S(1)}, u32[]{:S(2)}, u32[]{:S(2)}) collective-permute-start(bf16[24,3200]{1,0:T(8,128)(2,1)S(1)} %broadcast_select_fusion.refs_3_), channel_id=1, source_target_pairs={{0,1},{1,0},{2,3},{3,2},{4,5},{5,4},{6,7},{7,6},{8,9},{9,8},{10,11... | collective-permute-start | bytes 460808 | tf_op jit(solution)/shard_map/ppermute | solution.py:138
  27.6 0.0 collective-permute-done.8
  27.6 0.0 collective-permute-done.12
  27.7 0.0 collective-permute-done.9.refs_6_
  27.7 0.2 collective-permute-done.13.refs_17_
  27.9 0.7 %collective-permute-done.10.refs_7_ = bf16[24,3200]{1,0:T(8,128)(2,1)S(1)} collective-permute-done((bf16[24,3200]{1,0:T(8,128)(2,1)S(1)}, bf16[24,3200]{1,0:T(8,128)(2,1)S(1)}, u32[]{:S(2)}, u32[]{:S(2)}) %collective-permute-start.10) | collective-permute-done | bytes 153632 | tf_op jit(solution)/shard_map/ppermute | solution.py:138
  28.6 2.5 %group_kernel.1 = (bf16[88,640]{1,0:T(8,128)(2,1)S(1)}, bf16[88,640]{1,0:T(8,128)(2,1)S(1)}, bf16[2,24,1280]{2,1,0:T(8,128)(2,1)S(1)}) custom-call(f32[1]{0:T(128)S(6)} %copy.14.log_scale, bf16[24,3200]{1,0:T(8,128)(2,1)S(1)} %broadcast_select_fusion.1.refs_0_, bf16[24,3200]{1,0:T(8,128)(2,1)S(1)} %collective-permute-done.2.refs_1_, ...), custom_call_target="tpu_custom_call" | custom-call | tf_op jit(solution)/shard_map/group_kernel/pallas_call | solution.py:321
  31.1 1.3 %collective-permute-start.14 = (bf16[88,640]{1,0:T(8,128)(2,1)S(1)}, bf16[88,640]{1,0:T(8,128)(2,1)S(1)}, u32[]{:S(2)}, u32[]{:S(2)}) collective-permute-start(bf16[88,640]{1,0:T(8,128)(2,1)S(1)} %get-tuple-element.19), channel_id=1, source_target_pairs={{0,2},{1,3},{2,0},{3,1},{4,6},{5,7},{6,4},{7,5},{8,10},{9,11},{10,... | collective-permute-start | bytes 337928 | tf_op jit(solution)/shard_map/ppermute | solution.py:138
  32.4 0.2 collective-permute-start.15
  32.7 1.2 %collective-permute-start.16 = (bf16[88,640]{1,0:T(8,128)(2,1)S(1)}, bf16[88,640]{1,0:T(8,128)(2,1)S(1)}, u32[]{:S(2)}, u32[]{:S(2)}) collective-permute-start(bf16[88,640]{1,0:T(8,128)(2,1)S(1)} %get-tuple-element.20), channel_id=1, source_target_pairs={{0,6},{1,7},{2,4},{3,5},{4,2},{5,3},{6,0},{7,1},{8,14},{9,15},{10,... | collective-permute-start | bytes 337928 | tf_op jit(solution)/shard_map/ppermute | solution.py:138
  33.8 1.7 %collective-permute-done.14 = bf16[88,640]{1,0:T(8,128)(2,1)S(1)} collective-permute-done((bf16[88,640]{1,0:T(8,128)(2,1)S(1)}, bf16[88,640]{1,0:T(8,128)(2,1)S(1)}, u32[]{:S(2)}, u32[]{:S(2)}) %collective-permute-start.14) | collective-permute-done | bytes 112672 | tf_op jit(solution)/shard_map/ppermute | solution.py:138
  35.5 1.3 %collective-permute-start.17 = (bf16[2,24,1280]{2,1,0:T(8,128)(2,1)S(1)}, bf16[2,24,1280]{2,1,0:T(8,128)(2,1)S(1)}, u32[]{:S(2)}, u32[]{:S(2)}) collective-permute-start(bf16[2,24,1280]{2,1,0:T(8,128)(2,1)S(1)} %get-tuple-element.22), channel_id=1, source_target_pairs={{0,8},{1,4},{2,10},{3,6},{4,1},{5,13},{6,3},{7,15},{8,0},{9,12},{1... | collective-permute-start | bytes 368648 | tf_op jit(solution)/shard_map/ppermute | solution.py:138
  36.8 0.0 collective-permute-done.15
  36.8 2.0 %collective-permute-done.16 = bf16[88,640]{1,0:T(8,128)(2,1)S(1)} collective-permute-done((bf16[88,640]{1,0:T(8,128)(2,1)S(1)}, bf16[88,640]{1,0:T(8,128)(2,1)S(1)}, u32[]{:S(2)}, u32[]{:S(2)}) %collective-permute-start.16) | collective-permute-done | bytes 112672 | tf_op jit(solution)/shard_map/ppermute | solution.py:138
  38.8 0.1 add_add_fusion
  38.9 1.6 %collective-permute-start.18 = (f32[80,640]{1,0:T(8,128)S(1)}, f32[80,640]{1,0:T(8,128)S(1)}, u32[]{:S(2)}, u32[]{:S(2)}) collective-permute-start(f32[80,640]{1,0:T(8,128)S(1)} %slice.57), channel_id=1, source_target_pairs={{0,1},{1,0},{2,3},{3,2},{4,5},{5,4},{6,7},{7,6},{8,9},{9,8},{10,11... | collective-permute-start | bytes 614408 | tf_op jit(solution)/shard_map/ppermute | solution.py:138
  40.5 0.1 reshape_squeeze.3
  40.5 0.1 reduce_sum.9
  40.7 0.6 %fusion.3 = (f32[1]{0:T(128)}, f32[1]{0:T(128)}) fusion(f32[2]{0:T(128)S(1)} %reduce_sum.9), kind=kLoop, calls=%fused_computation.21 | loop fusion | bytes 16 | tf_op jit(solution)/shard_map/slice | solution.py:358
  41.3 0.0 collective-permute-done.17
  41.3 0.7 %fusion.2 = (bf16[1,24,1280]{2,1,0:T(8,128)(2,1)}, bf16[1,24,1280]{2,1,0:T(8,128)(2,1)}) fusion(bf16[2,24,1280]{2,1,0:T(8,128)(2,1)S(1)} %broadcast_select_fusion.2), kind=kLoop, calls=%fused_computation.20 | loop fusion | bytes 245760 | tf_op jit(solution)/shard_map/slice | solution.py:358
  41.9 0.0 collective-permute-done.18
  41.9 0.8 %maximum_select_fusion = f32[80,1280]{1,0:T(8,128)} fusion(f32[80,640]{1,0:T(8,128)S(1)} %collective-permute-done.18, f32[80,640]{1,0:T(8,128)S(1)} %slice.57, pred[]{:T(512)S(6)} %eq.10), kind=kLoop, calls=%fused_computation | loop fusion | flops 307200 | bytes 819201 | tf_op jit(solution)/shard_map/jit(_where)/select_n | solution.py:352
  (18 shorter events, 0.4 us)
Async XLA Ops:
  0.6 0.9 %copy-start = (bf16[80,1280]{1,0:T(8,128)(2,1)S(1)}, bf16[80,1280]{1,0:T(8,128)(2,1)}, u32[]{:S(2)}) copy-start(bf16[80,1280]{1,0:T(8,128)(2,1)} %param.8) | copy-start | bytes 614404
  1.6 4.5 %copy-start.1 = (bf16[1,24,1280]{2,1,0:T(8,128)(2,1)S(1)}, bf16[1,24,1280]{2,1,0:T(8,128)(2,1)}, u32[]{:S(2)}) copy-start(bf16[1,24,1280]{2,1,0:T(8,128)(2,1)} %param.7) | copy-start | bytes 184324
  1.6 4.5 %copy-start.2 = (bf16[1,24,1280]{2,1,0:T(8,128)(2,1)S(1)}, bf16[1,24,1280]{2,1,0:T(8,128)(2,1)}, u32[]{:S(2)}) copy-start(bf16[1,24,1280]{2,1,0:T(8,128)(2,1)} %param.5) | copy-start | bytes 184324
  1.6 4.5 %copy-start.3 = (bf16[1,24,640]{2,1,0:T(8,128)(2,1)S(1)}, bf16[1,24,640]{2,1,0:T(8,128)(2,1)}, u32[]{:S(2)}) copy-start(bf16[1,24,640]{2,1,0:T(8,128)(2,1)} %param.6) | copy-start | bytes 92164
  1.6 7.6 %collective-permute-start.1 = (bf16[80,640]{1,0:T(8,128)(2,1)S(1)}, bf16[80,640]{1,0:T(8,128)(2,1)S(1)}, u32[]{:S(2)}, u32[]{:S(2)}) collective-permute-start(bf16[80,640]{1,0:T(8,128)(2,1)S(1)} %constant_dynamic-slice_fusion), channel_id=1, source_target_pairs={{0,16},{1,17},{2,18},{3,19},{4,20},{5,21},{6,22},{7,23},{8,24},{9,... | collective-permute-start | bytes 307208 | tf_op jit(solution)/shard_map/ppermute | solution.py:138
  4.8 4.4 %collective-permute-start.5 = (bf16[80,640]{1,0:T(8,128)(2,1)S(1)}, bf16[80,640]{1,0:T(8,128)(2,1)S(1)}, u32[]{:S(2)}, u32[]{:S(2)}) collective-permute-start(bf16[80,640]{1,0:T(8,128)(2,1)S(1)} %constant_dynamic-slice_fusion), channel_id=1, source_target_pairs={{0,8},{1,9},{2,10},{3,11},{4,12},{5,13},{6,14},{7,15},{8,0},{9,1},... | collective-permute-start | bytes 307208 | tf_op jit(solution)/shard_map/ppermute | solution.py:138
  6.1 6.3 %collective-permute-start = (bf16[24,3200]{1,0:T(8,128)(2,1)S(1)}, bf16[24,3200]{1,0:T(8,128)(2,1)S(1)}, u32[]{:S(2)}, u32[]{:S(2)}) collective-permute-start(bf16[24,3200]{1,0:T(8,128)(2,1)S(1)} %pad_maximum_fusion.3), channel_id=1, source_target_pairs={{0,16},{1,4},{2,18},{3,6},{4,1},{5,21},{6,3},{7,23},{8,24},{9,12},... | collective-permute-start | bytes 460808 | tf_op jit(solution)/shard_map/ppermute | solution.py:138
  9.2 7.2 %collective-permute-start.11 = (bf16[2,80,640]{2,1,0:T(8,128)(2,1)S(1)}, bf16[2,80,640]{2,1,0:T(8,128)(2,1)S(1)}, u32[]{:S(2)}, u32[]{:S(2)}) collective-permute-start(bf16[2,80,640]{2,1,0:T(8,128)(2,1)S(1)} %pad_maximum_fusion.2.refs_8_), channel_id=1, source_target_pairs={{0,4},{1,5},{2,6},{3,7},{4,0},{5,1},{6,2},{7,3},{8,12},{9,13},{10,... | collective-permute-start | bytes 614408 | tf_op jit(solution)/shard_map/ppermute | solution.py:138
  10.1 6.1 %collective-permute-start.6 = (bf16[80,640]{1,0:T(8,128)(2,1)S(1)}, bf16[80,640]{1,0:T(8,128)(2,1)S(1)}, u32[]{:S(2)}, u32[]{:S(2)}) collective-permute-start(bf16[80,640]{1,0:T(8,128)(2,1)S(1)} %collective-permute-done.1), channel_id=1, source_target_pairs={{0,8},{1,9},{2,10},{3,11},{4,12},{5,13},{6,14},{7,15},{8,0},{9,1},... | collective-permute-start | bytes 307208 | tf_op jit(solution)/shard_map/ppermute | solution.py:138
  12.5 8.0 %collective-permute-start.2 = (bf16[24,3200]{1,0:T(8,128)(2,1)S(1)}, bf16[24,3200]{1,0:T(8,128)(2,1)S(1)}, u32[]{:S(2)}, u32[]{:S(2)}) collective-permute-start(bf16[24,3200]{1,0:T(8,128)(2,1)S(1)} %broadcast_select_fusion.1.refs_0_), channel_id=1, source_target_pairs={{0,8},{1,17},{2,10},{3,19},{4,20},{5,13},{6,22},{7,15},{8,0},{9,25... | collective-permute-start | bytes 460808 | tf_op jit(solution)/shard_map/ppermute | solution.py:138
  16.1 7.1 %collective-permute-start.3 = (bf16[24,3200]{1,0:T(8,128)(2,1)S(1)}, bf16[24,3200]{1,0:T(8,128)(2,1)S(1)}, u32[]{:S(2)}, u32[]{:S(2)}) collective-permute-start(bf16[24,3200]{1,0:T(8,128)(2,1)S(1)} %collective-permute-done), channel_id=1, source_target_pairs={{0,8},{1,9},{2,10},{3,11},{4,12},{5,13},{6,14},{7,15},{8,0},{9,1},... | collective-permute-start | bytes 460808 | tf_op jit(solution)/shard_map/ppermute | solution.py:138
  16.2 9.7 %collective-permute-start.7 = (bf16[2,80,640]{2,1,0:T(8,128)(2,1)S(1)}, bf16[2,80,640]{2,1,0:T(8,128)(2,1)S(1)}, u32[]{:S(2)}, u32[]{:S(2)}) collective-permute-start(bf16[2,80,640]{2,1,0:T(8,128)(2,1)S(1)} %pad_maximum_fusion.1), channel_id=1, source_target_pairs={{0,4},{1,5},{2,6},{3,7},{4,0},{5,1},{6,2},{7,3},{8,12},{9,13},{10,... | collective-permute-start | bytes 614408 | tf_op jit(solution)/shard_map/ppermute | solution.py:138
  16.5 11.1 %collective-permute-start.12 = (bf16[6,80,640]{2,1,0:T(8,128)(2,1)S(1)}, bf16[6,80,640]{2,1,0:T(8,128)(2,1)S(1)}, u32[]{:S(2)}, u32[]{:S(2)}) collective-permute-start(bf16[6,80,640]{2,1,0:T(8,128)(2,1)S(1)} %constant_dynamic-update-slice_fusion), channel_id=1, source_target_pairs={{0,1},{1,0},{2,3},{3,2},{4,5},{5,4},{6,7},{7,6},{8,9},{9,8},{10,11... | collective-permute-start | bytes 1843208 | tf_op jit(solution)/shard_map/ppermute | solution.py:138
  20.5 6.0 %collective-permute-start.4 = (bf16[24,3200]{1,0:T(8,128)(2,1)S(1)}, bf16[24,3200]{1,0:T(8,128)(2,1)S(1)}, u32[]{:S(2)}, u32[]{:S(2)}) collective-permute-start(bf16[24,3200]{1,0:T(8,128)(2,1)S(1)} %collective-permute-done.2.refs_1_), channel_id=1, source_target_pairs={{0,5},{1,9},{2,7},{3,11},{4,12},{5,0},{6,14},{7,2},{8,13},{9,1},{1... | collective-permute-start | bytes 460808 | tf_op jit(solution)/shard_map/ppermute | solution.py:138
  23.2 4.5 %collective-permute-start.9 = (bf16[24,3200]{1,0:T(8,128)(2,1)S(1)}, bf16[24,3200]{1,0:T(8,128)(2,1)S(1)}, u32[]{:S(2)}, u32[]{:S(2)}) collective-permute-start(bf16[24,3200]{1,0:T(8,128)(2,1)S(1)} %collective-permute-done.3.refs_2_), channel_id=1, source_target_pairs={{0,1},{1,0},{2,3},{3,2},{4,5},{5,4},{6,7},{7,6},{8,9},{9,8},{10,11... | collective-permute-start | bytes 460808 | tf_op jit(solution)/shard_map/ppermute | solution.py:138
  25.9 1.7 %collective-permute-start.8 = (bf16[2,24,3200]{2,1,0:T(8,128)(2,1)S(1)}, bf16[2,24,3200]{2,1,0:T(8,128)(2,1)S(1)}, u32[]{:S(2)}, u32[]{:S(2)}) collective-permute-start(bf16[2,24,3200]{2,1,0:T(8,128)(2,1)S(1)} %pad_maximum_fusion), channel_id=1, source_target_pairs={{0,1},{1,0},{2,3},{3,2},{4,5},{5,4},{6,7},{7,6},{8,9},{9,8},{10,11... | collective-permute-start | bytes 921608 | tf_op jit(solution)/shard_map/ppermute | solution.py:138
  26.0 1.9 %collective-permute-start.13 = (bf16[2,80,640]{2,1,0:T(8,128)(2,1)S(1)}, bf16[2,80,640]{2,1,0:T(8,128)(2,1)S(1)}, u32[]{:S(2)}, u32[]{:S(2)}) collective-permute-start(bf16[2,80,640]{2,1,0:T(8,128)(2,1)S(1)} %collective-permute-done.7.refs_12_), channel_id=1, source_target_pairs={{0,1},{1,0},{2,3},{3,2},{4,5},{5,4},{6,7},{7,6},{8,9},{9,8},{10,11... | collective-permute-start | bytes 614408 | tf_op jit(solution)/shard_map/ppermute | solution.py:138
  26.5 2.0 %collective-permute-start.10 = (bf16[24,3200]{1,0:T(8,128)(2,1)S(1)}, bf16[24,3200]{1,0:T(8,128)(2,1)S(1)}, u32[]{:S(2)}, u32[]{:S(2)}) collective-permute-start(bf16[24,3200]{1,0:T(8,128)(2,1)S(1)} %broadcast_select_fusion.refs_3_), channel_id=1, source_target_pairs={{0,1},{1,0},{2,3},{3,2},{4,5},{5,4},{6,7},{7,6},{8,9},{9,8},{10,11... | collective-permute-start | bytes 460808 | tf_op jit(solution)/shard_map/ppermute | solution.py:138
  31.1 4.4 %collective-permute-start.14 = (bf16[88,640]{1,0:T(8,128)(2,1)S(1)}, bf16[88,640]{1,0:T(8,128)(2,1)S(1)}, u32[]{:S(2)}, u32[]{:S(2)}) collective-permute-start(bf16[88,640]{1,0:T(8,128)(2,1)S(1)} %get-tuple-element.19), channel_id=1, source_target_pairs={{0,2},{1,3},{2,0},{3,1},{4,6},{5,7},{6,4},{7,5},{8,10},{9,11},{10,... | collective-permute-start | bytes 337928 | tf_op jit(solution)/shard_map/ppermute | solution.py:138
  32.4 4.4 %collective-permute-start.15 = (bf16[88,640]{1,0:T(8,128)(2,1)S(1)}, bf16[88,640]{1,0:T(8,128)(2,1)S(1)}, u32[]{:S(2)}, u32[]{:S(2)}) collective-permute-start(bf16[88,640]{1,0:T(8,128)(2,1)S(1)} %get-tuple-element.20), channel_id=1, source_target_pairs={{0,4},{1,5},{2,6},{3,7},{4,0},{5,1},{6,2},{7,3},{8,12},{9,13},{10,... | collective-permute-start | bytes 337928 | tf_op jit(solution)/shard_map/ppermute | solution.py:138
  32.7 6.1 %collective-permute-start.16 = (bf16[88,640]{1,0:T(8,128)(2,1)S(1)}, bf16[88,640]{1,0:T(8,128)(2,1)S(1)}, u32[]{:S(2)}, u32[]{:S(2)}) collective-permute-start(bf16[88,640]{1,0:T(8,128)(2,1)S(1)} %get-tuple-element.20), channel_id=1, source_target_pairs={{0,6},{1,7},{2,4},{3,5},{4,2},{5,3},{6,0},{7,1},{8,14},{9,15},{10,... | collective-permute-start | bytes 337928 | tf_op jit(solution)/shard_map/ppermute | solution.py:138
  35.5 5.7 %collective-permute-start.17 = (bf16[2,24,1280]{2,1,0:T(8,128)(2,1)S(1)}, bf16[2,24,1280]{2,1,0:T(8,128)(2,1)S(1)}, u32[]{:S(2)}, u32[]{:S(2)}) collective-permute-start(bf16[2,24,1280]{2,1,0:T(8,128)(2,1)S(1)} %get-tuple-element.22), channel_id=1, source_target_pairs={{0,8},{1,4},{2,10},{3,6},{4,1},{5,13},{6,3},{7,15},{8,0},{9,12},{1... | collective-permute-start | bytes 368648 | tf_op jit(solution)/shard_map/ppermute | solution.py:138
  38.9 3.0 %collective-permute-start.18 = (f32[80,640]{1,0:T(8,128)S(1)}, f32[80,640]{1,0:T(8,128)S(1)}, u32[]{:S(2)}, u32[]{:S(2)}) collective-permute-start(f32[80,640]{1,0:T(8,128)S(1)} %slice.57), channel_id=1, source_target_pairs={{0,1},{1,0},{2,3},{3,2},{4,5},{5,4},{6,7},{7,6},{8,9},{9,8},{10,11... | collective-permute-start | bytes 614408 | tf_op jit(solution)/shard_map/ppermute | solution.py:138

commit v6 on v5

--- a/solution.py
+++ b/solution.py
@@ -282,10 +282,9 @@
         preferred_element_type=F32,
     )
     totals = lanes_of(in_parts(loss) + in_parts(scale_grad), 2 * y + x, (8, half))
-    keep[:depth, :] = share[pl.ds(pl.multiple_of(x * depth, 8), depth), :].astype(BF16)
-    keep[depth:, :] = totals.astype(BF16)
-    send[:depth, :] = share[pl.ds(pl.multiple_of((1 - x) * depth, 8), depth), :].astype(BF16)
-    send[depth:, :] = totals.astype(BF16)
+    for part, at in ((keep, x), (send, 1 - x)):
+        rows_of = share[pl.ds(pl.multiple_of(at * depth, 8), depth), :]
+        part[...] = jnp.concatenate([rows_of, totals]).astype(BF16)
 
 
 def on_device_whole_group(image_embed, text_hidden, text_rest, proj_window, log_scale):
@@ -345,7 +344,7 @@
         *arrived
     )
     over_y, over_x, over_both = y_peer(keep), x_peer(send), xy_peer(send)
-    grads = jnp.where(ahead, grads, trade_back(*after(over_y, grads)))
+    grads = jnp.where(ahead, grads, trade_back(grads))
     share = (keep.astype(F32) + over_y.astype(F32)) + (over_x.astype(F32) + over_both.astype(F32))
     ours = share[:depth]
     theirs = core_peer(ours)

time: 43.1 us -> 42.9 us (level)
  transfers between devices with their start and end apart: 19 -> 19, of which waited for: 6 -> 7; matrix products, arithmetic and copies ran while one was open for 4% -> 4% of each run, Pallas kernels for 0% -> 0%
where the time goes in v6:
time: 42.9 us; the launch traced here: 42.7 us
  starting transfers between devices  26.1 us (61%)
  waiting for transfers between devices  9.03 us (21%)
  Pallas kernels  2.54 us (6%)
  local copies, waits for them, and re-layouts  2.45 us (6%)
  between operations  1.48 us (3%)
  other arithmetic  1.14 us (3%)
    ppermute x19, starting transfers between devices, moved(): lax.ppermute(value, ('blk', 'rep'), [(number(*place), number(*to(*place))...  26.1 us
    ppermute x19, waiting for transfers between devices, moved(): lax.ppermute(value, ('blk', 'rep'), [(number(*place), number(*to(*place))...  9.03 us
    pallas_call x1, Pallas kernels, on_device_whole_group(): pl.pallas_call(functools.partial(group_kernel, factor), out_shape=(jax.Sh...  2.54 us
    slice x2, local copies, waits for them, and re-layouts, on_device_whole_group(): return (totals[0:1], totals[1:2], grads[0][None], grads[1][None], grad_proj)  1.24 us
    unnamed x12, local copies, waits for them, and re-layouts  0.98 us
  transfers between devices with their start and end apart: 19, of which 7 were waited for; matrix products, arithmetic and copies ran while one was open for 4% of the time, Pallas kernels for 0%

profile of v6, /device:TPU:1, one launch (start us, length us, event | category | flops | bytes accessed | tf_op | source)
XLA Modules:
  0.0 42.7 jit_solution(13712854906349183672)
XLA Ops:
  0.6 0.0 copy-start
  0.7 0.9 %copy-done = bf16[80,1280]{1,0:T(8,128)(2,1)S(1)} copy-done((bf16[80,1280]{1,0:T(8,128)(2,1)S(1)}, bf16[80,1280]{1,0:T(8,128)(2,1)}, u32[]{:S(2)}) %copy-start) | copy-done | bytes 204824
  1.6 0.0 copy-start.1
  1.6 0.0 copy-start.2
  1.6 0.0 copy-start.3
  1.6 3.2 %collective-permute-start.1 = (bf16[80,640]{1,0:T(8,128)(2,1)S(1)}, bf16[80,640]{1,0:T(8,128)(2,1)S(1)}, u32[]{:S(2)}, u32[]{:S(2)}) collective-permute-start(bf16[80,640]{1,0:T(8,128)(2,1)S(1)} %constant_dynamic-slice_fusion), channel_id=1, source_target_pairs={{0,16},{1,17},{2,18},{3,19},{4,20},{5,21},{6,22},{7,23},{8,24},{9,... | collective-permute-start | bytes 307208 | tf_op jit(solution)/shard_map/ppermute | solution.py:138
  4.8 1.3 %collective-permute-start.5 = (bf16[80,640]{1,0:T(8,128)(2,1)S(1)}, bf16[80,640]{1,0:T(8,128)(2,1)S(1)}, u32[]{:S(2)}, u32[]{:S(2)}) collective-permute-start(bf16[80,640]{1,0:T(8,128)(2,1)S(1)} %constant_dynamic-slice_fusion), channel_id=1, source_target_pairs={{0,8},{1,9},{2,10},{3,11},{4,12},{5,13},{6,14},{7,15},{8,0},{9,1},... | collective-permute-start | bytes 307208 | tf_op jit(solution)/shard_map/ppermute | solution.py:138
  6.1 0.0 copy-done.1
  6.1 0.0 copy-done.2
  6.1 0.0 copy-done.3
  6.1 2.4 %collective-permute-start = (bf16[24,3200]{1,0:T(8,128)(2,1)S(1)}, bf16[24,3200]{1,0:T(8,128)(2,1)S(1)}, u32[]{:S(2)}, u32[]{:S(2)}) collective-permute-start(bf16[24,3200]{1,0:T(8,128)(2,1)S(1)} %pad_maximum_fusion.3), channel_id=1, source_target_pairs={{0,16},{1,4},{2,18},{3,6},{4,1},{5,21},{6,3},{7,23},{8,24},{9,12},... | collective-permute-start | bytes 460808 | tf_op jit(solution)/shard_map/ppermute | solution.py:138
  9.2 0.0 collective-permute-done.1
  9.2 0.0 collective-permute-done.5
  9.2 0.8 %collective-permute-start.11 = (bf16[2,80,640]{2,1,0:T(8,128)(2,1)S(1)}, bf16[2,80,640]{2,1,0:T(8,128)(2,1)S(1)}, u32[]{:S(2)}, u32[]{:S(2)}) collective-permute-start(bf16[2,80,640]{2,1,0:T(8,128)(2,1)S(1)} %pad_maximum_fusion.2.refs_8_), channel_id=1, source_target_pairs={{0,4},{1,5},{2,6},{3,7},{4,0},{5,1},{6,2},{7,3},{8,12},{9,13},{10,... | collective-permute-start | bytes 614408 | tf_op jit(solution)/shard_map/ppermute | solution.py:138
  10.1 2.3 %collective-permute-start.6 = (bf16[80,640]{1,0:T(8,128)(2,1)S(1)}, bf16[80,640]{1,0:T(8,128)(2,1)S(1)}, u32[]{:S(2)}, u32[]{:S(2)}) collective-permute-start(bf16[80,640]{1,0:T(8,128)(2,1)S(1)} %collective-permute-done.1), channel_id=1, source_target_pairs={{0,8},{1,9},{2,10},{3,11},{4,12},{5,13},{6,14},{7,15},{8,0},{9,1},... | collective-permute-start | bytes 307208 | tf_op jit(solution)/shard_map/ppermute | solution.py:138
  12.4 0.0 collective-permute-done
  12.5 3.7 %collective-permute-start.2 = (bf16[24,3200]{1,0:T(8,128)(2,1)S(1)}, bf16[24,3200]{1,0:T(8,128)(2,1)S(1)}, u32[]{:S(2)}, u32[]{:S(2)}) collective-permute-start(bf16[24,3200]{1,0:T(8,128)(2,1)S(1)} %broadcast_select_fusion.1.refs_0_), channel_id=1, source_target_pairs={{0,8},{1,17},{2,10},{3,19},{4,20},{5,13},{6,22},{7,15},{8,0},{9,25... | collective-permute-start | bytes 460808 | tf_op jit(solution)/shard_map/ppermute | solution.py:138
  16.1 0.0 collective-permute-start.3
  16.2 0.0 collective-permute-done.6
  16.2 0.3 collective-permute-start.7
  16.5 0.0 collective-permute-done.11.refs_11_
  16.5 2.2 %collective-permute-start.12 = (bf16[6,80,640]{2,1,0:T(8,128)(2,1)S(1)}, bf16[6,80,640]{2,1,0:T(8,128)(2,1)S(1)}, u32[]{:S(2)}, u32[]{:S(2)}) collective-permute-start(bf16[6,80,640]{2,1,0:T(8,128)(2,1)S(1)} %constant_dynamic-update-slice_fusion), channel_id=1, source_target_pairs={{0,1},{1,0},{2,3},{3,2},{4,5},{5,4},{6,7},{7,6},{8,9},{9,8},{10,11... | collective-permute-start | bytes 1843208 | tf_op jit(solution)/shard_map/ppermute | solution.py:138
  18.7 1.8 %collective-permute-done.2.refs_1_ = bf16[24,3200]{1,0:T(8,128)(2,1)S(1)} collective-permute-done((bf16[24,3200]{1,0:T(8,128)(2,1)S(1)}, bf16[24,3200]{1,0:T(8,128)(2,1)S(1)}, u32[]{:S(2)}, u32[]{:S(2)}) %collective-permute-start.2) | collective-permute-done | bytes 153632 | tf_op jit(solution)/shard_map/ppermute | solution.py:138
  20.5 0.0 collective-permute-start.4
  20.5 2.7 %collective-permute-done.3.refs_2_ = bf16[24,3200]{1,0:T(8,128)(2,1)S(1)} collective-permute-done((bf16[24,3200]{1,0:T(8,128)(2,1)S(1)}, bf16[24,3200]{1,0:T(8,128)(2,1)S(1)}, u32[]{:S(2)}, u32[]{:S(2)}) %collective-permute-start.3) | collective-permute-done | bytes 153632 | tf_op jit(solution)/shard_map/ppermute | solution.py:138
  23.2 2.7 %collective-permute-start.9 = (bf16[24,3200]{1,0:T(8,128)(2,1)S(1)}, bf16[24,3200]{1,0:T(8,128)(2,1)S(1)}, u32[]{:S(2)}, u32[]{:S(2)}) collective-permute-start(bf16[24,3200]{1,0:T(8,128)(2,1)S(1)} %collective-permute-done.3.refs_2_), channel_id=1, source_target_pairs={{0,1},{1,0},{2,3},{3,2},{4,5},{5,4},{6,7},{7,6},{8,9},{9,8},{10,11... | collective-permute-start | bytes 460808 | tf_op jit(solution)/shard_map/ppermute | solution.py:138
  25.9 0.0 collective-permute-done.7.refs_12_
  25.9 0.1 collective-permute-start.8
  26.0 0.5 %collective-permute-start.13 = (bf16[2,80,640]{2,1,0:T(8,128)(2,1)S(1)}, bf16[2,80,640]{2,1,0:T(8,128)(2,1)S(1)}, u32[]{:S(2)}, u32[]{:S(2)}) collective-permute-start(bf16[2,80,640]{2,1,0:T(8,128)(2,1)S(1)} %collective-permute-done.7.refs_12_), channel_id=1, source_target_pairs={{0,1},{1,0},{2,3},{3,2},{4,5},{5,4},{6,7},{7,6},{8,9},{9,8},{10,11... | collective-permute-start | bytes 614408 | tf_op jit(solution)/shard_map/ppermute | solution.py:138
  26.5 0.0 collective-permute-done.4
  26.5 1.0 %collective-permute-start.10 = (bf16[24,3200]{1,0:T(8,128)(2,1)S(1)}, bf16[24,3200]{1,0:T(8,128)(2,1)S(1)}, u32[]{:S(2)}, u32[]{:S(2)}) collective-permute-start(bf16[24,3200]{1,0:T(8,128)(2,1)S(1)} %broadcast_select_fusion.refs_3_), channel_id=1, source_target_pairs={{0,1},{1,0},{2,3},{3,2},{4,5},{5,4},{6,7},{7,6},{8,9},{9,8},{10,11... | collective-permute-start | bytes 460808 | tf_op jit(solution)/shard_map/ppermute | solution.py:138
  27.6 0.0 collective-permute-done.8
  27.6 0.0 collective-permute-done.12
  27.7 0.0 collective-permute-done.9.refs_6_
  27.7 0.2 collective-permute-done.13.refs_17_
  27.9 0.7 %collective-permute-done.10.refs_7_ = bf16[24,3200]{1,0:T(8,128)(2,1)S(1)} collective-permute-done((bf16[24,3200]{1,0:T(8,128)(2,1)S(1)}, bf16[24,3200]{1,0:T(8,128)(2,1)S(1)}, u32[]{:S(2)}, u32[]{:S(2)}) %collective-permute-start.10) | collective-permute-done | bytes 153632 | tf_op jit(solution)/shard_map/ppermute | solution.py:138
  28.6 2.5 %group_kernel.1 = (bf16[88,640]{1,0:T(8,128)(2,1)S(1)}, bf16[88,640]{1,0:T(8,128)(2,1)S(1)}, bf16[2,24,1280]{2,1,0:T(8,128)(2,1)S(1)}) custom-call(f32[1]{0:T(128)S(6)} %copy.14.log_scale, bf16[24,3200]{1,0:T(8,128)(2,1)S(1)} %broadcast_select_fusion.1.refs_0_, bf16[24,3200]{1,0:T(8,128)(2,1)S(1)} %collective-permute-done.2.refs_1_, ...), custom_call_target="tpu_custom_call" | custom-call | tf_op jit(solution)/shard_map/group_kernel/pallas_call | solution.py:320
  31.1 1.3 %collective-permute-start.14 = (bf16[88,640]{1,0:T(8,128)(2,1)S(1)}, bf16[88,640]{1,0:T(8,128)(2,1)S(1)}, u32[]{:S(2)}, u32[]{:S(2)}) collective-permute-start(bf16[88,640]{1,0:T(8,128)(2,1)S(1)} %get-tuple-element.18), channel_id=1, source_target_pairs={{0,2},{1,3},{2,0},{3,1},{4,6},{5,7},{6,4},{7,5},{8,10},{9,11},{10,... | collective-permute-start | bytes 337928 | tf_op jit(solution)/shard_map/ppermute | solution.py:138
  32.4 0.2 collective-permute-start.15
  32.7 1.2 %collective-permute-start.16 = (bf16[88,640]{1,0:T(8,128)(2,1)S(1)}, bf16[88,640]{1,0:T(8,128)(2,1)S(1)}, u32[]{:S(2)}, u32[]{:S(2)}) collective-permute-start(bf16[88,640]{1,0:T(8,128)(2,1)S(1)} %get-tuple-element.19), channel_id=1, source_target_pairs={{0,6},{1,7},{2,4},{3,5},{4,2},{5,3},{6,0},{7,1},{8,14},{9,15},{10,... | collective-permute-start | bytes 337928 | tf_op jit(solution)/shard_map/ppermute | solution.py:138
  33.8 1.3 %collective-permute-start.17 = (bf16[2,24,1280]{2,1,0:T(8,128)(2,1)S(1)}, bf16[2,24,1280]{2,1,0:T(8,128)(2,1)S(1)}, u32[]{:S(2)}, u32[]{:S(2)}) collective-permute-start(bf16[2,24,1280]{2,1,0:T(8,128)(2,1)S(1)} %get-tuple-element.20), channel_id=1, source_target_pairs={{0,8},{1,4},{2,10},{3,6},{4,1},{5,13},{6,3},{7,15},{8,0},{9,12},{1... | collective-permute-start | bytes 368648 | tf_op jit(solution)/shard_map/ppermute | solution.py:138
  35.2 0.4 collective-permute-done.14
  35.5 0.9 %collective-permute-done.15 = bf16[88,640]{1,0:T(8,128)(2,1)S(1)} collective-permute-done((bf16[88,640]{1,0:T(8,128)(2,1)S(1)}, bf16[88,640]{1,0:T(8,128)(2,1)S(1)}, u32[]{:S(2)}, u32[]{:S(2)}) %collective-permute-start.15) | collective-permute-done | bytes 112672 | tf_op jit(solution)/shard_map/ppermute | solution.py:138
  36.4 2.4 %collective-permute-done.16 = bf16[88,640]{1,0:T(8,128)(2,1)S(1)} collective-permute-done((bf16[88,640]{1,0:T(8,128)(2,1)S(1)}, bf16[88,640]{1,0:T(8,128)(2,1)S(1)}, u32[]{:S(2)}, u32[]{:S(2)}) %collective-permute-start.16) | collective-permute-done | bytes 112672 | tf_op jit(solution)/shard_map/ppermute | solution.py:138
  38.8 0.1 add_add_fusion
  38.9 1.6 %collective-permute-start.18 = (f32[80,640]{1,0:T(8,128)S(1)}, f32[80,640]{1,0:T(8,128)S(1)}, u32[]{:S(2)}, u32[]{:S(2)}) collective-permute-start(f32[80,640]{1,0:T(8,128)S(1)} %slice.57), channel_id=1, source_target_pairs={{0,1},{1,0},{2,3},{3,2},{4,5},{5,4},{6,7},{7,6},{8,9},{9,8},{10,11... | collective-permute-start | bytes 614408 | tf_op jit(solution)/shard_map/ppermute | solution.py:138
  40.5 0.1 reshape_squeeze.3
  40.5 0.1 reduce_sum.9
  40.7 0.6 %fusion.3 = (f32[1]{0:T(128)}, f32[1]{0:T(128)}) fusion(f32[2]{0:T(128)S(1)} %reduce_sum.9), kind=kLoop, calls=%fused_computation.21 | loop fusion | bytes 16 | tf_op jit(solution)/shard_map/slice | solution.py:357
  41.3 0.0 collective-permute-done.17
  41.3 0.7 %fusion.2 = (bf16[1,24,1280]{2,1,0:T(8,128)(2,1)}, bf16[1,24,1280]{2,1,0:T(8,128)(2,1)}) fusion(bf16[2,24,1280]{2,1,0:T(8,128)(2,1)S(1)} %broadcast_select_fusion.2), kind=kLoop, calls=%fused_computation.20 | loop fusion | bytes 245760 | tf_op jit(solution)/shard_map/slice | solution.py:357
  41.9 0.0 collective-permute-done.18
  41.9 0.8 %maximum_select_fusion = f32[80,1280]{1,0:T(8,128)} fusion(f32[80,640]{1,0:T(8,128)S(1)} %collective-permute-done.18, f32[80,640]{1,0:T(8,128)S(1)} %slice.57, pred[]{:T(512)S(6)} %eq.10), kind=kLoop, calls=%fused_computation | loop fusion | flops 307200 | bytes 819201 | tf_op jit(solution)/shard_map/jit(_where)/select_n | solution.py:351
  (18 shorter events, 0.4 us)
Async XLA Ops:
  0.6 0.9 %copy-start = (bf16[80,1280]{1,0:T(8,128)(2,1)S(1)}, bf16[80,1280]{1,0:T(8,128)(2,1)}, u32[]{:S(2)}) copy-start(bf16[80,1280]{1,0:T(8,128)(2,1)} %param.8) | copy-start | bytes 614404
  1.6 4.5 %copy-start.1 = (bf16[1,24,1280]{2,1,0:T(8,128)(2,1)S(1)}, bf16[1,24,1280]{2,1,0:T(8,128)(2,1)}, u32[]{:S(2)}) copy-start(bf16[1,24,1280]{2,1,0:T(8,128)(2,1)} %param.7) | copy-start | bytes 184324
  1.6 4.5 %copy-start.2 = (bf16[1,24,1280]{2,1,0:T(8,128)(2,1)S(1)}, bf16[1,24,1280]{2,1,0:T(8,128)(2,1)}, u32[]{:S(2)}) copy-start(bf16[1,24,1280]{2,1,0:T(8,128)(2,1)} %param.5) | copy-start | bytes 184324
  1.6 4.5 %copy-start.3 = (bf16[1,24,640]{2,1,0:T(8,128)(2,1)S(1)}, bf16[1,24,640]{2,1,0:T(8,128)(2,1)}, u32[]{:S(2)}) copy-start(bf16[1,24,640]{2,1,0:T(8,128)(2,1)} %param.6) | copy-start | bytes 92164
  1.6 7.6 %collective-permute-start.1 = (bf16[80,640]{1,0:T(8,128)(2,1)S(1)}, bf16[80,640]{1,0:T(8,128)(2,1)S(1)}, u32[]{:S(2)}, u32[]{:S(2)}) collective-permute-start(bf16[80,640]{1,0:T(8,128)(2,1)S(1)} %constant_dynamic-slice_fusion), channel_id=1, source_target_pairs={{0,16},{1,17},{2,18},{3,19},{4,20},{5,21},{6,22},{7,23},{8,24},{9,... | collective-permute-start | bytes 307208 | tf_op jit(solution)/shard_map/ppermute | solution.py:138
  4.8 4.4 %collective-permute-start.5 = (bf16[80,640]{1,0:T(8,128)(2,1)S(1)}, bf16[80,640]{1,0:T(8,128)(2,1)S(1)}, u32[]{:S(2)}, u32[]{:S(2)}) collective-permute-start(bf16[80,640]{1,0:T(8,128)(2,1)S(1)} %constant_dynamic-slice_fusion), channel_id=1, source_target_pairs={{0,8},{1,9},{2,10},{3,11},{4,12},{5,13},{6,14},{7,15},{8,0},{9,1},... | collective-permute-start | bytes 307208 | tf_op jit(solution)/shard_map/ppermute | solution.py:138
  6.1 6.3 %collective-permute-start = (bf16[24,3200]{1,0:T(8,128)(2,1)S(1)}, bf16[24,3200]{1,0:T(8,128)(2,1)S(1)}, u32[]{:S(2)}, u32[]{:S(2)}) collective-permute-start(bf16[24,3200]{1,0:T(8,128)(2,1)S(1)} %pad_maximum_fusion.3), channel_id=1, source_target_pairs={{0,16},{1,4},{2,18},{3,6},{4,1},{5,21},{6,3},{7,23},{8,24},{9,12},... | collective-permute-start | bytes 460808 | tf_op jit(solution)/shard_map/ppermute | solution.py:138
  9.2 7.2 %collective-permute-start.11 = (bf16[2,80,640]{2,1,0:T(8,128)(2,1)S(1)}, bf16[2,80,640]{2,1,0:T(8,128)(2,1)S(1)}, u32[]{:S(2)}, u32[]{:S(2)}) collective-permute-start(bf16[2,80,640]{2,1,0:T(8,128)(2,1)S(1)} %pad_maximum_fusion.2.refs_8_), channel_id=1, source_target_pairs={{0,4},{1,5},{2,6},{3,7},{4,0},{5,1},{6,2},{7,3},{8,12},{9,13},{10,... | collective-permute-start | bytes 614408 | tf_op jit(solution)/shard_map/ppermute | solution.py:138
  10.1 6.1 %collective-permute-start.6 = (bf16[80,640]{1,0:T(8,128)(2,1)S(1)}, bf16[80,640]{1,0:T(8,128)(2,1)S(1)}, u32[]{:S(2)}, u32[]{:S(2)}) collective-permute-start(bf16[80,640]{1,0:T(8,128)(2,1)S(1)} %collective-permute-done.1), channel_id=1, source_target_pairs={{0,8},{1,9},{2,10},{3,11},{4,12},{5,13},{6,14},{7,15},{8,0},{9,1},... | collective-permute-start | bytes 307208 | tf_op jit(solution)/shard_map/ppermute | solution.py:138
  12.5 8.0 %collective-permute-start.2 = (bf16[24,3200]{1,0:T(8,128)(2,1)S(1)}, bf16[24,3200]{1,0:T(8,128)(2,1)S(1)}, u32[]{:S(2)}, u32[]{:S(2)}) collective-permute-start(bf16[24,3200]{1,0:T(8,128)(2,1)S(1)} %broadcast_select_fusion.1.refs_0_), channel_id=1, source_target_pairs={{0,8},{1,17},{2,10},{3,19},{4,20},{5,13},{6,22},{7,15},{8,0},{9,25... | collective-permute-start | bytes 460808 | tf_op jit(solution)/shard_map/ppermute | solution.py:138
  16.1 7.1 %collective-permute-start.3 = (bf16[24,3200]{1,0:T(8,128)(2,1)S(1)}, bf16[24,3200]{1,0:T(8,128)(2,1)S(1)}, u32[]{:S(2)}, u32[]{:S(2)}) collective-permute-start(bf16[24,3200]{1,0:T(8,128)(2,1)S(1)} %collective-permute-done), channel_id=1, source_target_pairs={{0,8},{1,9},{2,10},{3,11},{4,12},{5,13},{6,14},{7,15},{8,0},{9,1},... | collective-permute-start | bytes 460808 | tf_op jit(solution)/shard_map/ppermute | solution.py:138
  16.2 9.7 %collective-permute-start.7 = (bf16[2,80,640]{2,1,0:T(8,128)(2,1)S(1)}, bf16[2,80,640]{2,1,0:T(8,128)(2,1)S(1)}, u32[]{:S(2)}, u32[]{:S(2)}) collective-permute-start(bf16[2,80,640]{2,1,0:T(8,128)(2,1)S(1)} %pad_maximum_fusion.1), channel_id=1, source_target_pairs={{0,4},{1,5},{2,6},{3,7},{4,0},{5,1},{6,2},{7,3},{8,12},{9,13},{10,... | collective-permute-start | bytes 614408 | tf_op jit(solution)/shard_map/ppermute | solution.py:138
  16.5 11.1 %collective-permute-start.12 = (bf16[6,80,640]{2,1,0:T(8,128)(2,1)S(1)}, bf16[6,80,640]{2,1,0:T(8,128)(2,1)S(1)}, u32[]{:S(2)}, u32[]{:S(2)}) collective-permute-start(bf16[6,80,640]{2,1,0:T(8,128)(2,1)S(1)} %constant_dynamic-update-slice_fusion), channel_id=1, source_target_pairs={{0,1},{1,0},{2,3},{3,2},{4,5},{5,4},{6,7},{7,6},{8,9},{9,8},{10,11... | collective-permute-start | bytes 1843208 | tf_op jit(solution)/shard_map/ppermute | solution.py:138
  20.5 6.0 %collective-permute-start.4 = (bf16[24,3200]{1,0:T(8,128)(2,1)S(1)}, bf16[24,3200]{1,0:T(8,128)(2,1)S(1)}, u32[]{:S(2)}, u32[]{:S(2)}) collective-permute-start(bf16[24,3200]{1,0:T(8,128)(2,1)S(1)} %collective-permute-done.2.refs_1_), channel_id=1, source_target_pairs={{0,5},{1,9},{2,7},{3,11},{4,12},{5,0},{6,14},{7,2},{8,13},{9,1},{1... | collective-permute-start | bytes 460808 | tf_op jit(solution)/shard_map/ppermute | solution.py:138
  23.2 4.5 %collective-permute-start.9 = (bf16[24,3200]{1,0:T(8,128)(2,1)S(1)}, bf16[24,3200]{1,0:T(8,128)(2,1)S(1)}, u32[]{:S(2)}, u32[]{:S(2)}) collective-permute-start(bf16[24,3200]{1,0:T(8,128)(2,1)S(1)} %collective-permute-done.3.refs_2_), channel_id=1, source_target_pairs={{0,1},{1,0},{2,3},{3,2},{4,5},{5,4},{6,7},{7,6},{8,9},{9,8},{10,11... | collective-permute-start | bytes 460808 | tf_op jit(solution)/shard_map/ppermute | solution.py:138
  25.9 1.7 %collective-permute-start.8 = (bf16[2,24,3200]{2,1,0:T(8,128)(2,1)S(1)}, bf16[2,24,3200]{2,1,0:T(8,128)(2,1)S(1)}, u32[]{:S(2)}, u32[]{:S(2)}) collective-permute-start(bf16[2,24,3200]{2,1,0:T(8,128)(2,1)S(1)} %pad_maximum_fusion), channel_id=1, source_target_pairs={{0,1},{1,0},{2,3},{3,2},{4,5},{5,4},{6,7},{7,6},{8,9},{9,8},{10,11... | collective-permute-start | bytes 921608 | tf_op jit(solution)/shard_map/ppermute | solution.py:138
  26.0 1.9 %collective-permute-start.13 = (bf16[2,80,640]{2,1,0:T(8,128)(2,1)S(1)}, bf16[2,80,640]{2,1,0:T(8,128)(2,1)S(1)}, u32[]{:S(2)}, u32[]{:S(2)}) collective-permute-start(bf16[2,80,640]{2,1,0:T(8,128)(2,1)S(1)} %collective-permute-done.7.refs_12_), channel_id=1, source_target_pairs={{0,1},{1,0},{2,3},{3,2},{4,5},{5,4},{6,7},{7,6},{8,9},{9,8},{10,11... | collective-permute-start | bytes 614408 | tf_op jit(solution)/shard_map/ppermute | solution.py:138
  26.5 2.0 %collective-permute-start.10 = (bf16[24,3200]{1,0:T(8,128)(2,1)S(1)}, bf16[24,3200]{1,0:T(8,128)(2,1)S(1)}, u32[]{:S(2)}, u32[]{:S(2)}) collective-permute-start(bf16[24,3200]{1,0:T(8,128)(2,1)S(1)} %broadcast_select_fusion.refs_3_), channel_id=1, source_target_pairs={{0,1},{1,0},{2,3},{3,2},{4,5},{5,4},{6,7},{7,6},{8,9},{9,8},{10,11... | collective-permute-start | bytes 460808 | tf_op jit(solution)/shard_map/ppermute | solution.py:138
  31.1 4.4 %collective-permute-start.14 = (bf16[88,640]{1,0:T(8,128)(2,1)S(1)}, bf16[88,640]{1,0:T(8,128)(2,1)S(1)}, u32[]{:S(2)}, u32[]{:S(2)}) collective-permute-start(bf16[88,640]{1,0:T(8,128)(2,1)S(1)} %get-tuple-element.18), channel_id=1, source_target_pairs={{0,2},{1,3},{2,0},{3,1},{4,6},{5,7},{6,4},{7,5},{8,10},{9,11},{10,... | collective-permute-start | bytes 337928 | tf_op jit(solution)/shard_map/ppermute | solution.py:138
  32.4 4.0 %collective-permute-start.15 = (bf16[88,640]{1,0:T(8,128)(2,1)S(1)}, bf16[88,640]{1,0:T(8,128)(2,1)S(1)}, u32[]{:S(2)}, u32[]{:S(2)}) collective-permute-start(bf16[88,640]{1,0:T(8,128)(2,1)S(1)} %get-tuple-element.19), channel_id=1, source_target_pairs={{0,4},{1,5},{2,6},{3,7},{4,0},{5,1},{6,2},{7,3},{8,12},{9,13},{10,... | collective-permute-start | bytes 337928 | tf_op jit(solution)/shard_map/ppermute | solution.py:138
  32.7 6.1 %collective-permute-start.16 = (bf16[88,640]{1,0:T(8,128)(2,1)S(1)}, bf16[88,640]{1,0:T(8,128)(2,1)S(1)}, u32[]{:S(2)}, u32[]{:S(2)}) collective-permute-start(bf16[88,640]{1,0:T(8,128)(2,1)S(1)} %get-tuple-element.19), channel_id=1, source_target_pairs={{0,6},{1,7},{2,4},{3,5},{4,2},{5,3},{6,0},{7,1},{8,14},{9,15},{10,... | collective-permute-start | bytes 337928 | tf_op jit(solution)/shard_map/ppermute | solution.py:138
  33.8 7.4 %collective-permute-start.17 = (bf16[2,24,1280]{2,1,0:T(8,128)(2,1)S(1)}, bf16[2,24,1280]{2,1,0:T(8,128)(2,1)S(1)}, u32[]{:S(2)}, u32[]{:S(2)}) collective-permute-start(bf16[2,24,1280]{2,1,0:T(8,128)(2,1)S(1)} %get-tuple-element.20), channel_id=1, source_target_pairs={{0,8},{1,4},{2,10},{3,6},{4,1},{5,13},{6,3},{7,15},{8,0},{9,12},{1... | collective-permute-start | bytes 368648 | tf_op jit(solution)/shard_map/ppermute | solution.py:138
  38.9 3.0 %collective-permute-start.18 = (f32[80,640]{1,0:T(8,128)S(1)}, f32[80,640]{1,0:T(8,128)S(1)}, u32[]{:S(2)}, u32[]{:S(2)}) collective-permute-start(f32[80,640]{1,0:T(8,128)S(1)} %slice.57), channel_id=1, source_target_pairs={{0,1},{1,0},{2,3},{3,2},{4,5},{5,4},{6,7},{7,6},{8,9},{9,8},{10,11... | collective-permute-start | bytes 614408 | tf_op jit(solution)/shard_map/ppermute | solution.py:138

commit v7 on v6

--- a/solution.py
+++ b/solution.py
@@ -213,7 +213,7 @@
     keep, send, grads = refs[8 + count : 11 + count]
     image, text, hidden, hidden_t, norms, proj, coefs, grad_all, share = refs[11 + count :]
     z, x, y, core = own_place()
-    rows, depth = rows_here[0].shape[0], proj.shape[1] // 8
+    rows, depth = rows_here[0].shape[0], proj.shape[0] // 8
     width = image.shape[1]
     half = width // 2
     ahead = is_ahead(x, core)
@@ -226,15 +226,13 @@
             hidden[pl.ds(start, rows), :] = block[:, 2 * width :].astype(F32)
     for at, blocks in enumerate(projs):
         side, kind = divmod(at, len(PROJ_STEPS))
+        left = pl.multiple_of((core ^ side) * half, 128)
         steps, column = PROJ_STEPS[kind]
         for block, step in enumerate(steps):
             start = pl.multiple_of(((z ^ step) * 2 + (x ^ column)) * depth, 16)
-            proj[core ^ side, pl.ds(start, depth), :] = blocks[block]
+            proj[pl.ds(start, depth), pl.ds(left, half)] = blocks[block]
     hidden_short = hidden[...].astype(BF16)
-    for side in range(2):
-        text[:, side * half : (side + 1) * half] += jnp.dot(
-            hidden_short, proj[side], preferred_element_type=F32
-        )
+    text[...] += jnp.dot(hidden_short, proj[...], preferred_element_type=F32)
     hidden_t[...] = hidden[...].T
     text_inv = inverse_norm(text[...])
     text_short = (text[...] * text_inv).astype(BF16)
@@ -332,7 +330,7 @@
             pltpu.VMEM((total_rows, total_depth), F32),
             pltpu.VMEM((total_depth, total_rows), F32),
             pltpu.VMEM((total_rows, 128), F32),
-            pltpu.VMEM((2, total_depth, half), BF16),
+            pltpu.VMEM((total_depth, width), BF16),
             pltpu.VMEM((total_rows, total_rows), F32),
             pltpu.VMEM((total_rows, width), F32),
             pltpu.VMEM((2 * depth, half), F32),

time: 42.9 us -> 42.8 us (level)
  no operation moved by 1% of the time
where the time goes in v7:
time: 42.8 us; the launch traced here: 42.6 us
  starting transfers between devices  26.1 us (61%)
  waiting for transfers between devices  9.02 us (21%)
  local copies, waits for them, and re-layouts  2.45 us (6%)
  Pallas kernels  2.45 us (6%)
  between operations  1.48 us (3%)
  other arithmetic  1.14 us (3%)
    ppermute x19, starting transfers between devices, moved(): lax.ppermute(value, ('blk', 'rep'), [(number(*place), number(*to(*place))...  26.1 us
    ppermute x19, waiting for transfers between devices, moved(): lax.ppermute(value, ('blk', 'rep'), [(number(*place), number(*to(*place))...  9.02 us
    pallas_call x1, Pallas kernels, on_device_whole_group(): pl.pallas_call(functools.partial(group_kernel, factor), out_shape=(jax.Sh...  2.45 us
    slice x2, local copies, waits for them, and re-layouts, on_device_whole_group(): return (totals[0:1], totals[1:2], grads[0][None], grads[1][None], grad_proj)  1.24 us
    unnamed x12, local copies, waits for them, and re-layouts  0.98 us
  transfers between devices with their start and end apart: 19, of which 7 were waited for; matrix products, arithmetic and copies ran while one was open for 4% of the time, Pallas kernels for 0%

profile of v7, /device:TPU:1, one launch (start us, length us, event | category | flops | bytes accessed | tf_op | source)
XLA Modules:
  0.0 42.6 jit_solution(1900507539299368395)
XLA Ops:
  0.6 0.0 copy-start
  0.7 0.9 %copy-done = bf16[80,1280]{1,0:T(8,128)(2,1)S(1)} copy-done((bf16[80,1280]{1,0:T(8,128)(2,1)S(1)}, bf16[80,1280]{1,0:T(8,128)(2,1)}, u32[]{:S(2)}) %copy-start) | copy-done | bytes 204824
  1.6 0.0 copy-start.1
  1.6 0.0 copy-start.2
  1.6 0.0 copy-start.3
  1.6 3.2 %collective-permute-start.1 = (bf16[80,640]{1,0:T(8,128)(2,1)S(1)}, bf16[80,640]{1,0:T(8,128)(2,1)S(1)}, u32[]{:S(2)}, u32[]{:S(2)}) collective-permute-start(bf16[80,640]{1,0:T(8,128)(2,1)S(1)} %constant_dynamic-slice_fusion), channel_id=1, source_target_pairs={{0,16},{1,17},{2,18},{3,19},{4,20},{5,21},{6,22},{7,23},{8,24},{9,... | collective-permute-start | bytes 307208 | tf_op jit(solution)/shard_map/ppermute | solution.py:138
  4.8 1.3 %collective-permute-start.5 = (bf16[80,640]{1,0:T(8,128)(2,1)S(1)}, bf16[80,640]{1,0:T(8,128)(2,1)S(1)}, u32[]{:S(2)}, u32[]{:S(2)}) collective-permute-start(bf16[80,640]{1,0:T(8,128)(2,1)S(1)} %constant_dynamic-slice_fusion), channel_id=1, source_target_pairs={{0,8},{1,9},{2,10},{3,11},{4,12},{5,13},{6,14},{7,15},{8,0},{9,1},... | collective-permute-start | bytes 307208 | tf_op jit(solution)/shard_map/ppermute | solution.py:138
  6.1 0.0 copy-done.1
  6.1 0.0 copy-done.2
  6.1 0.0 copy-done.3
  6.1 2.4 %collective-permute-start = (bf16[24,3200]{1,0:T(8,128)(2,1)S(1)}, bf16[24,3200]{1,0:T(8,128)(2,1)S(1)}, u32[]{:S(2)}, u32[]{:S(2)}) collective-permute-start(bf16[24,3200]{1,0:T(8,128)(2,1)S(1)} %pad_maximum_fusion.3), channel_id=1, source_target_pairs={{0,16},{1,4},{2,18},{3,6},{4,1},{5,21},{6,3},{7,23},{8,24},{9,12},... | collective-permute-start | bytes 460808 | tf_op jit(solution)/shard_map/ppermute | solution.py:138
  9.2 0.0 collective-permute-done.1
  9.2 0.0 collective-permute-done.5
  9.2 0.8 %collective-permute-start.11 = (bf16[2,80,640]{2,1,0:T(8,128)(2,1)S(1)}, bf16[2,80,640]{2,1,0:T(8,128)(2,1)S(1)}, u32[]{:S(2)}, u32[]{:S(2)}) collective-permute-start(bf16[2,80,640]{2,1,0:T(8,128)(2,1)S(1)} %pad_maximum_fusion.2.refs_8_), channel_id=1, source_target_pairs={{0,4},{1,5},{2,6},{3,7},{4,0},{5,1},{6,2},{7,3},{8,12},{9,13},{10,... | collective-permute-start | bytes 614408 | tf_op jit(solution)/shard_map/ppermute | solution.py:138
  10.1 2.3 %collective-permute-start.6 = (bf16[80,640]{1,0:T(8,128)(2,1)S(1)}, bf16[80,640]{1,0:T(8,128)(2,1)S(1)}, u32[]{:S(2)}, u32[]{:S(2)}) collective-permute-start(bf16[80,640]{1,0:T(8,128)(2,1)S(1)} %collective-permute-done.1), channel_id=1, source_target_pairs={{0,8},{1,9},{2,10},{3,11},{4,12},{5,13},{6,14},{7,15},{8,0},{9,1},... | collective-permute-start | bytes 307208 | tf_op jit(solution)/shard_map/ppermute | solution.py:138
  12.4 0.0 collective-permute-done
  12.5 3.7 %collective-permute-start.2 = (bf16[24,3200]{1,0:T(8,128)(2,1)S(1)}, bf16[24,3200]{1,0:T(8,128)(2,1)S(1)}, u32[]{:S(2)}, u32[]{:S(2)}) collective-permute-start(bf16[24,3200]{1,0:T(8,128)(2,1)S(1)} %broadcast_select_fusion.1.refs_0_), channel_id=1, source_target_pairs={{0,8},{1,17},{2,10},{3,19},{4,20},{5,13},{6,22},{7,15},{8,0},{9,25... | collective-permute-start | bytes 460808 | tf_op jit(solution)/shard_map/ppermute | solution.py:138
  16.1 0.0 collective-permute-start.3
  16.2 0.0 collective-permute-done.6
  16.2 0.3 collective-permute-start.7
  16.5 0.0 collective-permute-done.11.refs_11_
  16.5 2.2 %collective-permute-start.12 = (bf16[6,80,640]{2,1,0:T(8,128)(2,1)S(1)}, bf16[6,80,640]{2,1,0:T(8,128)(2,1)S(1)}, u32[]{:S(2)}, u32[]{:S(2)}) collective-permute-start(bf16[6,80,640]{2,1,0:T(8,128)(2,1)S(1)} %constant_dynamic-update-slice_fusion), channel_id=1, source_target_pairs={{0,1},{1,0},{2,3},{3,2},{4,5},{5,4},{6,7},{7,6},{8,9},{9,8},{10,11... | collective-permute-start | bytes 1843208 | tf_op jit(solution)/shard_map/ppermute | solution.py:138
  18.7 1.8 %collective-permute-done.2.refs_1_ = bf16[24,3200]{1,0:T(8,128)(2,1)S(1)} collective-permute-done((bf16[24,3200]{1,0:T(8,128)(2,1)S(1)}, bf16[24,3200]{1,0:T(8,128)(2,1)S(1)}, u32[]{:S(2)}, u32[]{:S(2)}) %collective-permute-start.2) | collective-permute-done | bytes 153632 | tf_op jit(solution)/shard_map/ppermute | solution.py:138
  20.5 0.0 collective-permute-start.4
  20.5 2.7 %collective-permute-done.3.refs_2_ = bf16[24,3200]{1,0:T(8,128)(2,1)S(1)} collective-permute-done((bf16[24,3200]{1,0:T(8,128)(2,1)S(1)}, bf16[24,3200]{1,0:T(8,128)(2,1)S(1)}, u32[]{:S(2)}, u32[]{:S(2)}) %collective-permute-start.3) | collective-permute-done | bytes 153632 | tf_op jit(solution)/shard_map/ppermute | solution.py:138
  23.2 2.7 %collective-permute-start.9 = (bf16[24,3200]{1,0:T(8,128)(2,1)S(1)}, bf16[24,3200]{1,0:T(8,128)(2,1)S(1)}, u32[]{:S(2)}, u32[]{:S(2)}) collective-permute-start(bf16[24,3200]{1,0:T(8,128)(2,1)S(1)} %collective-permute-done.3.refs_2_), channel_id=1, source_target_pairs={{0,1},{1,0},{2,3},{3,2},{4,5},{5,4},{6,7},{7,6},{8,9},{9,8},{10,11... | collective-permute-start | bytes 460808 | tf_op jit(solution)/shard_map/ppermute | solution.py:138
  25.9 0.0 collective-permute-done.7.refs_12_
  25.9 0.1 collective-permute-start.8
  26.0 0.5 %collective-permute-start.13 = (bf16[2,80,640]{2,1,0:T(8,128)(2,1)S(1)}, bf16[2,80,640]{2,1,0:T(8,128)(2,1)S(1)}, u32[]{:S(2)}, u32[]{:S(2)}) collective-permute-start(bf16[2,80,640]{2,1,0:T(8,128)(2,1)S(1)} %collective-permute-done.7.refs_12_), channel_id=1, source_target_pairs={{0,1},{1,0},{2,3},{3,2},{4,5},{5,4},{6,7},{7,6},{8,9},{9,8},{10,11... | collective-permute-start | bytes 614408 | tf_op jit(solution)/shard_map/ppermute | solution.py:138
  26.5 0.0 collective-permute-done.4
  26.5 1.0 %collective-permute-start.10 = (bf16[24,3200]{1,0:T(8,128)(2,1)S(1)}, bf16[24,3200]{1,0:T(8,128)(2,1)S(1)}, u32[]{:S(2)}, u32[]{:S(2)}) collective-permute-start(bf16[24,3200]{1,0:T(8,128)(2,1)S(1)} %broadcast_select_fusion.refs_3_), channel_id=1, source_target_pairs={{0,1},{1,0},{2,3},{3,2},{4,5},{5,4},{6,7},{7,6},{8,9},{9,8},{10,11... | collective-permute-start | bytes 460808 | tf_op jit(solution)/shard_map/ppermute | solution.py:138
  27.6 0.0 collective-permute-done.8
  27.6 0.0 collective-permute-done.12
  27.7 0.0 collective-permute-done.9.refs_6_
  27.7 0.2 collective-permute-done.13.refs_17_
  27.9 0.7 %collective-permute-done.10.refs_7_ = bf16[24,3200]{1,0:T(8,128)(2,1)S(1)} collective-permute-done((bf16[24,3200]{1,0:T(8,128)(2,1)S(1)}, bf16[24,3200]{1,0:T(8,128)(2,1)S(1)}, u32[]{:S(2)}, u32[]{:S(2)}) %collective-permute-start.10) | collective-permute-done | bytes 153632 | tf_op jit(solution)/shard_map/ppermute | solution.py:138
  28.6 2.4 %group_kernel.1 = (bf16[88,640]{1,0:T(8,128)(2,1)S(1)}, bf16[88,640]{1,0:T(8,128)(2,1)S(1)}, bf16[2,24,1280]{2,1,0:T(8,128)(2,1)S(1)}) custom-call(f32[1]{0:T(128)S(6)} %copy.14.log_scale, bf16[24,3200]{1,0:T(8,128)(2,1)S(1)} %broadcast_select_fusion.1.refs_0_, bf16[24,3200]{1,0:T(8,128)(2,1)S(1)} %collective-permute-done.2.refs_1_, ...), custom_call_target="tpu_custom_call" | custom-call | tf_op jit(solution)/shard_map/group_kernel/pallas_call | solution.py:318
  31.0 1.3 %collective-permute-start.14 = (bf16[88,640]{1,0:T(8,128)(2,1)S(1)}, bf16[88,640]{1,0:T(8,128)(2,1)S(1)}, u32[]{:S(2)}, u32[]{:S(2)}) collective-permute-start(bf16[88,640]{1,0:T(8,128)(2,1)S(1)} %get-tuple-element.18), channel_id=1, source_target_pairs={{0,2},{1,3},{2,0},{3,1},{4,6},{5,7},{6,4},{7,5},{8,10},{9,11},{10,... | collective-permute-start | bytes 337928 | tf_op jit(solution)/shard_map/ppermute | solution.py:138
  32.3 0.3 collective-permute-start.15
  32.6 1.2 %collective-permute-start.16 = (bf16[88,640]{1,0:T(8,128)(2,1)S(1)}, bf16[88,640]{1,0:T(8,128)(2,1)S(1)}, u32[]{:S(2)}, u32[]{:S(2)}) collective-permute-start(bf16[88,640]{1,0:T(8,128)(2,1)S(1)} %get-tuple-element.19), channel_id=1, source_target_pairs={{0,6},{1,7},{2,4},{3,5},{4,2},{5,3},{6,0},{7,1},{8,14},{9,15},{10,... | collective-permute-start | bytes 337928 | tf_op jit(solution)/shard_map/ppermute | solution.py:138
  33.7 1.3 %collective-permute-start.17 = (bf16[2,24,1280]{2,1,0:T(8,128)(2,1)S(1)}, bf16[2,24,1280]{2,1,0:T(8,128)(2,1)S(1)}, u32[]{:S(2)}, u32[]{:S(2)}) collective-permute-start(bf16[2,24,1280]{2,1,0:T(8,128)(2,1)S(1)} %get-tuple-element.20), channel_id=1, source_target_pairs={{0,8},{1,4},{2,10},{3,6},{4,1},{5,13},{6,3},{7,15},{8,0},{9,12},{1... | collective-permute-start | bytes 368648 | tf_op jit(solution)/shard_map/ppermute | solution.py:138
  35.1 0.3 collective-permute-done.14
  35.4 0.9 %collective-permute-done.15 = bf16[88,640]{1,0:T(8,128)(2,1)S(1)} collective-permute-done((bf16[88,640]{1,0:T(8,128)(2,1)S(1)}, bf16[88,640]{1,0:T(8,128)(2,1)S(1)}, u32[]{:S(2)}, u32[]{:S(2)}) %collective-permute-start.15) | collective-permute-done | bytes 112672 | tf_op jit(solution)/shard_map/ppermute | solution.py:138
  36.3 2.4 %collective-permute-done.16 = bf16[88,640]{1,0:T(8,128)(2,1)S(1)} collective-permute-done((bf16[88,640]{1,0:T(8,128)(2,1)S(1)}, bf16[88,640]{1,0:T(8,128)(2,1)S(1)}, u32[]{:S(2)}, u32[]{:S(2)}) %collective-permute-start.16) | collective-permute-done | bytes 112672 | tf_op jit(solution)/shard_map/ppermute | solution.py:138
  38.7 0.1 add_add_fusion
  38.8 1.6 %collective-permute-start.18 = (f32[80,640]{1,0:T(8,128)S(1)}, f32[80,640]{1,0:T(8,128)S(1)}, u32[]{:S(2)}, u32[]{:S(2)}) collective-permute-start(f32[80,640]{1,0:T(8,128)S(1)} %slice.57), channel_id=1, source_target_pairs={{0,1},{1,0},{2,3},{3,2},{4,5},{5,4},{6,7},{7,6},{8,9},{9,8},{10,11... | collective-permute-start | bytes 614408 | tf_op jit(solution)/shard_map/ppermute | solution.py:138
  40.4 0.1 reshape_squeeze.3
  40.5 0.1 reduce_sum.9
  40.6 0.6 %fusion.3 = (f32[1]{0:T(128)}, f32[1]{0:T(128)}) fusion(f32[2]{0:T(128)S(1)} %reduce_sum.9), kind=kLoop, calls=%fused_computation.21 | loop fusion | bytes 16 | tf_op jit(solution)/shard_map/slice | solution.py:355
  41.2 0.0 collective-permute-done.17
  41.2 0.7 %fusion.2 = (bf16[1,24,1280]{2,1,0:T(8,128)(2,1)}, bf16[1,24,1280]{2,1,0:T(8,128)(2,1)}) fusion(bf16[2,24,1280]{2,1,0:T(8,128)(2,1)S(1)} %broadcast_select_fusion.2), kind=kLoop, calls=%fused_computation.20 | loop fusion | bytes 245760 | tf_op jit(solution)/shard_map/slice | solution.py:355
  41.8 0.0 collective-permute-done.18
  41.8 0.8 %maximum_select_fusion = f32[80,1280]{1,0:T(8,128)} fusion(f32[80,640]{1,0:T(8,128)S(1)} %collective-permute-done.18, f32[80,640]{1,0:T(8,128)S(1)} %slice.57, pred[]{:T(512)S(6)} %eq.10), kind=kLoop, calls=%fused_computation | loop fusion | flops 307200 | bytes 819201 | tf_op jit(solution)/shard_map/jit(_where)/select_n | solution.py:349
  (18 shorter events, 0.4 us)
Async XLA Ops:
  0.6 0.9 %copy-start = (bf16[80,1280]{1,0:T(8,128)(2,1)S(1)}, bf16[80,1280]{1,0:T(8,128)(2,1)}, u32[]{:S(2)}) copy-start(bf16[80,1280]{1,0:T(8,128)(2,1)} %param.8) | copy-start | bytes 614404
  1.6 4.5 %copy-start.1 = (bf16[1,24,1280]{2,1,0:T(8,128)(2,1)S(1)}, bf16[1,24,1280]{2,1,0:T(8,128)(2,1)}, u32[]{:S(2)}) copy-start(bf16[1,24,1280]{2,1,0:T(8,128)(2,1)} %param.7) | copy-start | bytes 184324
  1.6 4.5 %copy-start.2 = (bf16[1,24,1280]{2,1,0:T(8,128)(2,1)S(1)}, bf16[1,24,1280]{2,1,0:T(8,128)(2,1)}, u32[]{:S(2)}) copy-start(bf16[1,24,1280]{2,1,0:T(8,128)(2,1)} %param.5) | copy-start | bytes 184324
  1.6 4.5 %copy-start.3 = (bf16[1,24,640]{2,1,0:T(8,128)(2,1)S(1)}, bf16[1,24,640]{2,1,0:T(8,128)(2,1)}, u32[]{:S(2)}) copy-start(bf16[1,24,640]{2,1,0:T(8,128)(2,1)} %param.6) | copy-start | bytes 92164
  1.6 7.6 %collective-permute-start.1 = (bf16[80,640]{1,0:T(8,128)(2,1)S(1)}, bf16[80,640]{1,0:T(8,128)(2,1)S(1)}, u32[]{:S(2)}, u32[]{:S(2)}) collective-permute-start(bf16[80,640]{1,0:T(8,128)(2,1)S(1)} %constant_dynamic-slice_fusion), channel_id=1, source_target_pairs={{0,16},{1,17},{2,18},{3,19},{4,20},{5,21},{6,22},{7,23},{8,24},{9,... | collective-permute-start | bytes 307208 | tf_op jit(solution)/shard_map/ppermute | solution.py:138
  4.8 4.4 %collective-permute-start.5 = (bf16[80,640]{1,0:T(8,128)(2,1)S(1)}, bf16[80,640]{1,0:T(8,128)(2,1)S(1)}, u32[]{:S(2)}, u32[]{:S(2)}) collective-permute-start(bf16[80,640]{1,0:T(8,128)(2,1)S(1)} %constant_dynamic-slice_fusion), channel_id=1, source_target_pairs={{0,8},{1,9},{2,10},{3,11},{4,12},{5,13},{6,14},{7,15},{8,0},{9,1},... | collective-permute-start | bytes 307208 | tf_op jit(solution)/shard_map/ppermute | solution.py:138
  6.1 6.3 %collective-permute-start = (bf16[24,3200]{1,0:T(8,128)(2,1)S(1)}, bf16[24,3200]{1,0:T(8,128)(2,1)S(1)}, u32[]{:S(2)}, u32[]{:S(2)}) collective-permute-start(bf16[24,3200]{1,0:T(8,128)(2,1)S(1)} %pad_maximum_fusion.3), channel_id=1, source_target_pairs={{0,16},{1,4},{2,18},{3,6},{4,1},{5,21},{6,3},{7,23},{8,24},{9,12},... | collective-permute-start | bytes 460808 | tf_op jit(solution)/shard_map/ppermute | solution.py:138
  9.2 7.2 %collective-permute-start.11 = (bf16[2,80,640]{2,1,0:T(8,128)(2,1)S(1)}, bf16[2,80,640]{2,1,0:T(8,128)(2,1)S(1)}, u32[]{:S(2)}, u32[]{:S(2)}) collective-permute-start(bf16[2,80,640]{2,1,0:T(8,128)(2,1)S(1)} %pad_maximum_fusion.2.refs_8_), channel_id=1, source_target_pairs={{0,4},{1,5},{2,6},{3,7},{4,0},{5,1},{6,2},{7,3},{8,12},{9,13},{10,... | collective-permute-start | bytes 614408 | tf_op jit(solution)/shard_map/ppermute | solution.py:138
  10.1 6.1 %collective-permute-start.6 = (bf16[80,640]{1,0:T(8,128)(2,1)S(1)}, bf16[80,640]{1,0:T(8,128)(2,1)S(1)}, u32[]{:S(2)}, u32[]{:S(2)}) collective-permute-start(bf16[80,640]{1,0:T(8,128)(2,1)S(1)} %collective-permute-done.1), channel_id=1, source_target_pairs={{0,8},{1,9},{2,10},{3,11},{4,12},{5,13},{6,14},{7,15},{8,0},{9,1},... | collective-permute-start | bytes 307208 | tf_op jit(solution)/shard_map/ppermute | solution.py:138
  12.5 8.0 %collective-permute-start.2 = (bf16[24,3200]{1,0:T(8,128)(2,1)S(1)}, bf16[24,3200]{1,0:T(8,128)(2,1)S(1)}, u32[]{:S(2)}, u32[]{:S(2)}) collective-permute-start(bf16[24,3200]{1,0:T(8,128)(2,1)S(1)} %broadcast_select_fusion.1.refs_0_), channel_id=1, source_target_pairs={{0,8},{1,17},{2,10},{3,19},{4,20},{5,13},{6,22},{7,15},{8,0},{9,25... | collective-permute-start | bytes 460808 | tf_op jit(solution)/shard_map/ppermute | solution.py:138
  16.1 7.1 %collective-permute-start.3 = (bf16[24,3200]{1,0:T(8,128)(2,1)S(1)}, bf16[24,3200]{1,0:T(8,128)(2,1)S(1)}, u32[]{:S(2)}, u32[]{:S(2)}) collective-permute-start(bf16[24,3200]{1,0:T(8,128)(2,1)S(1)} %collective-permute-done), channel_id=1, source_target_pairs={{0,8},{1,9},{2,10},{3,11},{4,12},{5,13},{6,14},{7,15},{8,0},{9,1},... | collective-permute-start | bytes 460808 | tf_op jit(solution)/shard_map/ppermute | solution.py:138
  16.2 9.7 %collective-permute-start.7 = (bf16[2,80,640]{2,1,0:T(8,128)(2,1)S(1)}, bf16[2,80,640]{2,1,0:T(8,128)(2,1)S(1)}, u32[]{:S(2)}, u32[]{:S(2)}) collective-permute-start(bf16[2,80,640]{2,1,0:T(8,128)(2,1)S(1)} %pad_maximum_fusion.1), channel_id=1, source_target_pairs={{0,4},{1,5},{2,6},{3,7},{4,0},{5,1},{6,2},{7,3},{8,12},{9,13},{10,... | collective-permute-start | bytes 614408 | tf_op jit(solution)/shard_map/ppermute | solution.py:138
  16.5 11.1 %collective-permute-start.12 = (bf16[6,80,640]{2,1,0:T(8,128)(2,1)S(1)}, bf16[6,80,640]{2,1,0:T(8,128)(2,1)S(1)}, u32[]{:S(2)}, u32[]{:S(2)}) collective-permute-start(bf16[6,80,640]{2,1,0:T(8,128)(2,1)S(1)} %constant_dynamic-update-slice_fusion), channel_id=1, source_target_pairs={{0,1},{1,0},{2,3},{3,2},{4,5},{5,4},{6,7},{7,6},{8,9},{9,8},{10,11... | collective-permute-start | bytes 1843208 | tf_op jit(solution)/shard_map/ppermute | solution.py:138
  20.5 6.0 %collective-permute-start.4 = (bf16[24,3200]{1,0:T(8,128)(2,1)S(1)}, bf16[24,3200]{1,0:T(8,128)(2,1)S(1)}, u32[]{:S(2)}, u32[]{:S(2)}) collective-permute-start(bf16[24,3200]{1,0:T(8,128)(2,1)S(1)} %collective-permute-done.2.refs_1_), channel_id=1, source_target_pairs={{0,5},{1,9},{2,7},{3,11},{4,12},{5,0},{6,14},{7,2},{8,13},{9,1},{1... | collective-permute-start | bytes 460808 | tf_op jit(solution)/shard_map/ppermute | solution.py:138
  23.2 4.5 %collective-permute-start.9 = (bf16[24,3200]{1,0:T(8,128)(2,1)S(1)}, bf16[24,3200]{1,0:T(8,128)(2,1)S(1)}, u32[]{:S(2)}, u32[]{:S(2)}) collective-permute-start(bf16[24,3200]{1,0:T(8,128)(2,1)S(1)} %collective-permute-done.3.refs_2_), channel_id=1, source_target_pairs={{0,1},{1,0},{2,3},{3,2},{4,5},{5,4},{6,7},{7,6},{8,9},{9,8},{10,11... | collective-permute-start | bytes 460808 | tf_op jit(solution)/shard_map/ppermute | solution.py:138
  25.9 1.7 %collective-permute-start.8 = (bf16[2,24,3200]{2,1,0:T(8,128)(2,1)S(1)}, bf16[2,24,3200]{2,1,0:T(8,128)(2,1)S(1)}, u32[]{:S(2)}, u32[]{:S(2)}) collective-permute-start(bf16[2,24,3200]{2,1,0:T(8,128)(2,1)S(1)} %pad_maximum_fusion), channel_id=1, source_target_pairs={{0,1},{1,0},{2,3},{3,2},{4,5},{5,4},{6,7},{7,6},{8,9},{9,8},{10,11... | collective-permute-start | bytes 921608 | tf_op jit(solution)/shard_map/ppermute | solution.py:138
  26.0 1.9 %collective-permute-start.13 = (bf16[2,80,640]{2,1,0:T(8,128)(2,1)S(1)}, bf16[2,80,640]{2,1,0:T(8,128)(2,1)S(1)}, u32[]{:S(2)}, u32[]{:S(2)}) collective-permute-start(bf16[2,80,640]{2,1,0:T(8,128)(2,1)S(1)} %collective-permute-done.7.refs_12_), channel_id=1, source_target_pairs={{0,1},{1,0},{2,3},{3,2},{4,5},{5,4},{6,7},{7,6},{8,9},{9,8},{10,11... | collective-permute-start | bytes 614408 | tf_op jit(solution)/shard_map/ppermute | solution.py:138
  26.5 2.0 %collective-permute-start.10 = (bf16[24,3200]{1,0:T(8,128)(2,1)S(1)}, bf16[24,3200]{1,0:T(8,128)(2,1)S(1)}, u32[]{:S(2)}, u32[]{:S(2)}) collective-permute-start(bf16[24,3200]{1,0:T(8,128)(2,1)S(1)} %broadcast_select_fusion.refs_3_), channel_id=1, source_target_pairs={{0,1},{1,0},{2,3},{3,2},{4,5},{5,4},{6,7},{7,6},{8,9},{9,8},{10,11... | collective-permute-start | bytes 460808 | tf_op jit(solution)/shard_map/ppermute | solution.py:138
  31.0 4.4 %collective-permute-start.14 = (bf16[88,640]{1,0:T(8,128)(2,1)S(1)}, bf16[88,640]{1,0:T(8,128)(2,1)S(1)}, u32[]{:S(2)}, u32[]{:S(2)}) collective-permute-start(bf16[88,640]{1,0:T(8,128)(2,1)S(1)} %get-tuple-element.18), channel_id=1, source_target_pairs={{0,2},{1,3},{2,0},{3,1},{4,6},{5,7},{6,4},{7,5},{8,10},{9,11},{10,... | collective-permute-start | bytes 337928 | tf_op jit(solution)/shard_map/ppermute | solution.py:138
  32.3 4.0 %collective-permute-start.15 = (bf16[88,640]{1,0:T(8,128)(2,1)S(1)}, bf16[88,640]{1,0:T(8,128)(2,1)S(1)}, u32[]{:S(2)}, u32[]{:S(2)}) collective-permute-start(bf16[88,640]{1,0:T(8,128)(2,1)S(1)} %get-tuple-element.19), channel_id=1, source_target_pairs={{0,4},{1,5},{2,6},{3,7},{4,0},{5,1},{6,2},{7,3},{8,12},{9,13},{10,... | collective-permute-start | bytes 337928 | tf_op jit(solution)/shard_map/ppermute | solution.py:138
  32.6 6.1 %collective-permute-start.16 = (bf16[88,640]{1,0:T(8,128)(2,1)S(1)}, bf16[88,640]{1,0:T(8,128)(2,1)S(1)}, u32[]{:S(2)}, u32[]{:S(2)}) collective-permute-start(bf16[88,640]{1,0:T(8,128)(2,1)S(1)} %get-tuple-element.19), channel_id=1, source_target_pairs={{0,6},{1,7},{2,4},{3,5},{4,2},{5,3},{6,0},{7,1},{8,14},{9,15},{10,... | collective-permute-start | bytes 337928 | tf_op jit(solution)/shard_map/ppermute | solution.py:138
  33.7 7.4 %collective-permute-start.17 = (bf16[2,24,1280]{2,1,0:T(8,128)(2,1)S(1)}, bf16[2,24,1280]{2,1,0:T(8,128)(2,1)S(1)}, u32[]{:S(2)}, u32[]{:S(2)}) collective-permute-start(bf16[2,24,1280]{2,1,0:T(8,128)(2,1)S(1)} %get-tuple-element.20), channel_id=1, source_target_pairs={{0,8},{1,4},{2,10},{3,6},{4,1},{5,13},{6,3},{7,15},{8,0},{9,12},{1... | collective-permute-start | bytes 368648 | tf_op jit(solution)/shard_map/ppermute | solution.py:138
  38.8 3.0 %collective-permute-start.18 = (f32[80,640]{1,0:T(8,128)S(1)}, f32[80,640]{1,0:T(8,128)S(1)}, u32[]{:S(2)}, u32[]{:S(2)}) collective-permute-start(f32[80,640]{1,0:T(8,128)S(1)} %slice.57), channel_id=1, source_target_pairs={{0,1},{1,0},{2,3},{3,2},{4,5},{5,4},{6,7},{7,6},{8,9},{9,8},{10,11... | collective-permute-start | bytes 614408 | tf_op jit(solution)/shard_map/ppermute | solution.py:138

commit v8 on v7

--- a/solution.py
+++ b/solution.py
@@ -307,7 +307,7 @@
     fourth = jnp.where(ahead, first, fourth_move(second))
     there_01 = core_peer(jnp.stack(after(odd_x, own_rows, second)))
     there_third = core_peer(third)
-    there_fourth = core_peer(fourth)
+    there_fourth = core_peer(*after(odd_x, fourth))
     proj_early = core_peer(jnp.concatenate([even, near, last, even_x]))
     proj_late = core_peer(*after(third, odd_x))
     rows_here = own_rows, second, third, fourth

time: 42.8 us -> 42.8 us (level)
  transfers between devices with their start and end apart: 19 -> 19, of which waited for: 7 -> 6; matrix products, arithmetic and copies ran while one was open for 4% -> 4% of each run, Pallas kernels for 0% -> 0%
where the time goes in v8:
time: 42.8 us; the launch traced here: 42.6 us
  starting transfers between devices  26.1 us (61%)
  waiting for transfers between devices  9.02 us (21%)
  local copies, waits for them, and re-layouts  2.45 us (6%)
  Pallas kernels  2.45 us (6%)
  between operations  1.48 us (3%)
  other arithmetic  1.14 us (3%)
    ppermute x19, starting transfers between devices, moved(): lax.ppermute(value, ('blk', 'rep'), [(number(*place), number(*to(*place))...  26.1 us
    ppermute x19, waiting for transfers between devices, moved(): lax.ppermute(value, ('blk', 'rep'), [(number(*place), number(*to(*place))...  9.02 us
    pallas_call x1, Pallas kernels, on_device_whole_group(): pl.pallas_call(functools.partial(group_kernel, factor), out_shape=(jax.Sh...  2.45 us
    slice x2, local copies, waits for them, and re-layouts, on_device_whole_group(): return (totals[0:1], totals[1:2], grads[0][None], grads[1][None], grad_proj)  1.24 us
    unnamed x12, local copies, waits for them, and re-layouts  0.98 us
  transfers between devices with their start and end apart: 19, of which 6 were waited for; matrix products, arithmetic and copies ran while one was open for 4% of the time, Pallas kernels for 0%

profile of v8, /device:TPU:1, one launch (start us, length us, event | category | flops | bytes accessed | tf_op | source)
XLA Modules:
  0.0 42.6 jit_solution(3419899697952758567)
XLA Ops:
  0.6 0.0 copy-start
  0.7 0.9 %copy-done = bf16[80,1280]{1,0:T(8,128)(2,1)S(1)} copy-done((bf16[80,1280]{1,0:T(8,128)(2,1)S(1)}, bf16[80,1280]{1,0:T(8,128)(2,1)}, u32[]{:S(2)}) %copy-start) | copy-done | bytes 204824
  1.6 0.0 copy-start.1
  1.6 0.0 copy-start.2
  1.6 0.0 copy-start.3
  1.6 3.2 %collective-permute-start.1 = (bf16[80,640]{1,0:T(8,128)(2,1)S(1)}, bf16[80,640]{1,0:T(8,128)(2,1)S(1)}, u32[]{:S(2)}, u32[]{:S(2)}) collective-permute-start(bf16[80,640]{1,0:T(8,128)(2,1)S(1)} %constant_dynamic-slice_fusion), channel_id=1, source_target_pairs={{0,16},{1,17},{2,18},{3,19},{4,20},{5,21},{6,22},{7,23},{8,24},{9,... | collective-permute-start | bytes 307208 | tf_op jit(solution)/shard_map/ppermute | solution.py:138
  4.8 1.3 %collective-permute-start.5 = (bf16[80,640]{1,0:T(8,128)(2,1)S(1)}, bf16[80,640]{1,0:T(8,128)(2,1)S(1)}, u32[]{:S(2)}, u32[]{:S(2)}) collective-permute-start(bf16[80,640]{1,0:T(8,128)(2,1)S(1)} %constant_dynamic-slice_fusion), channel_id=1, source_target_pairs={{0,8},{1,9},{2,10},{3,11},{4,12},{5,13},{6,14},{7,15},{8,0},{9,1},... | collective-permute-start | bytes 307208 | tf_op jit(solution)/shard_map/ppermute | solution.py:138
  6.1 0.0 copy-done.1
  6.1 0.0 copy-done.2
  6.1 0.0 copy-done.3
  6.1 2.4 %collective-permute-start = (bf16[24,3200]{1,0:T(8,128)(2,1)S(1)}, bf16[24,3200]{1,0:T(8,128)(2,1)S(1)}, u32[]{:S(2)}, u32[]{:S(2)}) collective-permute-start(bf16[24,3200]{1,0:T(8,128)(2,1)S(1)} %pad_maximum_fusion.3), channel_id=1, source_target_pairs={{0,16},{1,4},{2,18},{3,6},{4,1},{5,21},{6,3},{7,23},{8,24},{9,12},... | collective-permute-start | bytes 460808 | tf_op jit(solution)/shard_map/ppermute | solution.py:138
  9.2 0.0 collective-permute-done.1
  9.2 0.0 collective-permute-done.5
  9.2 0.8 %collective-permute-start.11 = (bf16[2,80,640]{2,1,0:T(8,128)(2,1)S(1)}, bf16[2,80,640]{2,1,0:T(8,128)(2,1)S(1)}, u32[]{:S(2)}, u32[]{:S(2)}) collective-permute-start(bf16[2,80,640]{2,1,0:T(8,128)(2,1)S(1)} %pad_maximum_fusion.2.refs_8_), channel_id=1, source_target_pairs={{0,4},{1,5},{2,6},{3,7},{4,0},{5,1},{6,2},{7,3},{8,12},{9,13},{10,... | collective-permute-start | bytes 614408 | tf_op jit(solution)/shard_map/ppermute | solution.py:138
  10.1 2.3 %collective-permute-start.6 = (bf16[80,640]{1,0:T(8,128)(2,1)S(1)}, bf16[80,640]{1,0:T(8,128)(2,1)S(1)}, u32[]{:S(2)}, u32[]{:S(2)}) collective-permute-start(bf16[80,640]{1,0:T(8,128)(2,1)S(1)} %collective-permute-done.1), channel_id=1, source_target_pairs={{0,8},{1,9},{2,10},{3,11},{4,12},{5,13},{6,14},{7,15},{8,0},{9,1},... | collective-permute-start | bytes 307208 | tf_op jit(solution)/shard_map/ppermute | solution.py:138
  12.4 0.0 collective-permute-done
  12.5 3.7 %collective-permute-start.2 = (bf16[24,3200]{1,0:T(8,128)(2,1)S(1)}, bf16[24,3200]{1,0:T(8,128)(2,1)S(1)}, u32[]{:S(2)}, u32[]{:S(2)}) collective-permute-start(bf16[24,3200]{1,0:T(8,128)(2,1)S(1)} %broadcast_select_fusion.1.refs_0_), channel_id=1, source_target_pairs={{0,8},{1,17},{2,10},{3,19},{4,20},{5,13},{6,22},{7,15},{8,0},{9,25... | collective-permute-start | bytes 460808 | tf_op jit(solution)/shard_map/ppermute | solution.py:138
  16.1 0.0 collective-permute-start.3
  16.2 0.0 collective-permute-done.6
  16.2 0.3 collective-permute-start.7
  16.5 0.0 collective-permute-done.11.refs_11_
  16.5 2.2 %collective-permute-start.12 = (bf16[6,80,640]{2,1,0:T(8,128)(2,1)S(1)}, bf16[6,80,640]{2,1,0:T(8,128)(2,1)S(1)}, u32[]{:S(2)}, u32[]{:S(2)}) collective-permute-start(bf16[6,80,640]{2,1,0:T(8,128)(2,1)S(1)} %constant_dynamic-update-slice_fusion), channel_id=1, source_target_pairs={{0,1},{1,0},{2,3},{3,2},{4,5},{5,4},{6,7},{7,6},{8,9},{9,8},{10,11... | collective-permute-start | bytes 1843208 | tf_op jit(solution)/shard_map/ppermute | solution.py:138
  18.7 1.8 %collective-permute-done.2.refs_1_ = bf16[24,3200]{1,0:T(8,128)(2,1)S(1)} collective-permute-done((bf16[24,3200]{1,0:T(8,128)(2,1)S(1)}, bf16[24,3200]{1,0:T(8,128)(2,1)S(1)}, u32[]{:S(2)}, u32[]{:S(2)}) %collective-permute-start.2) | collective-permute-done | bytes 153632 | tf_op jit(solution)/shard_map/ppermute | solution.py:138
  20.5 0.0 collective-permute-start.4
  20.5 2.7 %collective-permute-done.3.refs_2_ = bf16[24,3200]{1,0:T(8,128)(2,1)S(1)} collective-permute-done((bf16[24,3200]{1,0:T(8,128)(2,1)S(1)}, bf16[24,3200]{1,0:T(8,128)(2,1)S(1)}, u32[]{:S(2)}, u32[]{:S(2)}) %collective-permute-start.3) | collective-permute-done | bytes 153632 | tf_op jit(solution)/shard_map/ppermute | solution.py:138
  23.2 2.7 %collective-permute-start.9 = (bf16[24,3200]{1,0:T(8,128)(2,1)S(1)}, bf16[24,3200]{1,0:T(8,128)(2,1)S(1)}, u32[]{:S(2)}, u32[]{:S(2)}) collective-permute-start(bf16[24,3200]{1,0:T(8,128)(2,1)S(1)} %collective-permute-done.3.refs_2_), channel_id=1, source_target_pairs={{0,1},{1,0},{2,3},{3,2},{4,5},{5,4},{6,7},{7,6},{8,9},{9,8},{10,11... | collective-permute-start | bytes 460808 | tf_op jit(solution)/shard_map/ppermute | solution.py:138
  25.9 0.0 collective-permute-done.7.refs_12_
  25.9 0.1 collective-permute-start.8
  26.0 0.5 %collective-permute-start.13 = (bf16[2,80,640]{2,1,0:T(8,128)(2,1)S(1)}, bf16[2,80,640]{2,1,0:T(8,128)(2,1)S(1)}, u32[]{:S(2)}, u32[]{:S(2)}) collective-permute-start(bf16[2,80,640]{2,1,0:T(8,128)(2,1)S(1)} %collective-permute-done.7.refs_12_), channel_id=1, source_target_pairs={{0,1},{1,0},{2,3},{3,2},{4,5},{5,4},{6,7},{7,6},{8,9},{9,8},{10,11... | collective-permute-start | bytes 614408 | tf_op jit(solution)/shard_map/ppermute | solution.py:138
  26.5 0.0 collective-permute-done.4
  26.5 1.0 %collective-permute-start.10 = (bf16[24,3200]{1,0:T(8,128)(2,1)S(1)}, bf16[24,3200]{1,0:T(8,128)(2,1)S(1)}, u32[]{:S(2)}, u32[]{:S(2)}) collective-permute-start(bf16[24,3200]{1,0:T(8,128)(2,1)S(1)} %broadcast_select_fusion.refs_3_), channel_id=1, source_target_pairs={{0,1},{1,0},{2,3},{3,2},{4,5},{5,4},{6,7},{7,6},{8,9},{9,8},{10,11... | collective-permute-start | bytes 460808 | tf_op jit(solution)/shard_map/ppermute | solution.py:138
  27.6 0.0 collective-permute-done.8
  27.6 0.0 collective-permute-done.12
  27.7 0.0 collective-permute-done.9.refs_6_
  27.7 0.8 %collective-permute-done.10.refs_7_ = bf16[24,3200]{1,0:T(8,128)(2,1)S(1)} collective-permute-done((bf16[24,3200]{1,0:T(8,128)(2,1)S(1)}, bf16[24,3200]{1,0:T(8,128)(2,1)S(1)}, u32[]{:S(2)}, u32[]{:S(2)}) %collective-permute-start.10) | collective-permute-done | bytes 153632 | tf_op jit(solution)/shard_map/ppermute | solution.py:138
  28.6 0.0 collective-permute-done.13.refs_17_
  28.6 2.4 %group_kernel.1 = (bf16[88,640]{1,0:T(8,128)(2,1)S(1)}, bf16[88,640]{1,0:T(8,128)(2,1)S(1)}, bf16[2,24,1280]{2,1,0:T(8,128)(2,1)S(1)}) custom-call(f32[1]{0:T(128)S(6)} %copy.14.log_scale, bf16[24,3200]{1,0:T(8,128)(2,1)S(1)} %broadcast_select_fusion.1.refs_0_, bf16[24,3200]{1,0:T(8,128)(2,1)S(1)} %collective-permute-done.2.refs_1_, ...), custom_call_target="tpu_custom_call" | custom-call | tf_op jit(solution)/shard_map/group_kernel/pallas_call | solution.py:318
  31.0 1.3 %collective-permute-start.14 = (bf16[88,640]{1,0:T(8,128)(2,1)S(1)}, bf16[88,640]{1,0:T(8,128)(2,1)S(1)}, u32[]{:S(2)}, u32[]{:S(2)}) collective-permute-start(bf16[88,640]{1,0:T(8,128)(2,1)S(1)} %get-tuple-element.20), channel_id=1, source_target_pairs={{0,2},{1,3},{2,0},{3,1},{4,6},{5,7},{6,4},{7,5},{8,10},{9,11},{10,... | collective-permute-start | bytes 337928 | tf_op jit(solution)/shard_map/ppermute | solution.py:138
  32.3 0.3 collective-permute-start.15
  32.6 1.2 %collective-permute-start.16 = (bf16[88,640]{1,0:T(8,128)(2,1)S(1)}, bf16[88,640]{1,0:T(8,128)(2,1)S(1)}, u32[]{:S(2)}, u32[]{:S(2)}) collective-permute-start(bf16[88,640]{1,0:T(8,128)(2,1)S(1)} %get-tuple-element.21), channel_id=1, source_target_pairs={{0,6},{1,7},{2,4},{3,5},{4,2},{5,3},{6,0},{7,1},{8,14},{9,15},{10,... | collective-permute-start | bytes 337928 | tf_op jit(solution)/shard_map/ppermute | solution.py:138
  33.7 1.3 %collective-permute-start.17 = (bf16[2,24,1280]{2,1,0:T(8,128)(2,1)S(1)}, bf16[2,24,1280]{2,1,0:T(8,128)(2,1)S(1)}, u32[]{:S(2)}, u32[]{:S(2)}) collective-permute-start(bf16[2,24,1280]{2,1,0:T(8,128)(2,1)S(1)} %get-tuple-element.22), channel_id=1, source_target_pairs={{0,8},{1,4},{2,10},{3,6},{4,1},{5,13},{6,3},{7,15},{8,0},{9,12},{1... | collective-permute-start | bytes 368648 | tf_op jit(solution)/shard_map/ppermute | solution.py:138
  35.1 0.3 collective-permute-done.14
  35.4 0.9 %collective-permute-done.15 = bf16[88,640]{1,0:T(8,128)(2,1)S(1)} collective-permute-done((bf16[88,640]{1,0:T(8,128)(2,1)S(1)}, bf16[88,640]{1,0:T(8,128)(2,1)S(1)}, u32[]{:S(2)}, u32[]{:S(2)}) %collective-permute-start.15) | collective-permute-done | bytes 112672 | tf_op jit(solution)/shard_map/ppermute | solution.py:138
  36.3 2.4 %collective-permute-done.16 = bf16[88,640]{1,0:T(8,128)(2,1)S(1)} collective-permute-done((bf16[88,640]{1,0:T(8,128)(2,1)S(1)}, bf16[88,640]{1,0:T(8,128)(2,1)S(1)}, u32[]{:S(2)}, u32[]{:S(2)}) %collective-permute-start.16) | collective-permute-done | bytes 112672 | tf_op jit(solution)/shard_map/ppermute | solution.py:138
  38.7 0.1 add_add_fusion
  38.8 1.6 %collective-permute-start.18 = (f32[80,640]{1,0:T(8,128)S(1)}, f32[80,640]{1,0:T(8,128)S(1)}, u32[]{:S(2)}, u32[]{:S(2)}) collective-permute-start(f32[80,640]{1,0:T(8,128)S(1)} %slice.57), channel_id=1, source_target_pairs={{0,1},{1,0},{2,3},{3,2},{4,5},{5,4},{6,7},{7,6},{8,9},{9,8},{10,11... | collective-permute-start | bytes 614408 | tf_op jit(solution)/shard_map/ppermute | solution.py:138
  40.4 0.1 reshape_squeeze.3
  40.5 0.1 reduce_sum.9
  40.6 0.6 %fusion.3 = (f32[1]{0:T(128)}, f32[1]{0:T(128)}) fusion(f32[2]{0:T(128)S(1)} %reduce_sum.9), kind=kLoop, calls=%fused_computation.21 | loop fusion | bytes 16 | tf_op jit(solution)/shard_map/slice | solution.py:355
  41.2 0.0 collective-permute-done.17
  41.2 0.7 %fusion.2 = (bf16[1,24,1280]{2,1,0:T(8,128)(2,1)}, bf16[1,24,1280]{2,1,0:T(8,128)(2,1)}) fusion(bf16[2,24,1280]{2,1,0:T(8,128)(2,1)S(1)} %broadcast_select_fusion.2), kind=kLoop, calls=%fused_computation.20 | loop fusion | bytes 245760 | tf_op jit(solution)/shard_map/slice | solution.py:355
  41.8 0.0 collective-permute-done.18
  41.8 0.8 %maximum_select_fusion = f32[80,1280]{1,0:T(8,128)} fusion(f32[80,640]{1,0:T(8,128)S(1)} %collective-permute-done.18, f32[80,640]{1,0:T(8,128)S(1)} %slice.57, pred[]{:T(512)S(6)} %eq.10), kind=kLoop, calls=%fused_computation | loop fusion | flops 307200 | bytes 819201 | tf_op jit(solution)/shard_map/jit(_where)/select_n | solution.py:349
  (18 shorter events, 0.4 us)
Async XLA Ops:
  0.6 0.9 %copy-start = (bf16[80,1280]{1,0:T(8,128)(2,1)S(1)}, bf16[80,1280]{1,0:T(8,128)(2,1)}, u32[]{:S(2)}) copy-start(bf16[80,1280]{1,0:T(8,128)(2,1)} %param.8) | copy-start | bytes 614404
  1.6 4.5 %copy-start.1 = (bf16[1,24,1280]{2,1,0:T(8,128)(2,1)S(1)}, bf16[1,24,1280]{2,1,0:T(8,128)(2,1)}, u32[]{:S(2)}) copy-start(bf16[1,24,1280]{2,1,0:T(8,128)(2,1)} %param.7) | copy-start | bytes 184324
  1.6 4.5 %copy-start.2 = (bf16[1,24,1280]{2,1,0:T(8,128)(2,1)S(1)}, bf16[1,24,1280]{2,1,0:T(8,128)(2,1)}, u32[]{:S(2)}) copy-start(bf16[1,24,1280]{2,1,0:T(8,128)(2,1)} %param.5) | copy-start | bytes 184324
  1.6 4.5 %copy-start.3 = (bf16[1,24,640]{2,1,0:T(8,128)(2,1)S(1)}, bf16[1,24,640]{2,1,0:T(8,128)(2,1)}, u32[]{:S(2)}) copy-start(bf16[1,24,640]{2,1,0:T(8,128)(2,1)} %param.6) | copy-start | bytes 92164
  1.6 7.6 %collective-permute-start.1 = (bf16[80,640]{1,0:T(8,128)(2,1)S(1)}, bf16[80,640]{1,0:T(8,128)(2,1)S(1)}, u32[]{:S(2)}, u32[]{:S(2)}) collective-permute-start(bf16[80,640]{1,0:T(8,128)(2,1)S(1)} %constant_dynamic-slice_fusion), channel_id=1, source_target_pairs={{0,16},{1,17},{2,18},{3,19},{4,20},{5,21},{6,22},{7,23},{8,24},{9,... | collective-permute-start | bytes 307208 | tf_op jit(solution)/shard_map/ppermute | solution.py:138
  4.8 4.4 %collective-permute-start.5 = (bf16[80,640]{1,0:T(8,128)(2,1)S(1)}, bf16[80,640]{1,0:T(8,128)(2,1)S(1)}, u32[]{:S(2)}, u32[]{:S(2)}) collective-permute-start(bf16[80,640]{1,0:T(8,128)(2,1)S(1)} %constant_dynamic-slice_fusion), channel_id=1, source_target_pairs={{0,8},{1,9},{2,10},{3,11},{4,12},{5,13},{6,14},{7,15},{8,0},{9,1},... | collective-permute-start | bytes 307208 | tf_op jit(solution)/shard_map/ppermute | solution.py:138
  6.1 6.3 %collective-permute-start = (bf16[24,3200]{1,0:T(8,128)(2,1)S(1)}, bf16[24,3200]{1,0:T(8,128)(2,1)S(1)}, u32[]{:S(2)}, u32[]{:S(2)}) collective-permute-start(bf16[24,3200]{1,0:T(8,128)(2,1)S(1)} %pad_maximum_fusion.3), channel_id=1, source_target_pairs={{0,16},{1,4},{2,18},{3,6},{4,1},{5,21},{6,3},{7,23},{8,24},{9,12},... | collective-permute-start | bytes 460808 | tf_op jit(solution)/shard_map/ppermute | solution.py:138
  9.2 7.2 %collective-permute-start.11 = (bf16[2,80,640]{2,1,0:T(8,128)(2,1)S(1)}, bf16[2,80,640]{2,1,0:T(8,128)(2,1)S(1)}, u32[]{:S(2)}, u32[]{:S(2)}) collective-permute-start(bf16[2,80,640]{2,1,0:T(8,128)(2,1)S(1)} %pad_maximum_fusion.2.refs_8_), channel_id=1, source_target_pairs={{0,4},{1,5},{2,6},{3,7},{4,0},{5,1},{6,2},{7,3},{8,12},{9,13},{10,... | collective-permute-start | bytes 614408 | tf_op jit(solution)/shard_map/ppermute | solution.py:138
  10.1 6.1 %collective-permute-start.6 = (bf16[80,640]{1,0:T(8,128)(2,1)S(1)}, bf16[80,640]{1,0:T(8,128)(2,1)S(1)}, u32[]{:S(2)}, u32[]{:S(2)}) collective-permute-start(bf16[80,640]{1,0:T(8,128)(2,1)S(1)} %collective-permute-done.1), channel_id=1, source_target_pairs={{0,8},{1,9},{2,10},{3,11},{4,12},{5,13},{6,14},{7,15},{8,0},{9,1},... | collective-permute-start | bytes 307208 | tf_op jit(solution)/shard_map/ppermute | solution.py:138
  12.5 8.0 %collective-permute-start.2 = (bf16[24,3200]{1,0:T(8,128)(2,1)S(1)}, bf16[24,3200]{1,0:T(8,128)(2,1)S(1)}, u32[]{:S(2)}, u32[]{:S(2)}) collective-permute-start(bf16[24,3200]{1,0:T(8,128)(2,1)S(1)} %broadcast_select_fusion.1.refs_0_), channel_id=1, source_target_pairs={{0,8},{1,17},{2,10},{3,19},{4,20},{5,13},{6,22},{7,15},{8,0},{9,25... | collective-permute-start | bytes 460808 | tf_op jit(solution)/shard_map/ppermute | solution.py:138
  16.1 7.1 %collective-permute-start.3 = (bf16[24,3200]{1,0:T(8,128)(2,1)S(1)}, bf16[24,3200]{1,0:T(8,128)(2,1)S(1)}, u32[]{:S(2)}, u32[]{:S(2)}) collective-permute-start(bf16[24,3200]{1,0:T(8,128)(2,1)S(1)} %collective-permute-done), channel_id=1, source_target_pairs={{0,8},{1,9},{2,10},{3,11},{4,12},{5,13},{6,14},{7,15},{8,0},{9,1},... | collective-permute-start | bytes 460808 | tf_op jit(solution)/shard_map/ppermute | solution.py:138
  16.2 9.7 %collective-permute-start.7 = (bf16[2,80,640]{2,1,0:T(8,128)(2,1)S(1)}, bf16[2,80,640]{2,1,0:T(8,128)(2,1)S(1)}, u32[]{:S(2)}, u32[]{:S(2)}) collective-permute-start(bf16[2,80,640]{2,1,0:T(8,128)(2,1)S(1)} %pad_maximum_fusion.1), channel_id=1, source_target_pairs={{0,4},{1,5},{2,6},{3,7},{4,0},{5,1},{6,2},{7,3},{8,12},{9,13},{10,... | collective-permute-start | bytes 614408 | tf_op jit(solution)/shard_map/ppermute | solution.py:138
  16.5 11.1 %collective-permute-start.12 = (bf16[6,80,640]{2,1,0:T(8,128)(2,1)S(1)}, bf16[6,80,640]{2,1,0:T(8,128)(2,1)S(1)}, u32[]{:S(2)}, u32[]{:S(2)}) collective-permute-start(bf16[6,80,640]{2,1,0:T(8,128)(2,1)S(1)} %constant_dynamic-update-slice_fusion), channel_id=1, source_target_pairs={{0,1},{1,0},{2,3},{3,2},{4,5},{5,4},{6,7},{7,6},{8,9},{9,8},{10,11... | collective-permute-start | bytes 1843208 | tf_op jit(solution)/shard_map/ppermute | solution.py:138
  20.5 6.0 %collective-permute-start.4 = (bf16[24,3200]{1,0:T(8,128)(2,1)S(1)}, bf16[24,3200]{1,0:T(8,128)(2,1)S(1)}, u32[]{:S(2)}, u32[]{:S(2)}) collective-permute-start(bf16[24,3200]{1,0:T(8,128)(2,1)S(1)} %collective-permute-done.2.refs_1_), channel_id=1, source_target_pairs={{0,5},{1,9},{2,7},{3,11},{4,12},{5,0},{6,14},{7,2},{8,13},{9,1},{1... | collective-permute-start | bytes 460808 | tf_op jit(solution)/shard_map/ppermute | solution.py:138
  23.2 4.5 %collective-permute-start.9 = (bf16[24,3200]{1,0:T(8,128)(2,1)S(1)}, bf16[24,3200]{1,0:T(8,128)(2,1)S(1)}, u32[]{:S(2)}, u32[]{:S(2)}) collective-permute-start(bf16[24,3200]{1,0:T(8,128)(2,1)S(1)} %collective-permute-done.3.refs_2_), channel_id=1, source_target_pairs={{0,1},{1,0},{2,3},{3,2},{4,5},{5,4},{6,7},{7,6},{8,9},{9,8},{10,11... | collective-permute-start | bytes 460808 | tf_op jit(solution)/shard_map/ppermute | solution.py:138
  25.9 1.7 %collective-permute-start.8 = (bf16[2,24,3200]{2,1,0:T(8,128)(2,1)S(1)}, bf16[2,24,3200]{2,1,0:T(8,128)(2,1)S(1)}, u32[]{:S(2)}, u32[]{:S(2)}) collective-permute-start(bf16[2,24,3200]{2,1,0:T(8,128)(2,1)S(1)} %pad_maximum_fusion), channel_id=1, source_target_pairs={{0,1},{1,0},{2,3},{3,2},{4,5},{5,4},{6,7},{7,6},{8,9},{9,8},{10,11... | collective-permute-start | bytes 921608 | tf_op jit(solution)/shard_map/ppermute | solution.py:138
  26.0 2.6 %collective-permute-start.13 = (bf16[2,80,640]{2,1,0:T(8,128)(2,1)S(1)}, bf16[2,80,640]{2,1,0:T(8,128)(2,1)S(1)}, u32[]{:S(2)}, u32[]{:S(2)}) collective-permute-start(bf16[2,80,640]{2,1,0:T(8,128)(2,1)S(1)} %collective-permute-done.7.refs_12_), channel_id=1, source_target_pairs={{0,1},{1,0},{2,3},{3,2},{4,5},{5,4},{6,7},{7,6},{8,9},{9,8},{10,11... | collective-permute-start | bytes 614408 | tf_op jit(solution)/shard_map/ppermute | solution.py:138
  26.5 2.0 %collective-permute-start.10 = (bf16[24,3200]{1,0:T(8,128)(2,1)S(1)}, bf16[24,3200]{1,0:T(8,128)(2,1)S(1)}, u32[]{:S(2)}, u32[]{:S(2)}) collective-permute-start(bf16[24,3200]{1,0:T(8,128)(2,1)S(1)} %broadcast_select_fusion.refs_3_), channel_id=1, source_target_pairs={{0,1},{1,0},{2,3},{3,2},{4,5},{5,4},{6,7},{7,6},{8,9},{9,8},{10,11... | collective-permute-start | bytes 460808 | tf_op jit(solution)/shard_map/ppermute | solution.py:138
  31.0 4.4 %collective-permute-start.14 = (bf16[88,640]{1,0:T(8,128)(2,1)S(1)}, bf16[88,640]{1,0:T(8,128)(2,1)S(1)}, u32[]{:S(2)}, u32[]{:S(2)}) collective-permute-start(bf16[88,640]{1,0:T(8,128)(2,1)S(1)} %get-tuple-element.20), channel_id=1, source_target_pairs={{0,2},{1,3},{2,0},{3,1},{4,6},{5,7},{6,4},{7,5},{8,10},{9,11},{10,... | collective-permute-start | bytes 337928 | tf_op jit(solution)/shard_map/ppermute | solution.py:138
  32.3 4.0 %collective-permute-start.15 = (bf16[88,640]{1,0:T(8,128)(2,1)S(1)}, bf16[88,640]{1,0:T(8,128)(2,1)S(1)}, u32[]{:S(2)}, u32[]{:S(2)}) collective-permute-start(bf16[88,640]{1,0:T(8,128)(2,1)S(1)} %get-tuple-element.21), channel_id=1, source_target_pairs={{0,4},{1,5},{2,6},{3,7},{4,0},{5,1},{6,2},{7,3},{8,12},{9,13},{10,... | collective-permute-start | bytes 337928 | tf_op jit(solution)/shard_map/ppermute | solution.py:138
  32.6 6.1 %collective-permute-start.16 = (bf16[88,640]{1,0:T(8,128)(2,1)S(1)}, bf16[88,640]{1,0:T(8,128)(2,1)S(1)}, u32[]{:S(2)}, u32[]{:S(2)}) collective-permute-start(bf16[88,640]{1,0:T(8,128)(2,1)S(1)} %get-tuple-element.21), channel_id=1, source_target_pairs={{0,6},{1,7},{2,4},{3,5},{4,2},{5,3},{6,0},{7,1},{8,14},{9,15},{10,... | collective-permute-start | bytes 337928 | tf_op jit(solution)/shard_map/ppermute | solution.py:138
  33.7 7.4 %collective-permute-start.17 = (bf16[2,24,1280]{2,1,0:T(8,128)(2,1)S(1)}, bf16[2,24,1280]{2,1,0:T(8,128)(2,1)S(1)}, u32[]{:S(2)}, u32[]{:S(2)}) collective-permute-start(bf16[2,24,1280]{2,1,0:T(8,128)(2,1)S(1)} %get-tuple-element.22), channel_id=1, source_target_pairs={{0,8},{1,4},{2,10},{3,6},{4,1},{5,13},{6,3},{7,15},{8,0},{9,12},{1... | collective-permute-start | bytes 368648 | tf_op jit(solution)/shard_map/ppermute | solution.py:138
  38.8 3.0 %collective-permute-start.18 = (f32[80,640]{1,0:T(8,128)S(1)}, f32[80,640]{1,0:T(8,128)S(1)}, u32[]{:S(2)}, u32[]{:S(2)}) collective-permute-start(f32[80,640]{1,0:T(8,128)S(1)} %slice.57), channel_id=1, source_target_pairs={{0,1},{1,0},{2,3},{3,2},{4,5},{5,4},{6,7},{7,6},{8,9},{9,8},{10,11... | collective-permute-start | bytes 614408 | tf_op jit(solution)/shard_map/ppermute | solution.py:138
